TPU v7x, 512 devices: a whole 4x8x8 slice. The times are simulated.
512 devices in a mesh: ctx: 32 (over x, z), tp: 16 (over y, core).
Axes of the slice: x: 4, y: 8, z: 8, core: 2. Of those that a mesh axis runs over, the one named last changes fastest.
Arguments:
- signal: bfloat16 [4096, 8192], P('tp', 'ctx'), may hold values from -6 to 6
- pre_gate: bfloat16 [4096, 8192], P('tp', 'ctx'), may hold values from -6 to 6
- post_gate: bfloat16 [4096, 8192], P('tp', 'ctx'), may hold values from -6 to 6
- filter_taps: float32 [4096, 8192], P('tp', 'ctx'), may hold values from -0.0625 to 0.0625
- skip_gain: float32 [4096], P('tp'), may hold values from -4 to 4
- out_weight: bfloat16 [4096, 4096], P('tp'), may hold values from -0.125 to 0.125
Outputs:
- projected: bfloat16 [4096, 8192], P('tp', 'ctx')
All inputs are finite; a program needn't handle non-finite values.
Results may differ from a plain program's by a relative error of at most 0.027.
Values may be sent and summed in bfloat16 or wider, within the bound.
No kernel may reach another device: no remote copies, remote signals or barrier semaphores. Data moves between devices by JAX's collectives and lax.ppermute only.
A program may use at most 64 MiB of HBM per device.

v0:
```python
import math

import jax
import jax.numpy as jnp
from jax import lax
from jax.sharding import PartitionSpec as P

highest = lax.Precision.HIGHEST
two_pi = 2.0 * math.pi


def shortened(shard):

    def short(part):
        return part.astype(jnp.bfloat16) if part.dtype == jnp.float32 else part

    return jax.tree.map(short, shard)


def angle_tables(count, period):
    first = jnp.arange(count, dtype=jnp.int32)
    second = jnp.arange(period, dtype=jnp.int32)
    angle = (first[:, None] * second[None, :] % period).astype(jnp.float32) * (two_pi / period)
    return (jnp.cos(angle), jnp.sin(angle))


def twiddle_tables(freq_first, freq_count, tokens_here, total_len):
    freq = freq_first + jnp.arange(freq_count, dtype=jnp.int32)
    place = jnp.arange(tokens_here, dtype=jnp.int32)
    angle = (freq[:, None] * place[None, :] % total_len).astype(jnp.float32) * (two_pi / total_len)
    return (jnp.cos(angle), jnp.sin(angle))


def matmul_high(left, right):
    return jnp.matmul(left, right, precision=highest)


def front_section(blocks, devices):
    cosine, sine = angle_tables(devices, 2 * devices)
    real_part = jnp.einsum("scan,ak->sckn", blocks, cosine, precision=highest)
    imag_part = -jnp.einsum("scan,ak->sckn", blocks, sine, precision=highest)
    return jnp.stack([real_part, imag_part])


def middle_section(spectrum, freq_first, total_len):
    tokens_here = spectrum.shape[-1]
    twid_cos, twid_sin = twiddle_tables(freq_first, spectrum.shape[3], tokens_here, total_len)
    turned_real = spectrum[0] * twid_cos + spectrum[1] * twid_sin
    turned_imag = spectrum[1] * twid_cos - spectrum[0] * twid_sin
    square_cos, square_sin = angle_tables(tokens_here, tokens_here)
    full_real = matmul_high(turned_real, square_cos) + matmul_high(turned_imag, square_sin)
    full_imag = matmul_high(turned_imag, square_cos) - matmul_high(turned_real, square_sin)
    prod_real = full_real[0] * full_real[1] - full_imag[0] * full_imag[1]
    prod_imag = full_real[0] * full_imag[1] + full_imag[0] * full_real[1]
    back_real = matmul_high(prod_real, square_cos) - matmul_high(prod_imag, square_sin)
    back_imag = matmul_high(prod_imag, square_cos) + matmul_high(prod_real, square_sin)
    out_real = back_real * twid_cos - back_imag * twid_sin
    out_imag = back_real * twid_sin + back_imag * twid_cos
    return jnp.stack([out_real, out_imag])


def back_section(wide, devices, total_len):
    cosine, sine = angle_tables(devices, 2 * devices)
    summed = jnp.einsum("ckn,ak->can", wide[0], cosine, precision=highest)
    summed = summed - jnp.einsum("ckn,ak->can", wide[1], sine, precision=highest)
    return summed * (1.0 / total_len)


def per_device(signal, pre_gate, post_gate, filter_taps, skip_gain, out_weight):
    channels_here, tokens_here = signal.shape
    devices = lax.axis_size("ctx")
    total_len = 2 * devices * tokens_here
    gated_input = signal.astype(jnp.float32) * pre_gate.astype(jnp.float32)
    stacked = jnp.stack([gated_input, filter_taps])[:, :, None, :]
    blocks = lax.all_to_all(
        stacked.astype(jnp.bfloat16), "ctx", split_axis=3, concat_axis=2, tiled=True
    ).astype(stacked.dtype)
    spectrum = lax.all_to_all(
        front_section(blocks, devices).astype(jnp.bfloat16),
        "ctx",
        split_axis=3,
        concat_axis=4,
        tiled=True,
    ).astype(jnp.float32)
    freq_first = lax.axis_index("ctx") * spectrum.shape[3]
    wide = middle_section(spectrum, freq_first, total_len)
    regathered = lax.all_to_all(
        shortened(wide), "ctx", split_axis=3, concat_axis=2, tiled=True
    ).astype(wide.dtype)
    convolved = lax.all_to_all(
        shortened(back_section(regathered, devices, total_len)),
        "ctx",
        split_axis=1,
        concat_axis=2,
        tiled=True,
    )[:, 0, :]
    mixed = (post_gate.astype(jnp.float32) * (convolved + skip_gain[:, None] * gated_input)).astype(
        jnp.bfloat16
    )
    return lax.psum_scatter(
        lax.dot_general(
            out_weight, mixed, (((0,), (0,)), ((), ())), preferred_element_type=jnp.float32
        ).astype(jnp.bfloat16),
        "tp",
        scatter_dimension=0,
        tiled=True,
    )


def solution(mesh):
    return jax.shard_map(
        per_device,
        mesh=mesh,
        in_specs=(
            P("tp", "ctx"),
            P("tp", "ctx"),
            P("tp", "ctx"),
            P("tp", "ctx"),
            P("tp"),
            P("tp", None),
        ),
        out_specs=P("tp", "ctx"),
        check_vma=False,
    )
```

profile of v0, /device:TPU:1, one launch (start us, length us, event | category | flops | bytes accessed | tf_op | source)
XLA Modules:
  0.0 196.2 jit_solution(17742948120013206484)
XLA Ops:
  6.5 0.0 copy-start
  6.5 1.1 copy.48
  7.7 1.0 copy.49
  8.7 1.0 copy.50
  9.8 0.3 copy.51
  10.1 23.2 %all_to_all.45 = bf16[2,256,1,256]{1,0,2,3:T(2,128)(2,1)S(1)} all-to-all(bf16[2,256,1,256]{1,0,2,3:T(2,128)(2,1)S(1)} %copy.51), channel_id=1, replica_groups=mesh['ctx'=32,'tp'=16] {'ctx'}, dimensions={3} | all-to-all | bytes 524288 | tf_op jit(solution)/shard_map/all_to_all | solution.py:75
  33.4 0.7 fusion.2
  34.1 0.7 fusion.3
  34.8 0.1 pad_maximum_fusion
  34.9 1.6 copy.55
  36.4 6.5 %all-to-all-start.1 = ((bf16[2,2,256,64,8]{2,4,1,0,3:T(8,128)(2,1)}), bf16[2,2,256,64,8]{2,4,1,0,3:T(8,128)(2,1)S(1)}, u32[]{:S(2)}, u32[]{:S(2)}) async-start(bf16[2,2,256,64,8]{2,4,1,0,3:T(8,128)(2,1)} %copy.55), calls=%async_computation.1 | async-start | bytes 2097152 | tf_op jit(solution)/shard_map/all_to_all | solution.py:78
  42.9 0.1 fusion.77
  43.1 24.3 %all-to-all-done.1 = bf16[2,2,256,64,8]{2,4,1,0,3:T(8,128)(2,1)S(1)} async-done(((bf16[2,2,256,64,8]{2,4,1,0,3:T(8,128)(2,1)}), bf16[2,2,256,64,8]{2,4,1,0,3:T(8,128)(2,1)S(1)}, u32[]{:S(2)}, u32[]{:S(2)}) %all-to-all-start.1) | async-done | bytes 1048608 | tf_op jit(solution)/shard_map/all_to_all | solution.py:78
  67.3 0.1 copy.56
  67.4 0.3 convert_bitcast_fusion
  67.7 0.2 fusion.126
  67.9 2.9 %fusion.30 = f32[2,256,2,256]{3,1,2,0:T(8,128)S(1)} fusion(f32[1,2,256,2,32,8]{2,5,3,4,1,0:T(8,128)S(1)} %get-tuple-element.8, f32[1,2,256,2,32,8]{2,5,3,4,1,0:T(8,128)S(1)} %get-tuple-element.7, f32[2,256]{1,0:T(2,128)S(1)} %get-tuple-element.14, f32[2,256]{1,0:T(2,128)S(1)} %get-tuple-element.13), kind=kOutput, calls=%fused_computation.55 | convolution fusion | flops 807010304 | bytes 3149824 | tf_op jit(solution)/shard_map/dot_general | solution.py:35
  70.8 2.9 %fusion.28 = f32[2,256,2,256]{3,1,2,0:T(8,128)S(1)} fusion(f32[1,2,256,2,32,8]{2,5,3,4,1,0:T(8,128)S(1)} %get-tuple-element.8, f32[1,2,256,2,32,8]{2,5,3,4,1,0:T(8,128)S(1)} %get-tuple-element.7, f32[2,256]{1,0:T(2,128)S(1)} %get-tuple-element.14, f32[2,256]{1,0:T(2,128)S(1)} %get-tuple-element.13), kind=kOutput, calls=%fused_computation.53 | convolution fusion | flops 807010304 | bytes 3149824 | tf_op jit(solution)/shard_map/dot_general | solution.py:35
  73.6 2.9 %convolution_add_fusion = f32[2,256,2,256]{3,1,2,0:T(8,128)S(1)} fusion(f32[2,256,2,256]{3,1,2,0:T(8,128)S(1)} %fusion.30, f32[1,2,256,2,32,8]{2,5,3,4,1,0:T(8,128)S(1)} %get-tuple-element.8, f32[1,2,256,2,32,8]{2,5,3,4,1,0:T(8,128)S(1)} %get-tuple-element.7, f32[2,256]{1,0:T(2,128)S(1)} %get-tuple-element.14, f32[2,256]{1,0:T(2,128)S(1)} %get-tuple-element.13), kind=kOutput, calls=%fused_computation.5 | convolution fusion | flops 807272448 | bytes 4198400 | tf_op jit(solution)/shard_map/dot_general | solution.py:35
  76.5 3.1 %convolution_subtract_fusion = f32[2,256,2,256]{3,1,2,0:T(8,128)S(1)} fusion(f32[2,256,2,256]{3,1,2,0:T(8,128)S(1)} %fusion.28, f32[1,2,256,2,32,8]{2,5,3,4,1,0:T(8,128)S(1)} %get-tuple-element.8, f32[1,2,256,2,32,8]{2,5,3,4,1,0:T(8,128)S(1)} %get-tuple-element.7, f32[2,256]{1,0:T(2,128)S(1)} %get-tuple-element.14, f32[2,256]{1,0:T(2,128)S(1)} %get-tuple-element.13), kind=kOutput, calls=%fused_computation.4 | convolution fusion | flops 807272448 | bytes 4198400 | tf_op jit(solution)/shard_map/dot_general | solution.py:35
  79.7 0.1 multiply_subtract_fusion
  79.8 1.6 fusion.9
  81.4 1.6 fusion.13
  82.9 1.6 convolution_add_fusion.1
  84.5 1.6 fusion.18
  86.1 0.1 pad_maximum_fusion.1
  86.2 0.5 copy.63
  86.7 21.8 %all_to_all.46 = bf16[2,256,2,256]{1,2,0,3:T(2,128)(2,1)S(1)} all-to-all(bf16[2,256,2,256]{1,2,0,3:T(2,128)(2,1)S(1)} %copy.63), channel_id=1, replica_groups=mesh['ctx'=32,'tp'=16] {'ctx'}, dimensions={3} | all-to-all | bytes 1048576 | tf_op jit(solution)/shard_map/all_to_all | solution.py:87
  108.5 0.1 copy.95
  108.6 0.0 copy-start.1
  108.7 0.0 copy-start.2
  108.7 0.3 copy.65
  108.9 0.1 squeeze.10
  109.1 0.3 fusion.62
  109.4 0.3 copy.66
  109.7 0.1 squeeze.11
  109.8 0.3 fusion.6
  110.1 0.7 copy.67
  110.9 8.0 %all-to-all-start.3 = ((bf16[256,32,8]{0,2,1:T(8,128)(2,1)}), bf16[256,32,8]{0,2,1:T(8,128)(2,1)S(1)}, u32[]{:S(2)}, u32[]{:S(2)}) async-start(bf16[256,32,8]{0,2,1:T(8,128)(2,1)} %copy.67), calls=%async_computation.3 | async-start | bytes 262144 | tf_op jit(solution)/shard_map/all_to_all | solution.py:90
  118.9 0.0 reduce-scatter.2.cloned.1.call-start
  119.0 0.0 copy-done.1
  119.0 0.1 copy.47
  119.1 9.1 %all-to-all-done.3 = bf16[256,32,8]{0,2,1:T(8,128)(2,1)S(1)} async-done(((bf16[256,32,8]{0,2,1:T(8,128)(2,1)}), bf16[256,32,8]{0,2,1:T(8,128)(2,1)S(1)}, u32[]{:S(2)}, u32[]{:S(2)}) %all-to-all-start.3) | async-done | bytes 131104 | tf_op jit(solution)/shard_map/all_to_all | solution.py:90
  128.2 0.0 copy-done
  128.2 2.1 %fusion = bf16[4096,256]{0,1:T(8,128)(2,1)} fusion(bf16[256,4096]{1,0:T(8,128)(2,1)S(1)} %copy-done, bf16[256,256]{0,1:T(8,128)(2,1)S(1)} %copy.47, bf16[256,256]{0,1:T(8,128)(2,1)S(1)} %copy.49, bf16[256,256]{0,1:T(8,128)(2,1)S(1)} %copy.48, bf16[256,32,8]{0,2,1:T(8,128)(2,1)S(1)} %all-to-all-done.3, f32[256]{0:T(256)S(1)} %copy-done.2), kind=kOutput, calls=%fused_computation.1 | convolution fusion | flops 538509312 | bytes 4719616 | tf_op jit(solution)/shard_map/dot_general | solution.py:101
  130.2 0.0 reduce-scatter.2.cloned.1.call-update
  130.3 57.5 %reduce-scatter.2.cloned.1.call-done = bf16[256,256]{0,1:T(8,128)(2,1)} async-done(((bf16[4096,256]{0,1:T(8,128)(2,1)}), bf16[256,256]{0,1:T(8,128)(2,1)}) %reduce-scatter.2.cloned.1.call-update) | async-done | bytes 131088 | tf_op jit(solution)/shard_map/reduce_scatter | solution.py:100
  187.7 1.7 copy.68
  (6 shorter events, 0.1 us)
Async XLA Ops:
  6.5 121.6 %copy-start = (bf16[256,4096]{1,0:T(8,128)(2,1)S(1)}, bf16[256,4096]{1,0:T(8,128)(2,1)}, u32[]{:S(2)}) copy-start(bf16[256,4096]{1,0:T(8,128)(2,1)} %param.11) | copy-start | bytes 6291460
  36.4 30.9 %all-to-all-start.1 = ((bf16[2,2,256,64,8]{2,4,1,0,3:T(8,128)(2,1)}), bf16[2,2,256,64,8]{2,4,1,0,3:T(8,128)(2,1)S(1)}, u32[]{:S(2)}, u32[]{:S(2)}) async-start(bf16[2,2,256,64,8]{2,4,1,0,3:T(8,128)(2,1)} %copy.55), calls=%async_computation.1 | async-start | bytes 2097152 | tf_op jit(solution)/shard_map/all_to_all | solution.py:78
  108.6 10.3 %copy-start.1 = (bf16[256,256]{1,0:T(8,128)(2,1)S(1)}, bf16[256,256]{1,0:T(8,128)(2,1)}, u32[]{:S(2)}) copy-start(bf16[256,256]{1,0:T(8,128)(2,1)} %param.8) | copy-start | bytes 393220
  108.7 19.5 %copy-start.2 = (f32[256]{0:T(256)S(1)}, f32[256]{0:T(256)}, u32[]{:S(2)}) copy-start(f32[256]{0:T(256)} %param.10) | copy-start | bytes 3076
  110.9 17.3 %all-to-all-start.3 = ((bf16[256,32,8]{0,2,1:T(8,128)(2,1)}), bf16[256,32,8]{0,2,1:T(8,128)(2,1)S(1)}, u32[]{:S(2)}, u32[]{:S(2)}) async-start(bf16[256,32,8]{0,2,1:T(8,128)(2,1)} %copy.67), calls=%async_computation.3 | async-start | bytes 262144 | tf_op jit(solution)/shard_map/all_to_all | solution.py:90
  118.9 68.8 %reduce-scatter.2.cloned.1.call-start = ((), (), s32[]{:S(2)}) async-start(), calls=%async_computation.5 | async-start | bytes 2228224 | tf_op jit(solution)/shard_map/reduce_scatter | solution.py:100
Sparse Core Ops, SparseCore 0:
  130.4 57.2 reduce-scatter.1
where the time goes:
time: 198 us; the launch traced here: 196 us
  waiting for transfers between devices  90.8 us (46%)
  blocking collectives  45 us (23%)
  matrix products  22.2 us (11%)
  starting transfers between devices  14.6 us (7%)
  between operations  13.7 us (7%)
  local copies, waits for them, and re-layouts  9.18 us (5%)
    reduce_scatter x1, waiting for transfers between devices, per_device(): lax.psum_scatter(lax.dot_general(out_weight, mixed, (((0,), (0,)), ((), (...  57.5 us
    all_to_all x1, waiting for transfers between devices, per_device(): lax.all_to_all(front_section(blocks, devices).astype(jnp.bfloat16), 'ctx'...  24.3 us
    all_to_all x1, blocking collectives, per_device(): lax.all_to_all(stacked.astype(jnp.bfloat16), 'ctx', split_axis=3, concat_...  23.2 us
    all_to_all x1, blocking collectives, per_device(): lax.all_to_all(shortened(wide), 'ctx', split_axis=3, concat_axis=2, tiled...  21.8 us
    dot_general x8, matrix products, matmul_high(): return jnp.matmul(left, right, precision=highest)  18.1 us
    all_to_all x1, waiting for transfers between devices, per_device(): lax.all_to_all(shortened(back_section(regathered, devices, total_len)), '...  9.09 us
    all_to_all x1, starting transfers between devices, per_device(): lax.all_to_all(shortened(back_section(regathered, devices, total_len)), '...  8.05 us
    all_to_all x1, starting transfers between devices, per_device(): lax.all_to_all(front_section(blocks, devices).astype(jnp.bfloat16), 'ctx'...  6.47 us
  transfers between devices with their start and end apart: 3, of which 3 were waited for; matrix products, arithmetic and copies ran while one was open for 0% of the time, Pallas kernels for 0%

commit v1 on v0

v1 whole, which is shorter than its diff:
```python
import math

import jax
import jax.numpy as jnp
import numpy as np
from jax import lax
from jax.sharding import Mesh
from jax.sharding import PartitionSpec as P

TP_AXES = ("quad", "pair", "core")
GROUP = ("pair", "core")


def dft_tables(blocks, tokens, channels):
    period = 2 * blocks
    total = period * tokens
    low = blocks + 1
    k1 = np.arange(low)
    i = np.arange(blocks)
    s = np.arange(tokens)
    first = 2 * np.pi * (np.outer(k1, i) % period) / period
    turn = 2 * np.pi * (np.outer(k1, s) % total) / total
    square = 2 * np.pi * (np.outer(s, s) % tokens) / tokens
    both = 2 * channels
    front = np.concatenate(
        [np.kron(np.cos(first), np.eye(both)), np.kron(-np.sin(first), np.eye(both))]
    )
    cos, sin = np.cos(square), np.sin(square)
    ahead = np.block([[cos, -sin], [sin, cos]])
    again = np.block([[cos, sin], [-sin, cos]])
    weight = np.where((k1 == 0) | (k1 == blocks), 1.0, 2.0)[:, None] / total
    back = np.concatenate(
        [
            np.kron((weight * np.cos(first)).T, np.eye(channels)),
            np.kron(-(weight * np.sin(first)).T, np.eye(channels)),
        ],
        axis=1,
    )
    matrices = [jnp.asarray(m, jnp.bfloat16) for m in (front, ahead, again, back)]
    turns = [jnp.asarray(m, jnp.float32)[:, None, :] for m in (np.cos(turn), np.sin(turn))]
    return matrices, turns


def matmul(left, right):
    return jnp.dot(left, right, preferred_element_type=jnp.float32)


def convolve(blocks_in, channels):
    blocks, both, tokens = blocks_in.shape
    (front, ahead, again, back), (turn_cos, turn_sin) = dft_tables(blocks, tokens, channels)
    low = blocks + 1
    spread = matmul(front, blocks_in.reshape(blocks * both, tokens)).reshape(2, low, both, tokens)
    real = spread[0] * turn_cos + spread[1] * turn_sin
    imag = spread[1] * turn_cos - spread[0] * turn_sin
    rows = jnp.concatenate([real, imag], axis=2).astype(jnp.bfloat16)
    spectrum = matmul(rows.reshape(low * both, 2 * tokens), ahead).reshape(
        low, 2, channels, 2, tokens
    )
    sig_real, sig_imag = spectrum[:, 0, :, 0], spectrum[:, 0, :, 1]
    tap_real, tap_imag = spectrum[:, 1, :, 0], spectrum[:, 1, :, 1]
    product = jnp.concatenate(
        [
            sig_real * tap_real - sig_imag * tap_imag,
            sig_real * tap_imag + sig_imag * tap_real,
        ],
        axis=2,
    ).astype(jnp.bfloat16)
    folded = matmul(product.reshape(low * channels, 2 * tokens), again).reshape(
        low, channels, 2, tokens
    )
    real = folded[:, :, 0] * turn_cos - folded[:, :, 1] * turn_sin
    imag = folded[:, :, 0] * turn_sin + folded[:, :, 1] * turn_cos
    rows = jnp.concatenate([real, imag], axis=0).astype(jnp.bfloat16)
    out = matmul(back, rows.reshape(2 * low * channels, tokens))
    return out.astype(jnp.bfloat16).reshape(blocks, channels, tokens)


def per_device(signal, pre_gate, post_gate, filter_taps, skip_gain, out_weight):
    channels_here, tokens_here = signal.shape
    devices = lax.axis_size("ctx")
    channels = channels_here // devices
    quads = lax.axis_size("quad")
    group = lax.axis_size("pair") * lax.axis_size("core")
    features = out_weight.shape[1]
    width = features // (quads * group)

    gated_input = signal.astype(jnp.float32) * pre_gate.astype(jnp.float32)
    send = jnp.concatenate(
        [
            gated_input.astype(jnp.bfloat16).reshape(devices, channels, tokens_here),
            filter_taps.astype(jnp.bfloat16).reshape(devices, channels, tokens_here),
        ],
        axis=1,
    )
    blocks = lax.all_to_all(send, "ctx", split_axis=0, concat_axis=0, tiled=True)

    place = lax.axis_index(GROUP)
    columns = [
        jnp.concatenate(
            [
                lax.slice_in_dim(out_weight, (q * group + t) * width, (q * group + t + 1) * width, axis=1)
                for q in range(quads)
            ],
            axis=1,
        )
        for t in range(group)
    ]

    def columns_of(target):
        chosen = columns[0]
        for t in range(1, group):
            chosen = jnp.where(target == t, columns[t], chosen)
        return chosen

    weights = [columns_of(place)] + [
        lax.ppermute(columns_of(place ^ r), GROUP, [(t, t ^ r) for t in range(group)])
        for r in range(1, group)
    ]

    convolved = lax.all_to_all(
        convolve(blocks, channels), "ctx", split_axis=0, concat_axis=0, tiled=True
    ).reshape(channels_here, tokens_here)
    mixed = (
        post_gate.astype(jnp.float32)
        * (convolved.astype(jnp.float32) + skip_gain[:, None] * gated_input)
    ).astype(jnp.bfloat16)
    gathered = lax.all_gather(mixed, GROUP, axis=0, tiled=False)
    partial = sum(
        lax.dot_general(
            weights[r],
            lax.dynamic_index_in_dim(gathered, place ^ r, 0, keepdims=False),
            (((0,), (0,)), ((), ())),
            preferred_element_type=jnp.float32,
        )
        for r in range(group)
    )
    shares = lax.all_to_all(
        partial.astype(jnp.bfloat16).reshape(quads, width, tokens_here),
        "quad",
        split_axis=0,
        concat_axis=0,
        tiled=True,
    )
    return jnp.sum(shares.astype(jnp.float32), axis=0).astype(jnp.bfloat16)


def solution(mesh):
    ctx, tp = mesh.devices.shape
    fine = Mesh(mesh.devices.reshape(ctx, tp // 4, 2, 2), ("ctx",) + TP_AXES)
    return jax.shard_map(
        per_device,
        mesh=fine,
        in_specs=(
            P(TP_AXES, "ctx"),
            P(TP_AXES, "ctx"),
            P(TP_AXES, "ctx"),
            P(TP_AXES, "ctx"),
            P(TP_AXES),
            P(TP_AXES, None),
        ),
        out_specs=P(TP_AXES, "ctx"),
        check_vma=False,
    )
```

time: 198 us -> 84.4 us (0.43)
  the two profiles are of different devices: /device:TPU:1 before, /device:TPU:2 now
where the time goes in v1:
time: 84.4 us; the launch traced here: 83.8 us
  blocking collectives  31.9 us (38%)
  starting transfers between devices  26.8 us (32%)
  waiting for transfers between devices  8.33 us (10%)
  other arithmetic  6.45 us (8%)
  matrix products  5.85 us (7%)
  local copies, waits for them, and re-layouts  4.2 us (5%)
    all_to_all x1, blocking collectives, per_device(): lax.all_to_all(partial.astype(jnp.bfloat16).reshape(quads, width, tokens_...  23.5 us
    all_to_all x1, starting transfers between devices, per_device(): lax.all_to_all(send, 'ctx', split_axis=0, concat_axis=0, tiled=True)  13.5 us
    all_gather x1, blocking collectives, per_device(): gathered = lax.all_gather(mixed, GROUP, axis=0, tiled=False)  8.37 us
    ppermute x3, starting transfers between devices, per_device(): lax.ppermute(columns_of(place ^ r), GROUP, [(t, t ^ r) for t in range(gro...  7.75 us
    all_to_all x1, waiting for transfers between devices, per_device(): lax.all_to_all(send, 'ctx', split_axis=0, concat_axis=0, tiled=True)  5.99 us
    all_to_all x1, starting transfers between devices, per_device(): lax.all_to_all(convolve(blocks, channels), 'ctx', split_axis=0, concat_ax...  5.57 us
    dot_general x4, matrix products, per_device(): lax.dot_general(weights[r], lax.dynamic_index_in_dim(gathered, place ^ r,...  3.67 us
    select_n x3, other arithmetic, columns_of(): chosen = jnp.where(target == t, columns[t], chosen)  2.42 us
  transfers between devices with their start and end apart: 5, of which 2 were waited for; matrix products, arithmetic and copies ran while one was open for 13% of the time, Pallas kernels for 0%

profile of v1, /device:TPU:2, one launch (start us, length us, event | category | flops | bytes accessed | tf_op | source)
XLA Modules:
  0.0 83.8 jit_solution(952113243242228887)
XLA Ops:
  0.0 1.1 %fusion.26 = (bf16[32,8,256]{2,1,0:T(8,128)(2,1)S(1)}, bf16[32,8,256]{2,1,0:T(8,128)(2,1)S(1)}) fusion(bf16[256,256]{1,0:T(8,128)(2,1)} %param.13, bf16[256,256]{1,0:T(8,128)(2,1)} %param.12, f32[256,256]{1,0:T(8,128)} %param.15), kind=kLoop, calls=%fused_computation.53 | loop fusion | flops 327680 | bytes 786432 | tf_op jit(solution)/shard_map/reshape | solution.py:90
  1.1 0.7 pad_maximum_fusion.4
  1.9 13.5 %all-to-all-start = ((bf16[32,16,256]{2,1,0:T(8,128)(2,1)}), bf16[32,16,256]{2,1,0:T(8,128)(2,1)S(1)}, u32[]{:S(2)}, u32[]{:S(2)}) async-start(bf16[32,16,256]{2,1,0:T(8,128)(2,1)} %pad_maximum_fusion.4), calls=%async_computation | async-start | bytes 524288 | tf_op jit(solution)/shard_map/all_to_all | solution.py:95
  15.3 1.8 %fusion.43 = (bf16[256,256]{1,0:T(8,128)(2,1)S(1)}, bf16[256,256]{1,0:T(8,128)(2,1)S(1)}, bf16[256,256]{1,0:T(8,128)(2,1)S(1)}, bf16[256,256]{1,0:T(8,128)(2,1)S...) fusion(bf16[256,4096]{1,0:T(8,128)(2,1)} %param.17), kind=kLoop, calls=%fused_computation.71 | loop fusion | bytes 4194304 | tf_op jit(solution)/shard_map/slice | solution.py:101
  17.2 0.0 copy-start
  17.2 1.1 %select_select_fusion = bf16[256,1024]{1,0:T(8,128)(2,1)} fusion(pred[]{:T(512)S(6)} %eq.47, pred[]{:T(512)S(6)} %eq.46, pred[]{:T(512)S(6)} %eq.45, bf16[256,256]{1,0:T(8,128)(2,1)S(1)} %get-tuple-element.19, bf16[256,256]{1,0:T(8,128)(2,1)S(1)} %get-tuple-element.20, bf16[256,256]{1,0:T(8,128)(2,1)S(1)} %get-tuple-element.6, ...), kind=kLoop, calls=%fused_computation.16 | loop fusion | flops 9175040 | bytes 2621443 | tf_op jit(solution)/shard_map/jit(_where)/select_n | solution.py:112
  18.2 2.4 %collective-permute-start.2 = (bf16[256,1024]{1,0:T(8,128)(2,1)}, bf16[256,1024]{1,0:T(8,128)(2,1)}, u32[]{:S(2)}, u32[]{:S(2)}) collective-permute-start(bf16[256,1024]{1,0:T(8,128)(2,1)} %select_select_fusion), channel_id=1, source_target_pairs={{0,3},{1,2},{2,1},{3,0},{4,7},{5,6},{6,5},{7,4},{8,11},{9,10},{10,... | collective-permute-start | bytes 1572872 | tf_op jit(solution)/shard_map/ppermute | solution.py:116
  20.6 6.0 %all-to-all-done = bf16[32,16,256]{2,1,0:T(8,128)(2,1)S(1)} async-done(((bf16[32,16,256]{2,1,0:T(8,128)(2,1)}), bf16[32,16,256]{2,1,0:T(8,128)(2,1)S(1)}, u32[]{:S(2)}, u32[]{:S(2)}) %all-to-all-start) | async-done | bytes 262176 | tf_op jit(solution)/shard_map/all_to_all | solution.py:95
  26.6 0.0 copy-done
  26.6 0.4 fusion.45
  27.1 0.0 copy-start.5
  27.1 0.0 copy-start.6
  27.1 0.1 fusion.44
  27.2 0.0 copy-start.4
  27.2 0.7 copy-done.5
  27.8 0.0 copy-done.6
  27.9 0.2 add_convert_fusion
  28.1 0.1 copy-done.4
  28.2 0.5 fusion.3
  28.7 0.0 copy-start.3
  28.7 0.1 fusion.25
  28.8 0.1 fusion.24
  28.8 0.9 %copy-done.3 = bf16[2,256,512,1]{2,1,0,3:T(8,128)(2,1)S(1)} copy-done((bf16[2,256,512,1]{2,1,0,3:T(8,128)(2,1)S(1)}, bf16[2,256,512,1]{2,1,0,3:T(8,128)(2,1)}, u32[]{:S(2)}) %copy-start.3) | copy-done | bytes 524312
  29.8 0.3 fusion.13
  30.1 0.1 subtract_convert_fusion.1
  30.2 0.5 copy-done.8
  30.7 0.9 %fusion.2 = bf16[32,8,256]{2,1,0:T(8,128)(2,1)} fusion(bf16[256,528]{1,0:T(8,128)(2,1)S(1)} %copy-done.8, bf16[33,8,256]{2,1,0:T(8,128)(2,1)S(1)} %get-tuple-element.26, bf16[33,8,256]{2,1,0:T(8,128)(2,1)S(1)} %get-tuple-element.25), kind=kOutput, calls=%fused_computation.5 | convolution fusion | flops 69406720 | bytes 671744 | tf_op jit(solution)/shard_map/dot_general | solution.py:45
  31.6 5.6 %all-to-all-start.1 = ((bf16[32,8,256]{2,1,0:T(8,128)(2,1)}), bf16[32,8,256]{2,1,0:T(8,128)(2,1)S(1)}, u32[]{:S(2)}, u32[]{:S(2)}) async-start(bf16[32,8,256]{2,1,0:T(8,128)(2,1)} %fusion.2), calls=%async_computation.1 | async-start | bytes 262144 | tf_op jit(solution)/shard_map/all_to_all | solution.py:120
  37.2 0.3 select_select_fusion.1
  37.5 3.5 %collective-permute-start.1 = (bf16[256,1024]{1,0:T(8,128)(2,1)S(1)}, bf16[256,1024]{1,0:T(8,128)(2,1)S(1)}, u32[]{:S(2)}, u32[]{:S(2)}) collective-permute-start(bf16[256,1024]{1,0:T(8,128)(2,1)S(1)} %select_select_fusion.1), channel_id=1, source_target_pairs={{0,2},{1,3},{2,0},{3,1},{4,6},{5,7},{6,4},{7,5},{8,10},{9,11},{10,... | collective-permute-start | bytes 1572872 | tf_op jit(solution)/shard_map/ppermute | solution.py:116
  41.0 0.0 copy-start.1
  41.0 0.0 copy-start.2
  41.0 0.0 copy-start.7
  41.0 1.1 %select_select_fusion.2 = bf16[256,1024]{1,0:T(8,128)(2,1)} fusion(pred[]{:T(512)S(6)} %eq.41, pred[]{:T(512)S(6)} %eq.40, pred[]{:T(512)S(6)} %eq.39, bf16[256,256]{1,0:T(8,128)(2,1)S(1)} %get-tuple-element.19, bf16[256,256]{1,0:T(8,128)(2,1)S(1)} %get-tuple-element.20, bf16[256,256]{1,0:T(8,128)(2,1)S(1)} %get-tuple-element.6, ...), kind=kLoop, calls=%fused_computation.18 | loop fusion | flops 9175040 | bytes 2621443 | tf_op jit(solution)/shard_map/jit(_where)/select_n | solution.py:112
  42.1 1.9 %collective-permute-start = (bf16[256,1024]{1,0:T(8,128)(2,1)}, bf16[256,1024]{1,0:T(8,128)(2,1)}, u32[]{:S(2)}, u32[]{:S(2)}) collective-permute-start(bf16[256,1024]{1,0:T(8,128)(2,1)} %select_select_fusion.2), channel_id=1, source_target_pairs={{0,1},{1,0},{2,3},{3,2},{4,5},{5,4},{6,7},{7,6},{8,9},{9,8},{10,11... | collective-permute-start | bytes 1572872 | tf_op jit(solution)/shard_map/ppermute | solution.py:116
  44.1 2.3 %all-to-all-done.1 = bf16[32,8,256]{2,1,0:T(8,128)(2,1)S(1)} async-done(((bf16[32,8,256]{2,1,0:T(8,128)(2,1)}), bf16[32,8,256]{2,1,0:T(8,128)(2,1)S(1)}, u32[]{:S(2)}, u32[]{:S(2)}) %all-to-all-start.1) | async-done | bytes 131104 | tf_op jit(solution)/shard_map/all_to_all | solution.py:120
  46.4 0.0 copy-done.1
  46.4 1.0 %fusion.22 = bf16[256,256]{1,0:T(8,128)(2,1)S(1)} fusion(bf16[256,256]{1,0:T(8,128)(2,1)} %param.14, bf16[256,256]{1,0:T(8,128)(2,1)S(1)} %copy-done.1, bf16[256,256]{1,0:T(8,128)(2,1)S(1)} %copy-done.2, bf16[32,8,256]{2,1,0:T(8,128)(2,1)S(1)} %all-to-all-done.1, f32[256]{0:T(256)S(1)} %copy-done.7), kind=kLoop, calls=%fused_computation.48 | loop fusion | flops 589824 | bytes 656384 | tf_op jit(solution)/shard_map/convert_element_type | solution.py:126
  47.5 8.4 %all-gather = bf16[1024,256]{1,0:T(8,128)(2,1)S(1)} all-gather(bf16[256,256]{1,0:T(8,128)(2,1)S(1)} %fusion.22), channel_id=2, replica_groups=mesh['ctx'=32,'quad'=4,'pair'=2,'core'=2] {'pair','core'}, dimensions={0}, use_global_device_ids=true | all-gather | bytes 655360 | tf_op jit(solution)/shard_map/all_gather | solution.py:127
  55.8 0.0 collective-permute-done.2
  55.8 1.4 %fusion.27 = f32[1024,256]{1,0:T(8,128)S(1)} fusion(bf16[256,1024]{1,0:T(8,128)(2,1)} %collective-permute-done.2, bf16[4,256,256]{2,1,0:T(8,128)(2,1)S(1)} %bitcast.116, s32[]{:T(128)S(6)} %select_n.114), kind=kOutput, calls=%fused_computation.54 | convolution fusion | flops 134217728 | bytes 1703940 | tf_op jit(solution)/shard_map/dot_general | solution.py:129
  57.2 0.5 fusion.6
  57.8 0.0 collective-permute-done
  57.8 1.4 %convolution_add_fusion.1 = f32[1024,256]{1,0:T(8,128)S(1)} fusion(f32[1024,256]{1,0:T(8,128)S(1)} %fusion.6, bf16[256,1024]{1,0:T(8,128)(2,1)} %collective-permute-done, bf16[4,256,256]{2,1,0:T(8,128)(2,1)S(1)} %bitcast.118, s32[]{:T(128)S(6)} %select_n.100), kind=kOutput, calls=%fused_computation.2 | convolution fusion | flops 134479872 | bytes 2752516 | tf_op jit(solution)/shard_map/dot_general | solution.py:129
  59.2 0.0 collective-permute-done.1
  59.2 0.4 fusion.1
  59.5 23.5 %all_to_all.15 = bf16[4,256,256]{2,1,0:T(8,128)(2,1)S(1)} all-to-all(bf16[4,256,256]{2,1,0:T(8,128)(2,1)S(1)} %bitcast.115), channel_id=1, replica_groups=mesh['ctx'=32,'quad'=4,'pair'=2,'core'=2] {'quad'}, dimensions={0} | all-to-all | bytes 1048576 | tf_op jit(solution)/shard_map/all_to_all | solution.py:137
  83.0 0.7 reduce_sum.12
  (3 shorter events, 0.0 us)
Async XLA Ops:
  1.9 24.8 %all-to-all-start = ((bf16[32,16,256]{2,1,0:T(8,128)(2,1)}), bf16[32,16,256]{2,1,0:T(8,128)(2,1)S(1)}, u32[]{:S(2)}, u32[]{:S(2)}) async-start(bf16[32,16,256]{2,1,0:T(8,128)(2,1)} %pad_maximum_fusion.4), calls=%async_computation | async-start | bytes 524288 | tf_op jit(solution)/shard_map/all_to_all | solution.py:95
  17.2 9.4 %copy-start = (bf16[1056,512]{1,0:T(8,128)(2,1)S(1)}, bf16[1056,512]{1,0:T(8,128)(2,1)}, u32[]{:S(2)}) copy-start(bf16[1056,512]{1,0:T(8,128)(2,1)} %constant.39.clone) | copy-start | bytes 3244036
  18.2 37.6 %collective-permute-start.2 = (bf16[256,1024]{1,0:T(8,128)(2,1)}, bf16[256,1024]{1,0:T(8,128)(2,1)}, u32[]{:S(2)}, u32[]{:S(2)}) collective-permute-start(bf16[256,1024]{1,0:T(8,128)(2,1)} %select_select_fusion), channel_id=1, source_target_pairs={{0,3},{1,2},{2,1},{3,0},{4,7},{5,6},{6,5},{7,4},{8,11},{9,10},{10,... | collective-permute-start | bytes 1572872 | tf_op jit(solution)/shard_map/ppermute | solution.py:116
  27.1 0.8 copy-start.5
  27.1 0.8 copy-start.6
  27.2 1.1 %copy-start.4 = (bf16[2,256,512,1,1]{2,1,0,4,3:T(8,128)(2,1)S(1)}, bf16[2,256,512,1,1]{2,1,0,4,3:T(8,128)(2,1)}, u32[]{:S(2)}) copy-start(bf16[2,256,512,1,1]{2,1,0,4,3:T(8,128)(2,1)} %constant.49) | copy-start | bytes 1572868
  28.7 1.0 %copy-start.3 = (bf16[2,256,512,1]{2,1,0,3:T(8,128)(2,1)S(1)}, bf16[2,256,512,1]{2,1,0,3:T(8,128)(2,1)}, u32[]{:S(2)}) copy-start(bf16[2,256,512,1]{2,1,0,3:T(8,128)(2,1)} %constant.50) | copy-start | bytes 1572868
  29.7 1.0 %copy-start.8 = (bf16[256,528]{1,0:T(8,128)(2,1)S(1)}, bf16[256,528]{1,0:T(8,128)(2,1)}, u32[]{:S(2)}) copy-start(bf16[256,528]{1,0:T(8,128)(2,1)} %constant.42.clone) | copy-start | bytes 811012
  31.6 14.8 %all-to-all-start.1 = ((bf16[32,8,256]{2,1,0:T(8,128)(2,1)}), bf16[32,8,256]{2,1,0:T(8,128)(2,1)S(1)}, u32[]{:S(2)}, u32[]{:S(2)}) async-start(bf16[32,8,256]{2,1,0:T(8,128)(2,1)} %fusion.2), calls=%async_computation.1 | async-start | bytes 262144 | tf_op jit(solution)/shard_map/all_to_all | solution.py:120
  37.5 21.7 %collective-permute-start.1 = (bf16[256,1024]{1,0:T(8,128)(2,1)S(1)}, bf16[256,1024]{1,0:T(8,128)(2,1)S(1)}, u32[]{:S(2)}, u32[]{:S(2)}) collective-permute-start(bf16[256,1024]{1,0:T(8,128)(2,1)S(1)} %select_select_fusion.1), channel_id=1, source_target_pairs={{0,2},{1,3},{2,0},{3,1},{4,6},{5,7},{6,4},{7,5},{8,10},{9,11},{10,... | collective-permute-start | bytes 1572872 | tf_op jit(solution)/shard_map/ppermute | solution.py:116
  41.0 5.4 %copy-start.1 = (bf16[256,256]{1,0:T(8,128)(2,1)S(1)}, bf16[256,256]{1,0:T(8,128)(2,1)}, u32[]{:S(2)}) copy-start(bf16[256,256]{1,0:T(8,128)(2,1)} %param.13) | copy-start | bytes 393220
  41.0 5.4 %copy-start.2 = (bf16[256,256]{1,0:T(8,128)(2,1)S(1)}, bf16[256,256]{1,0:T(8,128)(2,1)}, u32[]{:S(2)}) copy-start(bf16[256,256]{1,0:T(8,128)(2,1)} %param.12) | copy-start | bytes 393220
  41.0 5.4 %copy-start.7 = (f32[256]{0:T(256)S(1)}, f32[256]{0:T(256)}, u32[]{:S(2)}) copy-start(f32[256]{0:T(256)} %param.16) | copy-start | bytes 3076
  42.1 15.6 %collective-permute-start = (bf16[256,1024]{1,0:T(8,128)(2,1)}, bf16[256,1024]{1,0:T(8,128)(2,1)}, u32[]{:S(2)}, u32[]{:S(2)}) collective-permute-start(bf16[256,1024]{1,0:T(8,128)(2,1)} %select_select_fusion.2), channel_id=1, source_target_pairs={{0,1},{1,0},{2,3},{3,2},{4,5},{5,4},{6,7},{7,6},{8,9},{9,8},{10,11... | collective-permute-start | bytes 1572872 | tf_op jit(solution)/shard_map/ppermute | solution.py:116

commit v2 on v1

v2 whole, which is shorter than its diff:
```python
import math

import jax
import jax.numpy as jnp
import numpy as np
from jax import lax
from jax.experimental import pallas as pl
from jax.experimental.pallas import tpu as pltpu
from jax.sharding import Mesh
from jax.sharding import PartitionSpec as P

TP_AXES = ("quad", "pair", "core")
GROUP = ("pair", "core")
MIB = 1 << 20


def targets_of(quad, pair, core, quads):
    onward = jnp.where(pair == 1, 1, -1)
    chips = [
        ((quad + 2 * onward) % quads, 1 - pair),
        ((quad + onward) % quads, pair),
        ((quad + onward) % quads, 1 - pair),
        (quad, pair),
    ]
    return [(q * 2 + p) * 2 + core for q, p in chips]


def send_to_target(share, step, quads):
    pairs = []
    for quad in range(quads):
        for pair in range(2):
            onward = 1 if pair == 1 else -1
            q = (quad + (2 * onward if step == 0 else onward)) % quads
            p = pair if step == 1 else 1 - pair
            pairs += [((quad * 2 + pair) * 2 + c, (q * 2 + p) * 2 + c) for c in range(2)]
    return lax.ppermute(share, TP_AXES, pairs)


def arrange_kernel(group, width, order_ref, weight_ref, *out_refs):
    for r in range(group):
        for i in range(group):
            start = pl.multiple_of(order_ref[r * group + i] * width, width)
            out_refs[r][i * width : (i + 1) * width, :] = weight_ref[:, pl.ds(start, width)].T
    out_refs[group][0] = order_ref[0]


def arrange(out_weight, order, group, width):
    rows = out_weight.shape[0]
    piece = jax.ShapeDtypeStruct((group * width, rows), out_weight.dtype)
    return pl.pallas_call(
        lambda *refs: arrange_kernel(group, width, *refs),
        out_shape=[piece] * group + [jax.ShapeDtypeStruct((1,), jnp.int32)],
        in_specs=[
            pl.BlockSpec(memory_space=pltpu.SMEM),
            pl.BlockSpec(memory_space=pltpu.VMEM),
        ],
        out_specs=[pl.BlockSpec(memory_space=pltpu.VMEM)] * group
        + [pl.BlockSpec(memory_space=pltpu.SMEM)],
        compiler_params=pltpu.CompilerParams(vmem_limit_bytes=16 * MIB),
        cost_estimate=pl.CostEstimate(
            flops=0, bytes_accessed=4 * rows * group * group * width, transcendentals=0
        ),
    )(order, out_weight)


def project_kernel(group, place_ref, mixed_ref, *refs):
    weight_refs, out_refs = refs[:group], refs[group:]
    rows = mixed_ref.shape[0] // group
    width = out_refs[0].shape[0]
    mixed = [
        mixed_ref[pl.ds(pl.multiple_of((place_ref[0] ^ r) * rows, rows), rows), :]
        for r in range(group)
    ]
    for i in range(group):
        total = None
        for r in range(group):
            term = jnp.dot(
                weight_refs[r][i * width : (i + 1) * width, :],
                mixed[r],
                preferred_element_type=jnp.float32,
            )
            total = term if total is None else total + term
        out_refs[i][...] = total.astype(out_refs[i].dtype)


def project(place, mixed, weights, width):
    group = len(weights)
    tokens = mixed.shape[1]
    share = jax.ShapeDtypeStruct((width, tokens), mixed.dtype)
    return pl.pallas_call(
        lambda *refs: project_kernel(group, *refs),
        out_shape=[share] * group,
        in_specs=[pl.BlockSpec(memory_space=pltpu.SMEM)]
        + [pl.BlockSpec(memory_space=pltpu.VMEM)] * (1 + group),
        out_specs=[pl.BlockSpec(memory_space=pltpu.VMEM)] * group,
        compiler_params=pltpu.CompilerParams(vmem_limit_bytes=16 * MIB),
        cost_estimate=pl.CostEstimate(
            flops=2 * mixed.size * group * width,
            bytes_accessed=2 * (mixed.size + sum(w.size for w in weights) + group * share.size),
            transcendentals=0,
        ),
    )(place, mixed, *weights)


def dft_tables(blocks, tokens, channels):
    period = 2 * blocks
    total = period * tokens
    low = blocks + 1
    k1 = np.arange(low)
    i = np.arange(blocks)
    s = np.arange(tokens)
    first = 2 * np.pi * (np.outer(k1, i) % period) / period
    turn = 2 * np.pi * (np.outer(k1, s) % total) / total
    square = 2 * np.pi * (np.outer(s, s) % tokens) / tokens
    both = 2 * channels
    front = np.concatenate(
        [np.kron(np.cos(first), np.eye(both)), np.kron(-np.sin(first), np.eye(both))]
    )
    weight = np.where((k1 == 0) | (k1 == blocks), 1.0, 2.0)[:, None] / total
    back = np.concatenate(
        [
            np.kron((weight * np.cos(first)).T, np.eye(channels)),
            np.kron(-(weight * np.sin(first)).T, np.eye(channels)),
        ],
        axis=1,
    )
    matrices = [jnp.asarray(m, jnp.bfloat16) for m in (front, np.cos(square), np.sin(square), back)]
    turns = [jnp.asarray(m, jnp.float32) for m in (np.cos(turn), np.sin(turn))]
    return matrices, turns


def matmul(left, right):
    return jnp.dot(left, right, preferred_element_type=jnp.float32)


def convolve_kernel(
    channels, in_ref, front_ref, square_cos_ref, square_sin_ref, back_ref, cos_ref, sin_ref, after_ref, out_ref
):
    del after_ref
    low, tokens = cos_ref.shape
    both = 2 * channels
    turn_cos = cos_ref[...].reshape(low, 1, tokens)
    turn_sin = sin_ref[...].reshape(low, 1, tokens)
    spread = matmul(front_ref[...], in_ref[...])
    real = spread[: low * both].reshape(low, both, tokens)
    imag = spread[low * both :].reshape(low, both, tokens)
    turned_real = (real * turn_cos + imag * turn_sin).reshape(low * both, tokens).astype(jnp.bfloat16)
    turned_imag = (imag * turn_cos - real * turn_sin).reshape(low * both, tokens).astype(jnp.bfloat16)
    square_cos, square_sin = square_cos_ref[...], square_sin_ref[...]
    real = (matmul(turned_real, square_cos) + matmul(turned_imag, square_sin)).reshape(low, both, tokens)
    imag = (matmul(turned_imag, square_cos) - matmul(turned_real, square_sin)).reshape(low, both, tokens)
    sig_real, tap_real = real[:, :channels], real[:, channels:]
    sig_imag, tap_imag = imag[:, :channels], imag[:, channels:]
    prod_real = sig_real * tap_real - sig_imag * tap_imag
    prod_imag = sig_real * tap_imag + sig_imag * tap_real
    prod_real = prod_real.reshape(low * channels, tokens).astype(jnp.bfloat16)
    prod_imag = prod_imag.reshape(low * channels, tokens).astype(jnp.bfloat16)
    real = matmul(prod_real, square_cos) - matmul(prod_imag, square_sin)
    imag = matmul(prod_imag, square_cos) + matmul(prod_real, square_sin)
    real, imag = real.reshape(low, channels, tokens), imag.reshape(low, channels, tokens)
    rows = jnp.concatenate(
        [real * turn_cos - imag * turn_sin, real * turn_sin + imag * turn_cos], axis=0
    )
    out_ref[...] = matmul(
        back_ref[...], rows.reshape(2 * low * channels, tokens).astype(jnp.bfloat16)
    ).astype(out_ref.dtype)


def convolve(blocks_in, channels, after):
    blocks, both, tokens = blocks_in.shape
    matrices, turns = dft_tables(blocks, tokens, channels)
    out = pl.pallas_call(
        lambda *refs: convolve_kernel(channels, *refs),
        out_shape=jax.ShapeDtypeStruct((blocks * channels, tokens), jnp.bfloat16),
        in_specs=[pl.BlockSpec(memory_space=pltpu.VMEM)] * 7 + [pl.BlockSpec(memory_space=pltpu.SMEM)],
        out_specs=pl.BlockSpec(memory_space=pltpu.VMEM),
        compiler_params=pltpu.CompilerParams(vmem_limit_bytes=32 * MIB),
        cost_estimate=pl.CostEstimate(
            flops=800_000_000, bytes_accessed=3_000_000, transcendentals=0
        ),
    )(blocks_in.reshape(blocks * both, tokens), *matrices, *turns, after)
    return out.reshape(blocks, channels, tokens)


def outgoing_kernel(devices, signal_ref, gate_ref, taps_ref, out_ref):
    rows, tokens = signal_ref.shape
    gated = signal_ref[...].astype(jnp.float32) * gate_ref[...].astype(jnp.float32)
    both = jnp.concatenate(
        [
            gated.reshape(devices, rows // devices, tokens),
            taps_ref[...].reshape(devices, rows // devices, tokens),
        ],
        axis=1,
    )
    out_ref[...] = both.reshape(2 * rows, tokens).astype(out_ref.dtype)


def outgoing(signal, pre_gate, filter_taps, devices):
    rows, tokens = signal.shape
    out = pl.pallas_call(
        lambda *refs: outgoing_kernel(devices, *refs),
        out_shape=jax.ShapeDtypeStruct((2 * rows, tokens), jnp.bfloat16),
        in_specs=[pl.BlockSpec(memory_space=pltpu.VMEM)] * 3,
        out_specs=pl.BlockSpec(memory_space=pltpu.VMEM),
    )(signal, pre_gate, filter_taps)
    return out.reshape(devices, 2 * rows // devices, tokens)


def per_device(signal, pre_gate, post_gate, filter_taps, skip_gain, out_weight):
    channels_here, tokens_here = signal.shape
    devices = lax.axis_size("ctx")
    channels = channels_here // devices
    quads = lax.axis_size("quad")
    group = lax.axis_size("pair") * lax.axis_size("core")
    features = out_weight.shape[1]
    width = features // (quads * group)

    send = outgoing(signal, pre_gate, filter_taps, devices)
    blocks = lax.all_to_all(send, "ctx", split_axis=0, concat_axis=0, tiled=True)

    quad, pair, core = (lax.axis_index(axis) for axis in TP_AXES)
    place = pair * 2 + core
    order = [
        index
        for r in range(group)
        for index in targets_of(quad, pair ^ (r >> 1), core ^ (r & 1), quads)
    ]
    *weights, arranged = arrange(out_weight, jnp.stack(order).astype(jnp.int32), group, width)
    weights = [weights[0]] + [
        lax.ppermute(weights[r], GROUP, [(t, t ^ r) for t in range(group)])
        for r in range(1, group)
    ]

    convolved = lax.all_to_all(
        convolve(blocks, channels, arranged), "ctx", split_axis=0, concat_axis=0, tiled=True
    ).reshape(channels_here, tokens_here)
    gated_input = signal.astype(jnp.float32) * pre_gate.astype(jnp.float32)
    mixed = (
        post_gate.astype(jnp.float32)
        * (convolved.astype(jnp.float32) + skip_gain[:, None] * gated_input)
    ).astype(jnp.bfloat16)
    gathered = lax.all_gather(mixed, GROUP, axis=0, tiled=True)
    shares = project(place.astype(jnp.int32).reshape(1), gathered, weights, width)
    shares = [send_to_target(shares[step], step, quads) for step in range(3)] + [shares[3]]
    return sum(share.astype(jnp.float32) for share in shares).astype(jnp.bfloat16)


def solution(mesh):
    ctx, tp = mesh.devices.shape
    fine = Mesh(mesh.devices.reshape(ctx, tp // 4, 2, 2), ("ctx",) + TP_AXES)
    return jax.shard_map(
        per_device,
        mesh=fine,
        in_specs=(
            P(TP_AXES, "ctx"),
            P(TP_AXES, "ctx"),
            P(TP_AXES, "ctx"),
            P(TP_AXES, "ctx"),
            P(TP_AXES),
            P(TP_AXES, None),
        ),
        out_specs=P(TP_AXES, "ctx"),
        check_vma=False,
    )
```

time: 84.4 us -> 90.6 us (1.073)
  the two profiles are of different devices: /device:TPU:2 before, /device:TPU:1 now
where the time goes in v2:
time: 90.6 us; the launch traced here: 90.1 us
  starting transfers between devices  43.1 us (48%)
  blocking collectives  24.3 us (27%)
  waiting for transfers between devices  10.4 us (11%)
  Pallas kernels  7.5 us (8%)
  local copies, waits for them, and re-layouts  2.61 us (3%)
  other arithmetic  1.87 us (2%)
    all_gather x1, blocking collectives, per_device(): gathered = lax.all_gather(mixed, GROUP, axis=0, tiled=True)  24.3 us
    ppermute x3, starting transfers between devices, send_to_target(): return lax.ppermute(share, TP_AXES, pairs)  13.9 us
    all_to_all x1, starting transfers between devices, per_device(): lax.all_to_all(send, 'ctx', split_axis=0, concat_axis=0, tiled=True)  13.7 us
    ppermute x3, starting transfers between devices, per_device(): lax.ppermute(weights[r], GROUP, [(t, t ^ r) for t in range(group)])  9.19 us
    all_to_all x1, starting transfers between devices, per_device(): lax.all_to_all(convolve(blocks, channels, arranged), 'ctx', split_axis=0,...  6.29 us
    all_to_all x1, waiting for transfers between devices, per_device(): lax.all_to_all(send, 'ctx', split_axis=0, concat_axis=0, tiled=True)  6.05 us
    ppermute x3, waiting for transfers between devices, send_to_target(): return lax.ppermute(share, TP_AXES, pairs)  4.31 us
    pallas_call x1, Pallas kernels, convolve(): pl.pallas_call(lambda *refs: convolve_kernel(channels, *refs), out_shape=...  3.05 us
  transfers between devices with their start and end apart: 8, of which 3 were waited for; matrix products, arithmetic and copies ran while one was open for 1% of the time, Pallas kernels for 2%

profile of v2, /device:TPU:1, one launch (start us, length us, event | category | flops | bytes accessed | tf_op | source)
XLA Modules:
  0.0 90.1 jit_solution(17803337023789747075)
XLA Ops:
  0.0 0.0 copy-start.2
  0.0 0.0 copy-start.3
  0.0 0.0 copy-start.1
  0.0 1.9 %shard_map.118 = bf16[512,256]{1,0:T(8,128)(2,1)} custom-call(bf16[256,256]{1,0:T(8,128)(2,1)} %refs_0_.1, bf16[256,256]{1,0:T(8,128)(2,1)} %refs_1_.3, f32[256,256]{1,0:T(8,128)} %refs_2_.2), custom_call_target="tpu_custom_call" | custom-call | tf_op jit(solution)/shard_map/pallas_call | solution.py:200
  1.9 13.7 %all-to-all-start = ((bf16[32,16,256]{2,1,0:T(8,128)(2,1)}), bf16[32,16,256]{2,1,0:T(8,128)(2,1)S(1)}, u32[]{:S(2)}, u32[]{:S(2)}) async-start(bf16[32,16,256]{2,1,0:T(8,128)(2,1)} %bitcast.24), calls=%async_computation | async-start | bytes 524288 | tf_op jit(solution)/shard_map/all_to_all | solution.py:219
  15.8 0.1 stack.67.refs_0_
  15.9 0.0 copy-start
  15.9 1.6 %copy-done = bf16[256,4096]{1,0:T(8,128)(2,1)S(1)} copy-done((bf16[256,4096]{1,0:T(8,128)(2,1)S(1)}, bf16[256,4096]{1,0:T(8,128)(2,1)}, u32[]{:S(2)}) %copy-start) | copy-done | bytes 2097176
  17.4 0.0 copy-start.5
  17.5 0.0 copy-start.6
  17.5 1.8 %shard_map.119 = (bf16[1024,256]{1,0:T(8,128)(2,1)S(1)}, bf16[1024,256]{1,0:T(8,128)(2,1)}, bf16[1024,256]{1,0:T(8,128)(2,1)S(1)}, bf16[1024,256]{1,0:T(8,128)(2,1)S(1)}, s32[1]{0:T(128)}) custom-call(s32[16]{0:T(128)S(1)} %stack.67.refs_0_, bf16[256,4096]{1,0:T(8,128)(2,1)S(1)} %copy-done), custom_call_target="tpu_custom_call" | custom-call | bytes 4194304 | tf_op jit(solution)/shard_map/pallas_call | solution.py:50
  19.3 0.0 copy-start.7
  19.3 6.0 %all-to-all-done = bf16[32,16,256]{2,1,0:T(8,128)(2,1)S(1)} async-done(((bf16[32,16,256]{2,1,0:T(8,128)(2,1)}), bf16[32,16,256]{2,1,0:T(8,128)(2,1)S(1)}, u32[]{:S(2)}, u32[]{:S(2)}) %all-to-all-start) | async-done | bytes 262176 | tf_op jit(solution)/shard_map/all_to_all | solution.py:219
  25.3 0.0 copy-done.2
  25.3 0.0 copy-done.3
  25.4 0.0 copy-done.1
  25.4 0.0 copy-done.5
  25.4 0.0 copy-done.6
  25.4 0.0 copy-start.4
  25.4 0.9 copy-done.4
  26.3 3.0 %shard_map.120 = bf16[256,256]{1,0:T(8,128)(2,1)} custom-call(bf16[512,256]{1,0:T(8,128)(2,1)S(1)} %bitcast.23, bf16[1056,512]{1,0:T(8,128)(2,1)S(1)} %copy-done.1, bf16[256,256]{1,0:T(8,128)(2,1)S(1)} %copy-done.4, bf16[256,256]{1,0:T(8,128)(2,1)S(1)} %copy-done.3, bf16[256,528]{1,0:T(8,128)(2,1)S(1)} %copy-done.2, f32[33,256]{1,0:T(8,128)S(1)} %copy-done.6, ...), custom_call_target="tpu_custom_call" | custom-call | flops 800000000 | bytes 3000000 | tf_op jit(solution)/shard_map/pallas_call | solution.py:172
  29.3 6.3 %all-to-all-start.1 = ((bf16[32,8,256]{2,1,0:T(8,128)(2,1)}), bf16[32,8,256]{2,1,0:T(8,128)(2,1)S(1)}, u32[]{:S(2)}, u32[]{:S(2)}) async-start(bf16[32,8,256]{2,1,0:T(8,128)(2,1)} %bitcast.19), calls=%async_computation.1 | async-start | bytes 262144 | tf_op jit(solution)/shard_map/all_to_all | solution.py:234
  35.6 3.7 %collective-permute-start = (bf16[1024,256]{1,0:T(8,128)(2,1)}, bf16[1024,256]{1,0:T(8,128)(2,1)S(1)}, u32[]{:S(2)}, u32[]{:S(2)}) collective-permute-start(bf16[1024,256]{1,0:T(8,128)(2,1)} %get-tuple-element.16), channel_id=1, source_target_pairs={{0,1},{1,0},{2,3},{3,2},{4,5},{5,4},{6,7},{7,6},{8,9},{9,8},{10,11... | collective-permute-start | bytes 1572872 | tf_op jit(solution)/shard_map/ppermute | solution.py:230
  39.4 3.2 %collective-permute-start.1 = (bf16[1024,256]{1,0:T(8,128)(2,1)S(1)}, bf16[1024,256]{1,0:T(8,128)(2,1)S(1)}, u32[]{:S(2)}, u32[]{:S(2)}) collective-permute-start(bf16[1024,256]{1,0:T(8,128)(2,1)S(1)} %get-tuple-element.17), channel_id=1, source_target_pairs={{0,2},{1,3},{2,0},{3,1},{4,6},{5,7},{6,4},{7,5},{8,10},{9,11},{10,... | collective-permute-start | bytes 1572872 | tf_op jit(solution)/shard_map/ppermute | solution.py:230
  42.6 2.3 %collective-permute-start.2 = (bf16[1024,256]{1,0:T(8,128)(2,1)S(1)}, bf16[1024,256]{1,0:T(8,128)(2,1)S(1)}, u32[]{:S(2)}, u32[]{:S(2)}) collective-permute-start(bf16[1024,256]{1,0:T(8,128)(2,1)S(1)} %get-tuple-element.18), channel_id=1, source_target_pairs={{0,3},{1,2},{2,1},{3,0},{4,7},{5,6},{6,5},{7,4},{8,11},{9,10},{10,... | collective-permute-start | bytes 1572872 | tf_op jit(solution)/shard_map/ppermute | solution.py:230
  44.9 0.0 all-to-all-done.1
  44.9 0.0 copy-done.7
  44.9 1.1 %fusion.1 = bf16[256,256]{1,0:T(8,128)(2,1)S(1)} fusion(bf16[256,256]{1,0:T(8,128)(2,1)} %refs_1_.3, bf16[256,256]{1,0:T(8,128)(2,1)} %refs_0_.1, bf16[256,256]{1,0:T(8,128)(2,1)} %param.14, bf16[32,8,256]{2,1,0:T(8,128)(2,1)S(1)} %all-to-all-done.1, f32[256]{0:T(256)S(1)} %copy-done.7), kind=kLoop, calls=%fused_computation.2 | loop fusion | flops 589824 | bytes 656384 | tf_op jit(solution)/shard_map/convert_element_type | solution.py:241
  46.0 24.3 %all_gather.3.refs_1_ = bf16[1024,256]{1,0:T(8,128)(2,1)S(1)} all-gather(bf16[256,256]{1,0:T(8,128)(2,1)S(1)} %fusion.1), channel_id=1, replica_groups=mesh['ctx'=32,'quad'=4,'pair'=2,'core'=2] {'pair','core'}, dimensions={0}, use_global_device_ids=true | all-gather | bytes 655360 | tf_op jit(solution)/shard_map/all_gather | solution.py:242
  70.3 0.0 collective-permute-done.refs_3_
  70.4 0.0 collective-permute-done.1.refs_4_
  70.4 0.0 collective-permute-done.2.refs_5_
  70.4 0.7 shard_map.121
  71.1 6.7 %collective-permute-start.3 = (bf16[256,256]{1,0:T(8,128)(2,1)S(1)}, bf16[256,256]{1,0:T(8,128)(2,1)S(1)}, u32[]{:S(2)}, u32[]{:S(2)}) collective-permute-start(bf16[256,256]{1,0:T(8,128)(2,1)S(1)} %get-tuple-element.19), channel_id=1, source_target_pairs={{0,10},{1,11},{2,8},{3,9},{4,14},{5,15},{6,12},{7,13},{8,2},{9,3},... | collective-permute-start | bytes 393224 | tf_op jit(solution)/shard_map/ppermute | solution.py:36
  77.8 2.9 %collective-permute-start.4 = (bf16[256,256]{1,0:T(8,128)(2,1)S(1)}, bf16[256,256]{1,0:T(8,128)(2,1)S(1)}, u32[]{:S(2)}, u32[]{:S(2)}) collective-permute-start(bf16[256,256]{1,0:T(8,128)(2,1)S(1)} %get-tuple-element.20), channel_id=1, source_target_pairs={{0,12},{1,13},{2,6},{3,7},{4,0},{5,1},{6,10},{7,11},{8,4},{9,5},{1... | collective-permute-start | bytes 393224 | tf_op jit(solution)/shard_map/ppermute | solution.py:36
  80.6 4.4 %collective-permute-start.5 = (bf16[256,256]{1,0:T(8,128)(2,1)S(1)}, bf16[256,256]{1,0:T(8,128)(2,1)S(1)}, u32[]{:S(2)}, u32[]{:S(2)}) collective-permute-start(bf16[256,256]{1,0:T(8,128)(2,1)S(1)} %get-tuple-element.21), channel_id=1, source_target_pairs={{0,14},{1,15},{2,4},{3,5},{4,2},{5,3},{6,8},{7,9},{8,6},{9,7},{10,... | collective-permute-start | bytes 393224 | tf_op jit(solution)/shard_map/ppermute | solution.py:36
  85.0 0.0 collective-permute-done.3
  85.1 2.5 %collective-permute-done.4 = bf16[256,256]{1,0:T(8,128)(2,1)S(1)} collective-permute-done((bf16[256,256]{1,0:T(8,128)(2,1)S(1)}, bf16[256,256]{1,0:T(8,128)(2,1)S(1)}, u32[]{:S(2)}, u32[]{:S(2)}) %collective-permute-start.4) | collective-permute-done | bytes 131104 | tf_op jit(solution)/shard_map/ppermute | solution.py:36
  87.6 1.8 %collective-permute-done.5 = bf16[256,256]{1,0:T(8,128)(2,1)S(1)} collective-permute-done((bf16[256,256]{1,0:T(8,128)(2,1)S(1)}, bf16[256,256]{1,0:T(8,128)(2,1)S(1)}, u32[]{:S(2)}, u32[]{:S(2)}) %collective-permute-start.5) | collective-permute-done | bytes 131104 | tf_op jit(solution)/shard_map/ppermute | solution.py:36
  89.4 0.7 add_convert_fusion
Async XLA Ops:
  0.0 25.3 %copy-start.2 = (bf16[256,528]{1,0:T(8,128)(2,1)S(1)}, bf16[256,528]{1,0:T(8,128)(2,1)}, u32[]{:S(2)}) copy-start(bf16[256,528]{1,0:T(8,128)(2,1)} %constant.73.clone.refs_4_) | copy-start | bytes 811012
  0.0 25.3 %copy-start.3 = (bf16[256,256]{1,0:T(8,128)(2,1)S(1)}, bf16[256,256]{1,0:T(8,128)(2,1)}, u32[]{:S(2)}) copy-start(bf16[256,256]{1,0:T(8,128)(2,1)} %constant.72.clone.refs_3_) | copy-start | bytes 393220
  0.0 25.3 %copy-start.1 = (bf16[1056,512]{1,0:T(8,128)(2,1)S(1)}, bf16[1056,512]{1,0:T(8,128)(2,1)}, u32[]{:S(2)}) copy-start(bf16[1056,512]{1,0:T(8,128)(2,1)} %constant.70.clone.refs_1_) | copy-start | bytes 3244036
  1.9 23.4 %all-to-all-start = ((bf16[32,16,256]{2,1,0:T(8,128)(2,1)}), bf16[32,16,256]{2,1,0:T(8,128)(2,1)S(1)}, u32[]{:S(2)}, u32[]{:S(2)}) async-start(bf16[32,16,256]{2,1,0:T(8,128)(2,1)} %bitcast.24), calls=%async_computation | async-start | bytes 524288 | tf_op jit(solution)/shard_map/all_to_all | solution.py:219
  15.9 1.6 %copy-start = (bf16[256,4096]{1,0:T(8,128)(2,1)S(1)}, bf16[256,4096]{1,0:T(8,128)(2,1)}, u32[]{:S(2)}) copy-start(bf16[256,4096]{1,0:T(8,128)(2,1)} %refs_1_.4) | copy-start | bytes 6291460
  17.4 7.9 %copy-start.5 = (f32[33,256]{1,0:T(8,128)S(1)}, f32[33,256]{1,0:T(8,128)}, u32[]{:S(2)}) copy-start(f32[33,256]{1,0:T(8,128)} %constant.75.clone.refs_6_) | copy-start | bytes 101380
  17.5 7.9 %copy-start.6 = (f32[33,256]{1,0:T(8,128)S(1)}, f32[33,256]{1,0:T(8,128)}, u32[]{:S(2)}) copy-start(f32[33,256]{1,0:T(8,128)} %constant.74.clone.refs_5_) | copy-start | bytes 101380
  19.3 25.6 %copy-start.7 = (f32[256]{0:T(256)S(1)}, f32[256]{0:T(256)}, u32[]{:S(2)}) copy-start(f32[256]{0:T(256)} %param.16) | copy-start | bytes 3076
  25.4 0.9 %copy-start.4 = (bf16[256,256]{1,0:T(8,128)(2,1)S(1)}, bf16[256,256]{1,0:T(8,128)(2,1)}, u32[]{:S(2)}) copy-start(bf16[256,256]{1,0:T(8,128)(2,1)} %constant.71.clone.refs_2_) | copy-start | bytes 393220
  29.3 15.6 %all-to-all-start.1 = ((bf16[32,8,256]{2,1,0:T(8,128)(2,1)}), bf16[32,8,256]{2,1,0:T(8,128)(2,1)S(1)}, u32[]{:S(2)}, u32[]{:S(2)}) async-start(bf16[32,8,256]{2,1,0:T(8,128)(2,1)} %bitcast.19), calls=%async_computation.1 | async-start | bytes 262144 | tf_op jit(solution)/shard_map/all_to_all | solution.py:234
  35.6 34.7 %collective-permute-start = (bf16[1024,256]{1,0:T(8,128)(2,1)}, bf16[1024,256]{1,0:T(8,128)(2,1)S(1)}, u32[]{:S(2)}, u32[]{:S(2)}) collective-permute-start(bf16[1024,256]{1,0:T(8,128)(2,1)} %get-tuple-element.16), channel_id=1, source_target_pairs={{0,1},{1,0},{2,3},{3,2},{4,5},{5,4},{6,7},{7,6},{8,9},{9,8},{10,11... | collective-permute-start | bytes 1572872 | tf_op jit(solution)/shard_map/ppermute | solution.py:230
  39.4 31.0 %collective-permute-start.1 = (bf16[1024,256]{1,0:T(8,128)(2,1)S(1)}, bf16[1024,256]{1,0:T(8,128)(2,1)S(1)}, u32[]{:S(2)}, u32[]{:S(2)}) collective-permute-start(bf16[1024,256]{1,0:T(8,128)(2,1)S(1)} %get-tuple-element.17), channel_id=1, source_target_pairs={{0,2},{1,3},{2,0},{3,1},{4,6},{5,7},{6,4},{7,5},{8,10},{9,11},{10,... | collective-permute-start | bytes 1572872 | tf_op jit(solution)/shard_map/ppermute | solution.py:230
  42.6 27.8 %collective-permute-start.2 = (bf16[1024,256]{1,0:T(8,128)(2,1)S(1)}, bf16[1024,256]{1,0:T(8,128)(2,1)S(1)}, u32[]{:S(2)}, u32[]{:S(2)}) collective-permute-start(bf16[1024,256]{1,0:T(8,128)(2,1)S(1)} %get-tuple-element.18), channel_id=1, source_target_pairs={{0,3},{1,2},{2,1},{3,0},{4,7},{5,6},{6,5},{7,4},{8,11},{9,10},{10,... | collective-permute-start | bytes 1572872 | tf_op jit(solution)/shard_map/ppermute | solution.py:230
  71.1 14.0 %collective-permute-start.3 = (bf16[256,256]{1,0:T(8,128)(2,1)S(1)}, bf16[256,256]{1,0:T(8,128)(2,1)S(1)}, u32[]{:S(2)}, u32[]{:S(2)}) collective-permute-start(bf16[256,256]{1,0:T(8,128)(2,1)S(1)} %get-tuple-element.19), channel_id=1, source_target_pairs={{0,10},{1,11},{2,8},{3,9},{4,14},{5,15},{6,12},{7,13},{8,2},{9,3},... | collective-permute-start | bytes 393224 | tf_op jit(solution)/shard_map/ppermute | solution.py:36
  77.8 9.8 %collective-permute-start.4 = (bf16[256,256]{1,0:T(8,128)(2,1)S(1)}, bf16[256,256]{1,0:T(8,128)(2,1)S(1)}, u32[]{:S(2)}, u32[]{:S(2)}) collective-permute-start(bf16[256,256]{1,0:T(8,128)(2,1)S(1)} %get-tuple-element.20), channel_id=1, source_target_pairs={{0,12},{1,13},{2,6},{3,7},{4,0},{5,1},{6,10},{7,11},{8,4},{9,5},{1... | collective-permute-start | bytes 393224 | tf_op jit(solution)/shard_map/ppermute | solution.py:36
  80.6 8.7 %collective-permute-start.5 = (bf16[256,256]{1,0:T(8,128)(2,1)S(1)}, bf16[256,256]{1,0:T(8,128)(2,1)S(1)}, u32[]{:S(2)}, u32[]{:S(2)}) collective-permute-start(bf16[256,256]{1,0:T(8,128)(2,1)S(1)} %get-tuple-element.21), channel_id=1, source_target_pairs={{0,14},{1,15},{2,4},{3,5},{4,2},{5,3},{6,8},{7,9},{8,6},{9,7},{10,... | collective-permute-start | bytes 393224 | tf_op jit(solution)/shard_map/ppermute | solution.py:36

commit v3 on v2

--- a/solution.py
+++ b/solution.py
@@ -36,12 +36,23 @@
     return lax.ppermute(share, TP_AXES, pairs)
 
 
-def arrange_kernel(group, width, order_ref, weight_ref, *out_refs):
-    for r in range(group):
-        for i in range(group):
-            start = pl.multiple_of(order_ref[r * group + i] * width, width)
-            out_refs[r][i * width : (i + 1) * width, :] = weight_ref[:, pl.ds(start, width)].T
-    out_refs[group][0] = order_ref[0]
+def arrange_kernel(group, width, order_ref, weight_ref, *refs):
+    out_refs, done_ref, blocks, sems = refs[:group], refs[group], refs[group + 1], refs[group + 2]
+    loads = []
+    for n in range(group * group):
+        start = pl.multiple_of(order_ref[n] * width, width)
+        loads.append(
+            pltpu.make_async_copy(
+                weight_ref.at[:, pl.ds(start, width)], blocks.at[n], sems.at[n]
+            )
+        )
+    for load in loads:
+        load.start()
+    for n, load in enumerate(loads):
+        load.wait()
+        r, i = divmod(n, group)
+        out_refs[r][i * width : (i + 1) * width, :] = blocks[n].T
+    done_ref[0] = order_ref[0]
 
 
 def arrange(out_weight, order, group, width):
@@ -52,11 +63,15 @@
         out_shape=[piece] * group + [jax.ShapeDtypeStruct((1,), jnp.int32)],
         in_specs=[
             pl.BlockSpec(memory_space=pltpu.SMEM),
-            pl.BlockSpec(memory_space=pltpu.VMEM),
+            pl.BlockSpec(memory_space=pltpu.HBM),
         ],
         out_specs=[pl.BlockSpec(memory_space=pltpu.VMEM)] * group
         + [pl.BlockSpec(memory_space=pltpu.SMEM)],
-        compiler_params=pltpu.CompilerParams(vmem_limit_bytes=16 * MIB),
+        scratch_shapes=[
+            pltpu.VMEM((group * group, rows, width), out_weight.dtype),
+            pltpu.SemaphoreType.DMA((group * group,)),
+        ],
+        compiler_params=pltpu.CompilerParams(vmem_limit_bytes=60 * MIB),
         cost_estimate=pl.CostEstimate(
             flops=0, bytes_accessed=4 * rows * group * group * width, transcendentals=0
         ),
@@ -93,7 +108,7 @@
         in_specs=[pl.BlockSpec(memory_space=pltpu.SMEM)]
         + [pl.BlockSpec(memory_space=pltpu.VMEM)] * (1 + group),
         out_specs=[pl.BlockSpec(memory_space=pltpu.VMEM)] * group,
-        compiler_params=pltpu.CompilerParams(vmem_limit_bytes=16 * MIB),
+        compiler_params=pltpu.CompilerParams(vmem_limit_bytes=10 * MIB),
         cost_estimate=pl.CostEstimate(
             flops=2 * mixed.size * group * width,
             bytes_accessed=2 * (mixed.size + sum(w.size for w in weights) + group * share.size),
@@ -112,10 +127,7 @@
     first = 2 * np.pi * (np.outer(k1, i) % period) / period
     turn = 2 * np.pi * (np.outer(k1, s) % total) / total
     square = 2 * np.pi * (np.outer(s, s) % tokens) / tokens
-    both = 2 * channels
-    front = np.concatenate(
-        [np.kron(np.cos(first), np.eye(both)), np.kron(-np.sin(first), np.eye(both))]
-    )
+    front = np.concatenate([np.cos(first), -np.sin(first)])
     weight = np.where((k1 == 0) | (k1 == blocks), 1.0, 2.0)[:, None] / total
     back = np.concatenate(
         [
@@ -126,7 +138,7 @@
     )
     matrices = [jnp.asarray(m, jnp.bfloat16) for m in (front, np.cos(square), np.sin(square), back)]
     turns = [jnp.asarray(m, jnp.float32) for m in (np.cos(turn), np.sin(turn))]
-    return matrices, turns
+    return matrices + turns
 
 
 def matmul(left, right):
@@ -141,7 +153,15 @@
     both = 2 * channels
     turn_cos = cos_ref[...].reshape(low, 1, tokens)
     turn_sin = sin_ref[...].reshape(low, 1, tokens)
-    spread = matmul(front_ref[...], in_ref[...])
+    blocks = front_ref.shape[1]
+    width = blocks * both
+    repeat = lax.broadcasted_iota(jnp.int32, (blocks, width), 1) // both
+    repeat = (repeat == lax.broadcasted_iota(jnp.int32, (blocks, width), 0)).astype(jnp.bfloat16)
+    agree = lax.broadcasted_iota(jnp.int32, (both, width), 1) % both
+    agree = agree == lax.broadcasted_iota(jnp.int32, (both, width), 0)
+    entries = matmul(front_ref[...], repeat).reshape(2 * low, 1, width)
+    front = jnp.where(agree[None], entries, 0.0).reshape(2 * low * both, width)
+    spread = matmul(front.astype(jnp.bfloat16), in_ref[...])
     real = spread[: low * both].reshape(low, both, tokens)
     imag = spread[low * both :].reshape(low, both, tokens)
     turned_real = (real * turn_cos + imag * turn_sin).reshape(low * both, tokens).astype(jnp.bfloat16)
@@ -166,23 +186,33 @@
     ).astype(out_ref.dtype)
 
 
-def convolve(blocks_in, channels, after):
+def convolve(blocks_in, channels, tables, after):
     blocks, both, tokens = blocks_in.shape
-    matrices, turns = dft_tables(blocks, tokens, channels)
     out = pl.pallas_call(
         lambda *refs: convolve_kernel(channels, *refs),
         out_shape=jax.ShapeDtypeStruct((blocks * channels, tokens), jnp.bfloat16),
-        in_specs=[pl.BlockSpec(memory_space=pltpu.VMEM)] * 7 + [pl.BlockSpec(memory_space=pltpu.SMEM)],
+        in_specs=[pl.BlockSpec(memory_space=pltpu.VMEM)] * (1 + len(tables))
+        + [pl.BlockSpec(memory_space=pltpu.SMEM)],
         out_specs=pl.BlockSpec(memory_space=pltpu.VMEM),
         compiler_params=pltpu.CompilerParams(vmem_limit_bytes=32 * MIB),
         cost_estimate=pl.CostEstimate(
             flops=800_000_000, bytes_accessed=3_000_000, transcendentals=0
         ),
-    )(blocks_in.reshape(blocks * both, tokens), *matrices, *turns, after)
+    )(blocks_in.reshape(blocks * both, tokens), *tables, after)
     return out.reshape(blocks, channels, tokens)
 
 
-def outgoing_kernel(devices, signal_ref, gate_ref, taps_ref, out_ref):
+def outgoing_kernel(devices, signal_hbm, gate_hbm, taps_hbm, out_ref, signal_ref, gate_ref, taps_ref, sems):
+    copies = [
+        pltpu.make_async_copy(source, target, sems.at[n])
+        for n, (source, target) in enumerate(
+            [(signal_hbm, signal_ref), (gate_hbm, gate_ref), (taps_hbm, taps_ref)]
+        )
+    ]
+    for copy in copies:
+        copy.start()
+    for copy in copies:
+        copy.wait()
     rows, tokens = signal_ref.shape
     gated = signal_ref[...].astype(jnp.float32) * gate_ref[...].astype(jnp.float32)
     both = jnp.concatenate(
@@ -200,10 +230,38 @@
     out = pl.pallas_call(
         lambda *refs: outgoing_kernel(devices, *refs),
         out_shape=jax.ShapeDtypeStruct((2 * rows, tokens), jnp.bfloat16),
-        in_specs=[pl.BlockSpec(memory_space=pltpu.VMEM)] * 3,
+        in_specs=[pl.BlockSpec(memory_space=pltpu.HBM)] * 3,
         out_specs=pl.BlockSpec(memory_space=pltpu.VMEM),
+        scratch_shapes=[
+            pltpu.VMEM(signal.shape, signal.dtype),
+            pltpu.VMEM(pre_gate.shape, pre_gate.dtype),
+            pltpu.VMEM(filter_taps.shape, filter_taps.dtype),
+            pltpu.SemaphoreType.DMA((3,)),
+        ],
+        compiler_params=pltpu.CompilerParams(vmem_limit_bytes=60 * MIB),
     )(signal, pre_gate, filter_taps)
     return out.reshape(devices, 2 * rows // devices, tokens)
+
+
+def gate_kernel(post_ref, signal_ref, pre_ref, convolved_ref, gain_ref, after_ref, out_ref):
+    del after_ref
+    gated = signal_ref[...].astype(jnp.float32) * pre_ref[...].astype(jnp.float32)
+    inner = convolved_ref[...].astype(jnp.float32) + gain_ref[...] * gated
+    out_ref[...] = (post_ref[...].astype(jnp.float32) * inner).astype(out_ref.dtype)
+
+
+def gate(post_gate, signal, pre_gate, convolved, skip_gain, after):
+    corners = jnp.concatenate([array[:16, :128] for array in after])
+    return pl.pallas_call(
+        gate_kernel,
+        out_shape=jax.ShapeDtypeStruct(post_gate.shape, post_gate.dtype),
+        in_specs=[pl.BlockSpec(memory_space=pltpu.VMEM)] * 6,
+        out_specs=pl.BlockSpec(memory_space=pltpu.VMEM),
+        compiler_params=pltpu.CompilerParams(vmem_limit_bytes=6 * MIB),
+        cost_estimate=pl.CostEstimate(
+            flops=5 * post_gate.size, bytes_accessed=10 * post_gate.size, transcendentals=0
+        ),
+    )(post_gate, signal, pre_gate, convolved, skip_gain[:, None], corners)
 
 
 def per_device(signal, pre_gate, post_gate, filter_taps, skip_gain, out_weight):
@@ -225,20 +283,19 @@
         for r in range(group)
         for index in targets_of(quad, pair ^ (r >> 1), core ^ (r & 1), quads)
     ]
-    *weights, arranged = arrange(out_weight, jnp.stack(order).astype(jnp.int32), group, width)
+    tables = dft_tables(devices, tokens_here, channels)
+    *weights, arranged = arrange(
+        out_weight, jnp.stack(order).astype(jnp.int32), group, width
+    )
     weights = [weights[0]] + [
         lax.ppermute(weights[r], GROUP, [(t, t ^ r) for t in range(group)])
         for r in range(1, group)
     ]
 
     convolved = lax.all_to_all(
-        convolve(blocks, channels, arranged), "ctx", split_axis=0, concat_axis=0, tiled=True
+        convolve(blocks, channels, tables, arranged), "ctx", split_axis=0, concat_axis=0, tiled=True
     ).reshape(channels_here, tokens_here)
-    gated_input = signal.astype(jnp.float32) * pre_gate.astype(jnp.float32)
-    mixed = (
-        post_gate.astype(jnp.float32)
-        * (convolved.astype(jnp.float32) + skip_gain[:, None] * gated_input)
-    ).astype(jnp.bfloat16)
+    mixed = gate(post_gate, signal, pre_gate, convolved, skip_gain, weights[1:])
     gathered = lax.all_gather(mixed, GROUP, axis=0, tiled=True)
     shares = project(place.astype(jnp.int32).reshape(1), gathered, weights, width)
     shares = [send_to_target(shares[step], step, quads) for step in range(3)] + [shares[3]]

time: 90.6 us -> 81.5 us (0.90)
  blocking collectives: 24.3 us -> 9.2 us
  waiting for transfers between devices: 10.4 us -> 14.4 us
  Pallas kernels: 7.5 us -> 10.4 us
  starting transfers between devices: 43.1 us -> 44.9 us
  local copies, waits for them, and re-layouts: 2.61 us -> 0.89 us
  other arithmetic: 1.87 us -> 0.73 us
    all_gather x1, blocking collectives: 24.3 us -> 9.2 us  [per_device(): gathered = lax.all_gather(mixed, GROUP, axis=0, tiled=True)]
    ppermute x3, waiting for transfers between devices: 0.01 us -> 8.7 us  [per_device(): lax.ppermute(weights[r], GROUP, [(t, t ^ r) for t in range(group)])]
    all_to_all x1, waiting for transfers between devices: 6.05 us -> 0.01 us  [per_device(): lax.all_to_all(send, 'ctx', split_axis=0, concat_axis=0, tiled=True)]
    all_to_all x1, starting transfers between devices: 6.29 us -> 9.51 us  [per_device(): lax.all_to_all(convolve(blocks, channels, tables, arranged), 'ctx', split...]
    pallas_call x1, Pallas kernels: 1.82 us -> 4.39 us  [arrange(): pl.pallas_call(lambda *refs: arrange_kernel(group, width, *refs), out_sha...]
    unnamed x16 -> x22, local copies, waits for them, and re-layouts: 2.51 us -> 0.06 us
    ppermute x3, waiting for transfers between devices: 4.31 us -> 5.48 us  [send_to_target(): return lax.ppermute(share, TP_AXES, pairs)]
    convert_element_type x1 -> x0, other arithmetic: 1.15 us -> none  [per_device(): mixed = (post_gate.astype(jnp.float32) * (convolved.astype(jnp.float32) +...]
  transfers between devices with their start and end apart: 8 -> 8, of which waited for: 3 -> 4; matrix products, arithmetic and copies ran while one was open for 1% -> 1% of each run, Pallas kernels for 2% -> 10%
where the time goes in v3:
time: 81.5 us; the launch traced here: 81 us
  starting transfers between devices  44.9 us (55%)
  waiting for transfers between devices  14.4 us (18%)
  Pallas kernels  10.4 us (13%)
  blocking collectives  9.2 us (11%)
  local copies, waits for them, and re-layouts  0.89 us (1%)
    all_to_all x1, starting transfers between devices, per_device(): lax.all_to_all(send, 'ctx', split_axis=0, concat_axis=0, tiled=True)  13.7 us
    ppermute x3, starting transfers between devices, send_to_target(): return lax.ppermute(share, TP_AXES, pairs)  13.2 us
    all_to_all x1, starting transfers between devices, per_device(): lax.all_to_all(convolve(blocks, channels, tables, arranged), 'ctx', split...  9.51 us
    all_gather x1, blocking collectives, per_device(): gathered = lax.all_gather(mixed, GROUP, axis=0, tiled=True)  9.2 us
    ppermute x3, waiting for transfers between devices, per_device(): lax.ppermute(weights[r], GROUP, [(t, t ^ r) for t in range(group)])  8.7 us
    ppermute x3, starting transfers between devices, per_device(): lax.ppermute(weights[r], GROUP, [(t, t ^ r) for t in range(group)])  8.45 us
    ppermute x3, waiting for transfers between devices, send_to_target(): return lax.ppermute(share, TP_AXES, pairs)  5.48 us
    pallas_call x1, Pallas kernels, arrange(): pl.pallas_call(lambda *refs: arrange_kernel(group, width, *refs), out_sha...  4.39 us
  transfers between devices with their start and end apart: 8, of which 4 were waited for; matrix products, arithmetic and copies ran while one was open for 1% of the time, Pallas kernels for 10%

profile of v3, /device:TPU:1, one launch (start us, length us, event | category | flops | bytes accessed | tf_op | source)
XLA Modules:
  0.0 81.0 jit_solution(13732301293617659406)
XLA Ops:
  0.0 0.0 copy-start.7
  0.0 0.0 copy-start.8
  0.0 0.0 copy-start.4
  0.0 0.0 copy-start.5
  0.0 0.0 copy-start.6
  0.0 0.0 copy-start.9
  0.0 1.9 %shard_map.118 = bf16[512,256]{1,0:T(8,128)(2,1)} custom-call(bf16[256,256]{1,0:T(8,128)(2,1)} %signal_ref.1, bf16[256,256]{1,0:T(8,128)(2,1)} %pre_ref.1, f32[256,256]{1,0:T(8,128)} %refs_2_.2), custom_call_target="tpu_custom_call" | custom-call | tf_op jit(solution)/shard_map/pallas_call | solution.py:230
  2.0 13.7 %all-to-all-start = ((bf16[32,16,256]{2,1,0:T(8,128)(2,1)}), bf16[32,16,256]{2,1,0:T(8,128)(2,1)S(1)}, u32[]{:S(2)}, u32[]{:S(2)}) async-start(bf16[32,16,256]{2,1,0:T(8,128)(2,1)} %bitcast.24), calls=%async_computation | async-start | bytes 524288 | tf_op jit(solution)/shard_map/all_to_all | solution.py:277
  15.8 0.7 stack.67.refs_0_
  16.5 4.4 %shard_map.119 = (bf16[1024,256]{1,0:T(8,128)(2,1)}, bf16[1024,256]{1,0:T(8,128)(2,1)}, bf16[1024,256]{1,0:T(8,128)(2,1)}, bf16[1024,256]{1,0:T(8,128)(2,1)}, s32[1]{0:T(128)}) custom-call(s32[16]{0:T(128)} %stack.67.refs_0_, bf16[256,4096]{1,0:T(8,128)(2,1)} %refs_1_.4), custom_call_target="tpu_custom_call" | custom-call | bytes 4194304 | tf_op jit(solution)/shard_map/pallas_call | solution.py:61
  20.9 0.0 copy-start.10
  20.9 0.0 copy-start
  20.9 0.0 copy-start.1
  20.9 0.0 copy-start.3
  20.9 3.0 %collective-permute-start = (bf16[1024,256]{1,0:T(8,128)(2,1)}, bf16[1024,256]{1,0:T(8,128)(2,1)S(1)}, u32[]{:S(2)}, u32[]{:S(2)}) collective-permute-start(bf16[1024,256]{1,0:T(8,128)(2,1)} %get-tuple-element.15), channel_id=1, source_target_pairs={{0,1},{1,0},{2,3},{3,2},{4,5},{5,4},{6,7},{7,6},{8,9},{9,8},{10,11... | collective-permute-start | bytes 1572872 | tf_op jit(solution)/shard_map/ppermute | solution.py:291
  23.9 3.2 %collective-permute-start.1 = (bf16[1024,256]{1,0:T(8,128)(2,1)}, bf16[1024,256]{1,0:T(8,128)(2,1)S(1)}, u32[]{:S(2)}, u32[]{:S(2)}) collective-permute-start(bf16[1024,256]{1,0:T(8,128)(2,1)} %get-tuple-element.16), channel_id=1, source_target_pairs={{0,2},{1,3},{2,0},{3,1},{4,6},{5,7},{6,4},{7,5},{8,10},{9,11},{10,... | collective-permute-start | bytes 1572872 | tf_op jit(solution)/shard_map/ppermute | solution.py:291
  27.1 2.3 %collective-permute-start.2 = (bf16[1024,256]{1,0:T(8,128)(2,1)}, bf16[1024,256]{1,0:T(8,128)(2,1)S(1)}, u32[]{:S(2)}, u32[]{:S(2)}) collective-permute-start(bf16[1024,256]{1,0:T(8,128)(2,1)} %get-tuple-element.17), channel_id=1, source_target_pairs={{0,3},{1,2},{2,1},{3,0},{4,7},{5,6},{6,5},{7,4},{8,11},{9,10},{10,... | collective-permute-start | bytes 1572872 | tf_op jit(solution)/shard_map/ppermute | solution.py:291
  29.4 0.0 all-to-all-done
  29.4 0.0 copy-done.7
  29.4 0.0 copy-done.8
  29.4 0.0 copy-done.4
  29.5 0.0 copy-done.5
  29.5 0.0 copy-done.6
  29.5 0.0 copy-done.9
  29.5 0.0 copy-start.2
  29.5 3.3 %shard_map.120 = bf16[256,256]{1,0:T(8,128)(2,1)} custom-call(bf16[512,256]{1,0:T(8,128)(2,1)S(1)} %bitcast.23, bf16[66,32]{1,0:T(8,128)(2,1)S(1)} %copy-done.9, bf16[256,256]{1,0:T(8,128)(2,1)S(1)} %copy-done.6, bf16[256,256]{1,0:T(8,128)(2,1)S(1)} %copy-done.5, bf16[256,528]{1,0:T(8,128)(2,1)S(1)} %copy-done.4, f32[33,256]{1,0:T(8,128)S(1)} %copy-done.8, ...), custom_call_target="tpu_custom_call" | custom-call | flops 800000000 | bytes 3000000 | tf_op jit(solution)/shard_map/pallas_call | solution.py:191
  32.8 9.5 %all-to-all-start.1 = ((bf16[32,8,256]{2,1,0:T(8,128)(2,1)}), bf16[32,8,256]{2,1,0:T(8,128)(2,1)S(1)}, u32[]{:S(2)}, u32[]{:S(2)}) async-start(bf16[32,8,256]{2,1,0:T(8,128)(2,1)} %bitcast.19), calls=%async_computation.1 | async-start | bytes 262144 | tf_op jit(solution)/shard_map/all_to_all | solution.py:295
  42.3 0.0 copy-done.10
  42.3 0.1 copy.13.gain_ref
  42.5 0.0 collective-permute-done.refs_3_
  42.5 0.0 collective-permute-done.1.refs_4_
  42.5 8.7 %collective-permute-done.2.refs_5_ = bf16[1024,256]{1,0:T(8,128)(2,1)S(1)} collective-permute-done((bf16[1024,256]{1,0:T(8,128)(2,1)}, bf16[1024,256]{1,0:T(8,128)(2,1)S(1)}, u32[]{:S(2)}, u32[]{:S(2)}) %collective-permute-start.2) | collective-permute-done | bytes 524320 | tf_op jit(solution)/shard_map/ppermute | solution.py:291
  51.2 0.2 all-to-all-done.1
  51.5 0.0 copy-done
  51.5 0.0 copy-done.1
  51.5 0.0 copy-done.3
  51.5 0.1 shard_map.121
  51.6 9.2 %all_gather.3.refs_1_ = bf16[1024,256]{1,0:T(8,128)(2,1)S(1)} all-gather(bf16[256,256]{1,0:T(8,128)(2,1)S(1)} %shard_map.121), channel_id=1, replica_groups=mesh['ctx'=32,'quad'=4,'pair'=2,'core'=2] {'pair','core'}, dimensions={0}, use_global_device_ids=true | all-gather | bytes 655360 | tf_op jit(solution)/shard_map/all_gather | solution.py:299
  60.8 0.0 copy-done.2
  60.8 0.7 shard_map.122
  61.5 6.4 %collective-permute-start.3 = (bf16[256,256]{1,0:T(8,128)(2,1)S(1)}, bf16[256,256]{1,0:T(8,128)(2,1)S(1)}, u32[]{:S(2)}, u32[]{:S(2)}) collective-permute-start(bf16[256,256]{1,0:T(8,128)(2,1)S(1)} %get-tuple-element.19), channel_id=1, source_target_pairs={{0,10},{1,11},{2,8},{3,9},{4,14},{5,15},{6,12},{7,13},{8,2},{9,3},... | collective-permute-start | bytes 393224 | tf_op jit(solution)/shard_map/ppermute | solution.py:36
  68.0 2.3 %collective-permute-start.4 = (bf16[256,256]{1,0:T(8,128)(2,1)S(1)}, bf16[256,256]{1,0:T(8,128)(2,1)S(1)}, u32[]{:S(2)}, u32[]{:S(2)}) collective-permute-start(bf16[256,256]{1,0:T(8,128)(2,1)S(1)} %get-tuple-element.20), channel_id=1, source_target_pairs={{0,12},{1,13},{2,6},{3,7},{4,0},{5,1},{6,10},{7,11},{8,4},{9,5},{1... | collective-permute-start | bytes 393224 | tf_op jit(solution)/shard_map/ppermute | solution.py:36
  70.3 4.4 %collective-permute-start.5 = (bf16[256,256]{1,0:T(8,128)(2,1)S(1)}, bf16[256,256]{1,0:T(8,128)(2,1)S(1)}, u32[]{:S(2)}, u32[]{:S(2)}) collective-permute-start(bf16[256,256]{1,0:T(8,128)(2,1)S(1)} %get-tuple-element.21), channel_id=1, source_target_pairs={{0,14},{1,15},{2,4},{3,5},{4,2},{5,3},{6,8},{7,9},{8,6},{9,7},{10,... | collective-permute-start | bytes 393224 | tf_op jit(solution)/shard_map/ppermute | solution.py:36
  74.8 0.0 collective-permute-done.3
  74.8 3.1 %collective-permute-done.4 = bf16[256,256]{1,0:T(8,128)(2,1)S(1)} collective-permute-done((bf16[256,256]{1,0:T(8,128)(2,1)S(1)}, bf16[256,256]{1,0:T(8,128)(2,1)S(1)}, u32[]{:S(2)}, u32[]{:S(2)}) %collective-permute-start.4) | collective-permute-done | bytes 131104 | tf_op jit(solution)/shard_map/ppermute | solution.py:36
  77.8 2.4 %collective-permute-done.5 = bf16[256,256]{1,0:T(8,128)(2,1)S(1)} collective-permute-done((bf16[256,256]{1,0:T(8,128)(2,1)S(1)}, bf16[256,256]{1,0:T(8,128)(2,1)S(1)}, u32[]{:S(2)}, u32[]{:S(2)}) %collective-permute-start.5) | collective-permute-done | bytes 131104 | tf_op jit(solution)/shard_map/ppermute | solution.py:36
  80.2 0.7 add_convert_fusion
  (4 shorter events, 0.0 us)
Async XLA Ops:
  0.0 29.4 %copy-start.7 = (f32[33,256]{1,0:T(8,128)S(1)}, f32[33,256]{1,0:T(8,128)}, u32[]{:S(2)}) copy-start(f32[33,256]{1,0:T(8,128)} %constant.75.clone.refs_6_) | copy-start | bytes 101380
  0.0 29.4 %copy-start.8 = (f32[33,256]{1,0:T(8,128)S(1)}, f32[33,256]{1,0:T(8,128)}, u32[]{:S(2)}) copy-start(f32[33,256]{1,0:T(8,128)} %constant.74.clone.refs_5_) | copy-start | bytes 101380
  0.0 29.4 %copy-start.4 = (bf16[256,528]{1,0:T(8,128)(2,1)S(1)}, bf16[256,528]{1,0:T(8,128)(2,1)}, u32[]{:S(2)}) copy-start(bf16[256,528]{1,0:T(8,128)(2,1)} %constant.73.clone.refs_4_) | copy-start | bytes 811012
  0.0 29.4 %copy-start.5 = (bf16[256,256]{1,0:T(8,128)(2,1)S(1)}, bf16[256,256]{1,0:T(8,128)(2,1)}, u32[]{:S(2)}) copy-start(bf16[256,256]{1,0:T(8,128)(2,1)} %constant.72.clone.refs_3_) | copy-start | bytes 393220
  0.0 29.4 %copy-start.6 = (bf16[256,256]{1,0:T(8,128)(2,1)S(1)}, bf16[256,256]{1,0:T(8,128)(2,1)}, u32[]{:S(2)}) copy-start(bf16[256,256]{1,0:T(8,128)(2,1)} %constant.71.clone.refs_2_) | copy-start | bytes 393220
  0.0 29.4 %copy-start.9 = (bf16[66,32]{1,0:T(8,128)(2,1)S(1)}, bf16[66,32]{1,0:T(8,128)(2,1)}, u32[]{:S(2)}) copy-start(bf16[66,32]{1,0:T(8,128)(2,1)} %constant.70.clone.refs_1_) | copy-start | bytes 12676
  2.0 27.4 %all-to-all-start = ((bf16[32,16,256]{2,1,0:T(8,128)(2,1)}), bf16[32,16,256]{2,1,0:T(8,128)(2,1)S(1)}, u32[]{:S(2)}, u32[]{:S(2)}) async-start(bf16[32,16,256]{2,1,0:T(8,128)(2,1)} %bitcast.24), calls=%async_computation | async-start | bytes 524288 | tf_op jit(solution)/shard_map/all_to_all | solution.py:277
  20.9 21.4 %copy-start.10 = (f32[256]{0:T(256)S(1)}, f32[256]{0:T(256)}, u32[]{:S(2)}) copy-start(f32[256]{0:T(256)} %param.16) | copy-start | bytes 3076
  20.9 30.6 %copy-start = (bf16[256,256]{1,0:T(8,128)(2,1)S(1)}, bf16[256,256]{1,0:T(8,128)(2,1)}, u32[]{:S(2)}) copy-start(bf16[256,256]{1,0:T(8,128)(2,1)} %signal_ref.1) | copy-start | bytes 393220
  20.9 30.6 %copy-start.1 = (bf16[256,256]{1,0:T(8,128)(2,1)S(1)}, bf16[256,256]{1,0:T(8,128)(2,1)}, u32[]{:S(2)}) copy-start(bf16[256,256]{1,0:T(8,128)(2,1)} %pre_ref.1) | copy-start | bytes 393220
  20.9 30.6 %copy-start.3 = (bf16[256,256]{1,0:T(8,128)(2,1)S(1)}, bf16[256,256]{1,0:T(8,128)(2,1)}, u32[]{:S(2)}) copy-start(bf16[256,256]{1,0:T(8,128)(2,1)} %post_ref.1) | copy-start | bytes 393220
  20.9 21.5 %collective-permute-start = (bf16[1024,256]{1,0:T(8,128)(2,1)}, bf16[1024,256]{1,0:T(8,128)(2,1)S(1)}, u32[]{:S(2)}, u32[]{:S(2)}) collective-permute-start(bf16[1024,256]{1,0:T(8,128)(2,1)} %get-tuple-element.15), channel_id=1, source_target_pairs={{0,1},{1,0},{2,3},{3,2},{4,5},{5,4},{6,7},{7,6},{8,9},{9,8},{10,11... | collective-permute-start | bytes 1572872 | tf_op jit(solution)/shard_map/ppermute | solution.py:291
  23.9 18.6 %collective-permute-start.1 = (bf16[1024,256]{1,0:T(8,128)(2,1)}, bf16[1024,256]{1,0:T(8,128)(2,1)S(1)}, u32[]{:S(2)}, u32[]{:S(2)}) collective-permute-start(bf16[1024,256]{1,0:T(8,128)(2,1)} %get-tuple-element.16), channel_id=1, source_target_pairs={{0,2},{1,3},{2,0},{3,1},{4,6},{5,7},{6,4},{7,5},{8,10},{9,11},{10,... | collective-permute-start | bytes 1572872 | tf_op jit(solution)/shard_map/ppermute | solution.py:291
  27.1 24.1 %collective-permute-start.2 = (bf16[1024,256]{1,0:T(8,128)(2,1)}, bf16[1024,256]{1,0:T(8,128)(2,1)S(1)}, u32[]{:S(2)}, u32[]{:S(2)}) collective-permute-start(bf16[1024,256]{1,0:T(8,128)(2,1)} %get-tuple-element.17), channel_id=1, source_target_pairs={{0,3},{1,2},{2,1},{3,0},{4,7},{5,6},{6,5},{7,4},{8,11},{9,10},{10,... | collective-permute-start | bytes 1572872 | tf_op jit(solution)/shard_map/ppermute | solution.py:291
  29.5 31.3 %copy-start.2 = (bf16[1024,256]{1,0:T(8,128)(2,1)S(1)}, bf16[1024,256]{1,0:T(8,128)(2,1)}, u32[]{:S(2)}) copy-start(bf16[1024,256]{1,0:T(8,128)(2,1)} %get-tuple-element.18.refs_2_) | copy-start | bytes 1572868
  32.8 18.7 %all-to-all-start.1 = ((bf16[32,8,256]{2,1,0:T(8,128)(2,1)}), bf16[32,8,256]{2,1,0:T(8,128)(2,1)S(1)}, u32[]{:S(2)}, u32[]{:S(2)}) async-start(bf16[32,8,256]{2,1,0:T(8,128)(2,1)} %bitcast.19), calls=%async_computation.1 | async-start | bytes 262144 | tf_op jit(solution)/shard_map/all_to_all | solution.py:295
  61.5 13.2 %collective-permute-start.3 = (bf16[256,256]{1,0:T(8,128)(2,1)S(1)}, bf16[256,256]{1,0:T(8,128)(2,1)S(1)}, u32[]{:S(2)}, u32[]{:S(2)}) collective-permute-start(bf16[256,256]{1,0:T(8,128)(2,1)S(1)} %get-tuple-element.19), channel_id=1, source_target_pairs={{0,10},{1,11},{2,8},{3,9},{4,14},{5,15},{6,12},{7,13},{8,2},{9,3},... | collective-permute-start | bytes 393224 | tf_op jit(solution)/shard_map/ppermute | solution.py:36
  68.0 9.9 %collective-permute-start.4 = (bf16[256,256]{1,0:T(8,128)(2,1)S(1)}, bf16[256,256]{1,0:T(8,128)(2,1)S(1)}, u32[]{:S(2)}, u32[]{:S(2)}) collective-permute-start(bf16[256,256]{1,0:T(8,128)(2,1)S(1)} %get-tuple-element.20), channel_id=1, source_target_pairs={{0,12},{1,13},{2,6},{3,7},{4,0},{5,1},{6,10},{7,11},{8,4},{9,5},{1... | collective-permute-start | bytes 393224 | tf_op jit(solution)/shard_map/ppermute | solution.py:36
  70.3 9.9 %collective-permute-start.5 = (bf16[256,256]{1,0:T(8,128)(2,1)S(1)}, bf16[256,256]{1,0:T(8,128)(2,1)S(1)}, u32[]{:S(2)}, u32[]{:S(2)}) collective-permute-start(bf16[256,256]{1,0:T(8,128)(2,1)S(1)} %get-tuple-element.21), channel_id=1, source_target_pairs={{0,14},{1,15},{2,4},{3,5},{4,2},{5,3},{6,8},{7,9},{8,6},{9,7},{10,... | collective-permute-start | bytes 393224 | tf_op jit(solution)/shard_map/ppermute | solution.py:36

commit v4 on v3

--- a/solution.py
+++ b/solution.py
@@ -15,13 +15,10 @@
 
 
 def targets_of(quad, pair, core, quads):
-    onward = jnp.where(pair == 1, 1, -1)
-    chips = [
-        ((quad + 2 * onward) % quads, 1 - pair),
-        ((quad + onward) % quads, pair),
-        ((quad + onward) % quads, 1 - pair),
-        (quad, pair),
-    ]
+    onward = 2 * pair - 1
+    far = lax.rem(quad + 2 * onward + quads, quads)
+    near = lax.rem(quad + onward + quads, quads)
+    chips = [(far, 1 - pair), (near, pair), (near, 1 - pair), (quad, pair)]
     return [(q * 2 + p) * 2 + core for q, p in chips]
 
 
@@ -36,62 +33,67 @@
     return lax.ppermute(share, TP_AXES, pairs)
 
 
-def arrange_kernel(group, width, order_ref, weight_ref, *refs):
-    out_refs, done_ref, blocks, sems = refs[:group], refs[group], refs[group + 1], refs[group + 2]
-    loads = []
-    for n in range(group * group):
-        start = pl.multiple_of(order_ref[n] * width, width)
-        loads.append(
-            pltpu.make_async_copy(
-                weight_ref.at[:, pl.ds(start, width)], blocks.at[n], sems.at[n]
+def arrange_kernel(group, quads, width, members, place_ref, weight_ref, *refs):
+    out_refs, done_ref, sems = refs[: len(members)], refs[-2], refs[-1]
+    tp = place_ref[0]
+    quad, place = tp // group, lax.rem(tp, group)
+    copies = []
+    for n, r in enumerate(members):
+        other = place ^ r
+        for i, target in enumerate(targets_of(quad, other // 2, lax.rem(other, 2), quads)):
+            start = pl.multiple_of(target * width, width)
+            copies.append(
+                pltpu.make_async_copy(
+                    weight_ref.at[:, pl.ds(start, width)],
+                    out_refs[n].at[:, pl.ds(i * width, width)],
+                    sems.at[n * group + i],
+                )
             )
-        )
-    for load in loads:
-        load.start()
-    for n, load in enumerate(loads):
-        load.wait()
-        r, i = divmod(n, group)
-        out_refs[r][i * width : (i + 1) * width, :] = blocks[n].T
-    done_ref[0] = order_ref[0]
-
-
-def arrange(out_weight, order, group, width):
+    for copy in copies:
+        copy.start()
+    for copy in copies:
+        copy.wait()
+    done_ref[0] = tp
+
+
+def arrange(out_weight, place, group, quads, width, members):
     rows = out_weight.shape[0]
-    piece = jax.ShapeDtypeStruct((group * width, rows), out_weight.dtype)
-    return pl.pallas_call(
-        lambda *refs: arrange_kernel(group, width, *refs),
-        out_shape=[piece] * group + [jax.ShapeDtypeStruct((1,), jnp.int32)],
+    piece = jax.ShapeDtypeStruct((rows, group * width), out_weight.dtype)
+    *pieces, done = pl.pallas_call(
+        lambda *refs: arrange_kernel(group, quads, width, members, *refs),
+        out_shape=[piece] * len(members) + [jax.ShapeDtypeStruct((1,), jnp.int32)],
         in_specs=[
             pl.BlockSpec(memory_space=pltpu.SMEM),
             pl.BlockSpec(memory_space=pltpu.HBM),
         ],
-        out_specs=[pl.BlockSpec(memory_space=pltpu.VMEM)] * group
+        out_specs=[pl.BlockSpec(memory_space=pltpu.HBM)] * len(members)
         + [pl.BlockSpec(memory_space=pltpu.SMEM)],
-        scratch_shapes=[
-            pltpu.VMEM((group * group, rows, width), out_weight.dtype),
-            pltpu.SemaphoreType.DMA((group * group,)),
-        ],
+        scratch_shapes=[pltpu.SemaphoreType.DMA((len(members) * group,))],
         compiler_params=pltpu.CompilerParams(vmem_limit_bytes=60 * MIB),
         cost_estimate=pl.CostEstimate(
-            flops=0, bytes_accessed=4 * rows * group * group * width, transcendentals=0
-        ),
-    )(order, out_weight)
+            flops=0,
+            bytes_accessed=4 * rows * len(members) * group * width,
+            transcendentals=0,
+        ),
+    )(place, out_weight)
+    return pieces, done
 
 
 def project_kernel(group, place_ref, mixed_ref, *refs):
     weight_refs, out_refs = refs[:group], refs[group:]
-    rows = mixed_ref.shape[0] // group
-    width = out_refs[0].shape[0]
+    tokens = mixed_ref.shape[0] // group
+    width = out_refs[0].shape[1]
+    place = lax.rem(place_ref[0], group)
     mixed = [
-        mixed_ref[pl.ds(pl.multiple_of((place_ref[0] ^ r) * rows, rows), rows), :]
+        mixed_ref[pl.ds(pl.multiple_of((place ^ r) * tokens, tokens), tokens), :]
         for r in range(group)
     ]
     for i in range(group):
         total = None
         for r in range(group):
             term = jnp.dot(
-                weight_refs[r][i * width : (i + 1) * width, :],
                 mixed[r],
+                weight_refs[r][:, i * width : (i + 1) * width],
                 preferred_element_type=jnp.float32,
             )
             total = term if total is None else total + term
@@ -100,8 +102,7 @@
 
 def project(place, mixed, weights, width):
     group = len(weights)
-    tokens = mixed.shape[1]
-    share = jax.ShapeDtypeStruct((width, tokens), mixed.dtype)
+    share = jax.ShapeDtypeStruct((mixed.shape[0] // group, width), mixed.dtype)
     return pl.pallas_call(
         lambda *refs: project_kernel(group, *refs),
         out_shape=[share] * group,
@@ -115,6 +116,24 @@
             transcendentals=0,
         ),
     )(place, mixed, *weights)
+
+
+def finish_kernel(*refs):
+    total = refs[0][...].astype(jnp.float32)
+    for ref in refs[1:-1]:
+        total = total + ref[...].astype(jnp.float32)
+    refs[-1][...] = total.astype(refs[-1].dtype).T
+
+
+def finish(shares):
+    tokens, width = shares[0].shape
+    return pl.pallas_call(
+        finish_kernel,
+        out_shape=jax.ShapeDtypeStruct((width, tokens), shares[0].dtype),
+        in_specs=[pl.BlockSpec(memory_space=pltpu.VMEM)] * len(shares),
+        out_specs=pl.BlockSpec(memory_space=pltpu.VMEM),
+        compiler_params=pltpu.CompilerParams(vmem_limit_bytes=6 * MIB),
+    )(*shares)
 
 
 def dft_tables(blocks, tokens, channels):
@@ -247,14 +266,14 @@
     del after_ref
     gated = signal_ref[...].astype(jnp.float32) * pre_ref[...].astype(jnp.float32)
     inner = convolved_ref[...].astype(jnp.float32) + gain_ref[...] * gated
-    out_ref[...] = (post_ref[...].astype(jnp.float32) * inner).astype(out_ref.dtype)
+    out_ref[...] = (post_ref[...].astype(jnp.float32) * inner).astype(out_ref.dtype).T
 
 
 def gate(post_gate, signal, pre_gate, convolved, skip_gain, after):
     corners = jnp.concatenate([array[:16, :128] for array in after])
     return pl.pallas_call(
         gate_kernel,
-        out_shape=jax.ShapeDtypeStruct(post_gate.shape, post_gate.dtype),
+        out_shape=jax.ShapeDtypeStruct(post_gate.shape[::-1], post_gate.dtype),
         in_specs=[pl.BlockSpec(memory_space=pltpu.VMEM)] * 6,
         out_specs=pl.BlockSpec(memory_space=pltpu.VMEM),
         compiler_params=pltpu.CompilerParams(vmem_limit_bytes=6 * MIB),
@@ -276,30 +295,23 @@
     send = outgoing(signal, pre_gate, filter_taps, devices)
     blocks = lax.all_to_all(send, "ctx", split_axis=0, concat_axis=0, tiled=True)
 
-    quad, pair, core = (lax.axis_index(axis) for axis in TP_AXES)
-    place = pair * 2 + core
-    order = [
-        index
-        for r in range(group)
-        for index in targets_of(quad, pair ^ (r >> 1), core ^ (r & 1), quads)
+    place = lax.axis_index(TP_AXES).astype(jnp.int32).reshape(1)
+    crossing = [r for r in range(group) if r >= 2]
+    pieces, arranged = arrange(out_weight, place, group, quads, width, crossing)
+    tables = dft_tables(devices, tokens_here, channels)
+    convolved = convolve(blocks, channels, tables, arranged)
+    inner, _ = arrange(out_weight, place, group, quads, width, [0, 1])
+    weights = [inner[0]] + [
+        lax.ppermute(piece, GROUP, [(t, t ^ r) for t in range(group)])
+        for r, piece in zip(range(1, group), [inner[1]] + pieces)
     ]
-    tables = dft_tables(devices, tokens_here, channels)
-    *weights, arranged = arrange(
-        out_weight, jnp.stack(order).astype(jnp.int32), group, width
-    )
-    weights = [weights[0]] + [
-        lax.ppermute(weights[r], GROUP, [(t, t ^ r) for t in range(group)])
-        for r in range(1, group)
-    ]
-
-    convolved = lax.all_to_all(
-        convolve(blocks, channels, tables, arranged), "ctx", split_axis=0, concat_axis=0, tiled=True
-    ).reshape(channels_here, tokens_here)
-    mixed = gate(post_gate, signal, pre_gate, convolved, skip_gain, weights[1:])
+    convolved = lax.all_to_all(convolved, "ctx", split_axis=0, concat_axis=0, tiled=True).reshape(
+        channels_here, tokens_here
+    )
+    mixed = gate(post_gate, signal, pre_gate, convolved, skip_gain, weights[2:])
     gathered = lax.all_gather(mixed, GROUP, axis=0, tiled=True)
-    shares = project(place.astype(jnp.int32).reshape(1), gathered, weights, width)
-    shares = [send_to_target(shares[step], step, quads) for step in range(3)] + [shares[3]]
-    return sum(share.astype(jnp.float32) for share in shares).astype(jnp.bfloat16)
+    shares = project(place, gathered, weights, width)
+    return finish([send_to_target(shares[step], step, quads) for step in range(3)] + [shares[3]])
 
 
 def solution(mesh):

time: 81.5 us -> 143 us (1.75)
  Pallas kernels: 10.4 us -> 73.7 us
    pallas_call x1 -> x3, Pallas kernels: 4.39 us -> 67.7 us  [the longest x2 67 us: arrange(): pl.pallas_call(lambda *refs: arrange_kernel(group, quads, width, members,...]
    all_to_all x1, waiting for transfers between devices: 0.24 us -> 8.96 us  [per_device(): lax.all_to_all(convolved, 'ctx', split_axis=0, concat_axis=0, tiled=True)]
    ppermute x3, waiting for transfers between devices: 8.7 us -> 0.01 us  [per_device(): lax.ppermute(piece, GROUP, [(t, t ^ r) for t in range(group)])]
  transfers between devices with their start and end apart: 8 -> 8, of which waited for: 4 -> 3; matrix products, arithmetic and copies ran while one was open for 1% -> 0% of each run, Pallas kernels for 10% -> 49%
where the time goes in v4:
time: 143 us
  Pallas kernels  73.7 us (52%)
  starting transfers between devices  44.9 us (31%)
  waiting for transfers between devices  14.5 us (10%)
  blocking collectives  9.09 us (6%)
    pallas_call x2, Pallas kernels, arrange(): pl.pallas_call(lambda *refs: arrange_kernel(group, quads, width, members,...  67 us
    all_to_all x1, starting transfers between devices, per_device(): lax.all_to_all(send, 'ctx', split_axis=0, concat_axis=0, tiled=True)  13.7 us
    ppermute x3, starting transfers between devices, send_to_target(): return lax.ppermute(share, TP_AXES, pairs)  13.2 us
    all_to_all x1, starting transfers between devices, per_device(): lax.all_to_all(convolved, 'ctx', split_axis=0, concat_axis=0, tiled=True)  9.5 us
    all_gather x1, blocking collectives, per_device(): gathered = lax.all_gather(mixed, GROUP, axis=0, tiled=True)  9.09 us
    all_to_all x1, waiting for transfers between devices, per_device(): lax.all_to_all(convolved, 'ctx', split_axis=0, concat_axis=0, tiled=True)  8.96 us
    ppermute x3, starting transfers between devices, per_device(): lax.ppermute(piece, GROUP, [(t, t ^ r) for t in range(group)])  8.45 us
    ppermute x3, waiting for transfers between devices, send_to_target(): return lax.ppermute(share, TP_AXES, pairs)  5.49 us
  transfers between devices with their start and end apart: 8, of which 3 were waited for; matrix products, arithmetic and copies ran while one was open for 0% of the time, Pallas kernels for 49%

profile of v4, /device:TPU:1, one launch (start us, length us, event | category | flops | bytes accessed | tf_op | source)
XLA Modules:
  0.0 142.6 jit_solution(582401441186918370)
XLA Ops:
  0.0 1.9 %shard_map.118 = bf16[512,256]{1,0:T(8,128)(2,1)} custom-call(bf16[256,256]{1,0:T(8,128)(2,1)} %signal_ref.1, bf16[256,256]{1,0:T(8,128)(2,1)} %pre_ref.1, f32[256,256]{1,0:T(8,128)} %refs_2_.2), custom_call_target="tpu_custom_call" | custom-call | tf_op jit(solution)/shard_map/pallas_call | solution.py:249
  1.9 13.7 %all-to-all-start = ((bf16[32,16,256]{2,1,0:T(8,128)(2,1)}), bf16[32,16,256]{2,1,0:T(8,128)(2,1)S(1)}, u32[]{:S(2)}, u32[]{:S(2)}) async-start(bf16[32,16,256]{2,1,0:T(8,128)(2,1)} %bitcast.8), calls=%async_computation | async-start | bytes 524288 | tf_op jit(solution)/shard_map/all_to_all | solution.py:296
  15.6 0.0 copy-start.4
  15.6 0.0 copy-start.5
  15.6 0.0 copy-start.6
  15.6 0.0 copy-start.7
  15.7 0.0 copy-start.8
  15.7 0.0 copy-start.9
  15.7 33.5 %shard_map.119 = (bf16[256,1024]{1,0:T(8,128)(2,1)}, bf16[256,1024]{1,0:T(8,128)(2,1)}, s32[1]{0:T(128)}) custom-call(s32[1]{0:T(128)} %bitcast.refs_0_, bf16[256,4096]{1,0:T(8,128)(2,1)} %refs_1_.6), custom_call_target="tpu_custom_call" | custom-call | bytes 2097152 | tf_op jit(solution)/shard_map/pallas_call | solution.py:62
  49.2 3.2 %collective-permute-start = (bf16[256,1024]{1,0:T(8,128)(2,1)}, bf16[256,1024]{1,0:T(8,128)(2,1)S(1)}, u32[]{:S(2)}, u32[]{:S(2)}) collective-permute-start(bf16[256,1024]{1,0:T(8,128)(2,1)} %get-tuple-element.15), channel_id=1, source_target_pairs={{0,2},{1,3},{2,0},{3,1},{4,6},{5,7},{6,4},{7,5},{8,10},{9,11},{10,... | collective-permute-start | bytes 1572872 | tf_op jit(solution)/shard_map/ppermute | solution.py:305
  52.4 3.2 %collective-permute-start.1 = (bf16[256,1024]{1,0:T(8,128)(2,1)}, bf16[256,1024]{1,0:T(8,128)(2,1)S(1)}, u32[]{:S(2)}, u32[]{:S(2)}) collective-permute-start(bf16[256,1024]{1,0:T(8,128)(2,1)} %get-tuple-element.16), channel_id=1, source_target_pairs={{0,3},{1,2},{2,1},{3,0},{4,7},{5,6},{6,5},{7,4},{8,11},{9,10},{10,... | collective-permute-start | bytes 1572872 | tf_op jit(solution)/shard_map/ppermute | solution.py:305
  55.6 33.5 %shard_map.122 = (bf16[256,1024]{1,0:T(8,128)(2,1)}, bf16[256,1024]{1,0:T(8,128)(2,1)}, s32[1]{0:T(128)}) custom-call(s32[1]{0:T(128)} %bitcast.refs_0_, bf16[256,4096]{1,0:T(8,128)(2,1)} %refs_1_.6), custom_call_target="tpu_custom_call" | custom-call | bytes 2097152 | tf_op jit(solution)/shard_map/pallas_call | solution.py:62
  89.1 0.0 copy-start.10
  89.1 0.0 copy-start
  89.1 0.0 copy-start.1
  89.1 0.0 copy-start.3
  89.1 2.1 %collective-permute-start.2 = (bf16[256,1024]{1,0:T(8,128)(2,1)}, bf16[256,1024]{1,0:T(8,128)(2,1)S(1)}, u32[]{:S(2)}, u32[]{:S(2)}) collective-permute-start(bf16[256,1024]{1,0:T(8,128)(2,1)} %get-tuple-element.18), channel_id=1, source_target_pairs={{0,1},{1,0},{2,3},{3,2},{4,5},{5,4},{6,7},{7,6},{8,9},{9,8},{10,11... | collective-permute-start | bytes 1572872 | tf_op jit(solution)/shard_map/ppermute | solution.py:305
  91.2 0.0 all-to-all-done
  91.2 0.0 copy-done.4
  91.2 0.0 copy-done.5
  91.2 0.0 copy-done.6
  91.2 0.0 copy-done.7
  91.2 0.0 copy-done.8
  91.2 0.0 copy-done.9
  91.2 0.0 copy-start.2
  91.3 3.2 %shard_map.120 = bf16[256,256]{1,0:T(8,128)(2,1)} custom-call(bf16[512,256]{1,0:T(8,128)(2,1)S(1)} %bitcast.7, bf16[66,32]{1,0:T(8,128)(2,1)S(1)} %copy-done.9, bf16[256,256]{1,0:T(8,128)(2,1)S(1)} %copy-done.6, bf16[256,256]{1,0:T(8,128)(2,1)S(1)} %copy-done.5, bf16[256,528]{1,0:T(8,128)(2,1)S(1)} %copy-done.4, f32[33,256]{1,0:T(8,128)S(1)} %copy-done.8, ...), custom_call_target="tpu_custom_call" | custom-call | flops 800000000 | bytes 3000000 | tf_op jit(solution)/shard_map/pallas_call | solution.py:210
  94.5 9.5 %all-to-all-start.1 = ((bf16[32,8,256]{2,1,0:T(8,128)(2,1)}), bf16[32,8,256]{2,1,0:T(8,128)(2,1)S(1)}, u32[]{:S(2)}, u32[]{:S(2)}) async-start(bf16[32,8,256]{2,1,0:T(8,128)(2,1)} %bitcast.3), calls=%async_computation.1 | async-start | bytes 262144 | tf_op jit(solution)/shard_map/all_to_all | solution.py:308
  104.0 0.0 copy-done.10
  104.0 0.1 copy.13.gain_ref
  104.1 0.0 collective-permute-done.refs_4_
  104.1 0.0 collective-permute-done.1.refs_5_
  104.2 9.0 %all-to-all-done.1 = bf16[32,8,256]{2,1,0:T(8,128)(2,1)S(1)} async-done(((bf16[32,8,256]{2,1,0:T(8,128)(2,1)}), bf16[32,8,256]{2,1,0:T(8,128)(2,1)S(1)}, u32[]{:S(2)}, u32[]{:S(2)}) %all-to-all-start.1) | async-done | bytes 131104 | tf_op jit(solution)/shard_map/all_to_all | solution.py:308
  113.1 0.0 copy-done
  113.1 0.0 copy-done.1
  113.1 0.0 copy-done.3
  113.2 0.2 shard_map.121
  113.3 9.1 %all_gather.3.refs_1_ = bf16[1024,256]{1,0:T(8,128)(2,1)S(1)} all-gather(bf16[256,256]{1,0:T(8,128)(2,1)S(1)} %shard_map.121), channel_id=1, replica_groups=mesh['ctx'=32,'quad'=4,'pair'=2,'core'=2] {'pair','core'}, dimensions={0}, use_global_device_ids=true | all-gather | bytes 655360 | tf_op jit(solution)/shard_map/all_gather | solution.py:312
  122.4 0.0 collective-permute-done.2.refs_3_
  122.4 0.0 copy-done.2
  122.4 0.7 shard_map.123
  123.1 6.4 %collective-permute-start.3 = (bf16[256,256]{1,0:T(8,128)(2,1)S(1)}, bf16[256,256]{1,0:T(8,128)(2,1)S(1)}, u32[]{:S(2)}, u32[]{:S(2)}) collective-permute-start(bf16[256,256]{1,0:T(8,128)(2,1)S(1)} %get-tuple-element.19), channel_id=1, source_target_pairs={{0,10},{1,11},{2,8},{3,9},{4,14},{5,15},{6,12},{7,13},{8,2},{9,3},... | collective-permute-start | bytes 393224 | tf_op jit(solution)/shard_map/ppermute | solution.py:33
  129.6 2.3 %collective-permute-start.4 = (bf16[256,256]{1,0:T(8,128)(2,1)S(1)}, bf16[256,256]{1,0:T(8,128)(2,1)S(1)}, u32[]{:S(2)}, u32[]{:S(2)}) collective-permute-start(bf16[256,256]{1,0:T(8,128)(2,1)S(1)} %get-tuple-element.20), channel_id=1, source_target_pairs={{0,12},{1,13},{2,6},{3,7},{4,0},{5,1},{6,10},{7,11},{8,4},{9,5},{1... | collective-permute-start | bytes 393224 | tf_op jit(solution)/shard_map/ppermute | solution.py:33
  131.9 4.4 %collective-permute-start.5 = (bf16[256,256]{1,0:T(8,128)(2,1)S(1)}, bf16[256,256]{1,0:T(8,128)(2,1)S(1)}, u32[]{:S(2)}, u32[]{:S(2)}) collective-permute-start(bf16[256,256]{1,0:T(8,128)(2,1)S(1)} %get-tuple-element.21), channel_id=1, source_target_pairs={{0,14},{1,15},{2,4},{3,5},{4,2},{5,3},{6,8},{7,9},{8,6},{9,7},{10,... | collective-permute-start | bytes 393224 | tf_op jit(solution)/shard_map/ppermute | solution.py:33
  136.4 0.0 collective-permute-done.3.refs_0_
  136.4 3.1 %collective-permute-done.4.refs_1_ = bf16[256,256]{1,0:T(8,128)(2,1)S(1)} collective-permute-done((bf16[256,256]{1,0:T(8,128)(2,1)S(1)}, bf16[256,256]{1,0:T(8,128)(2,1)S(1)}, u32[]{:S(2)}, u32[]{:S(2)}) %collective-permute-start.4) | collective-permute-done | bytes 131104 | tf_op jit(solution)/shard_map/ppermute | solution.py:33
  139.5 2.4 %collective-permute-done.5.refs_2_ = bf16[256,256]{1,0:T(8,128)(2,1)S(1)} collective-permute-done((bf16[256,256]{1,0:T(8,128)(2,1)S(1)}, bf16[256,256]{1,0:T(8,128)(2,1)S(1)}, u32[]{:S(2)}, u32[]{:S(2)}) %collective-permute-start.5) | collective-permute-done | bytes 131104 | tf_op jit(solution)/shard_map/ppermute | solution.py:33
  141.9 0.8 shard_map.124
  (3 shorter events, 0.0 us)
Async XLA Ops:
  1.9 89.3 %all-to-all-start = ((bf16[32,16,256]{2,1,0:T(8,128)(2,1)}), bf16[32,16,256]{2,1,0:T(8,128)(2,1)S(1)}, u32[]{:S(2)}, u32[]{:S(2)}) async-start(bf16[32,16,256]{2,1,0:T(8,128)(2,1)} %bitcast.8), calls=%async_computation | async-start | bytes 524288 | tf_op jit(solution)/shard_map/all_to_all | solution.py:296
  15.6 75.6 %copy-start.4 = (bf16[256,528]{1,0:T(8,128)(2,1)S(1)}, bf16[256,528]{1,0:T(8,128)(2,1)}, u32[]{:S(2)}) copy-start(bf16[256,528]{1,0:T(8,128)(2,1)} %constant.30.clone.refs_4_) | copy-start | bytes 811012
  15.6 75.6 %copy-start.5 = (bf16[256,256]{1,0:T(8,128)(2,1)S(1)}, bf16[256,256]{1,0:T(8,128)(2,1)}, u32[]{:S(2)}) copy-start(bf16[256,256]{1,0:T(8,128)(2,1)} %constant.29.clone.refs_3_) | copy-start | bytes 393220
  15.6 75.6 %copy-start.6 = (bf16[256,256]{1,0:T(8,128)(2,1)S(1)}, bf16[256,256]{1,0:T(8,128)(2,1)}, u32[]{:S(2)}) copy-start(bf16[256,256]{1,0:T(8,128)(2,1)} %constant.28.clone.refs_2_) | copy-start | bytes 393220
  15.6 75.6 %copy-start.7 = (f32[33,256]{1,0:T(8,128)S(1)}, f32[33,256]{1,0:T(8,128)}, u32[]{:S(2)}) copy-start(f32[33,256]{1,0:T(8,128)} %constant.32.clone.refs_6_) | copy-start | bytes 101380
  15.7 75.6 %copy-start.8 = (f32[33,256]{1,0:T(8,128)S(1)}, f32[33,256]{1,0:T(8,128)}, u32[]{:S(2)}) copy-start(f32[33,256]{1,0:T(8,128)} %constant.31.clone.refs_5_) | copy-start | bytes 101380
  15.7 75.6 %copy-start.9 = (bf16[66,32]{1,0:T(8,128)(2,1)S(1)}, bf16[66,32]{1,0:T(8,128)(2,1)}, u32[]{:S(2)}) copy-start(bf16[66,32]{1,0:T(8,128)(2,1)} %constant.27.clone.refs_1_) | copy-start | bytes 12676
  49.2 55.0 %collective-permute-start = (bf16[256,1024]{1,0:T(8,128)(2,1)}, bf16[256,1024]{1,0:T(8,128)(2,1)S(1)}, u32[]{:S(2)}, u32[]{:S(2)}) collective-permute-start(bf16[256,1024]{1,0:T(8,128)(2,1)} %get-tuple-element.15), channel_id=1, source_target_pairs={{0,2},{1,3},{2,0},{3,1},{4,6},{5,7},{6,4},{7,5},{8,10},{9,11},{10,... | collective-permute-start | bytes 1572872 | tf_op jit(solution)/shard_map/ppermute | solution.py:305
  52.4 51.8 %collective-permute-start.1 = (bf16[256,1024]{1,0:T(8,128)(2,1)}, bf16[256,1024]{1,0:T(8,128)(2,1)S(1)}, u32[]{:S(2)}, u32[]{:S(2)}) collective-permute-start(bf16[256,1024]{1,0:T(8,128)(2,1)} %get-tuple-element.16), channel_id=1, source_target_pairs={{0,3},{1,2},{2,1},{3,0},{4,7},{5,6},{6,5},{7,4},{8,11},{9,10},{10,... | collective-permute-start | bytes 1572872 | tf_op jit(solution)/shard_map/ppermute | solution.py:305
  89.1 14.9 %copy-start.10 = (f32[256]{0:T(256)S(1)}, f32[256]{0:T(256)}, u32[]{:S(2)}) copy-start(f32[256]{0:T(256)} %param.16) | copy-start | bytes 3076
  89.1 24.1 %copy-start = (bf16[256,256]{1,0:T(8,128)(2,1)S(1)}, bf16[256,256]{1,0:T(8,128)(2,1)}, u32[]{:S(2)}) copy-start(bf16[256,256]{1,0:T(8,128)(2,1)} %signal_ref.1) | copy-start | bytes 393220
  89.1 24.1 %copy-start.1 = (bf16[256,256]{1,0:T(8,128)(2,1)S(1)}, bf16[256,256]{1,0:T(8,128)(2,1)}, u32[]{:S(2)}) copy-start(bf16[256,256]{1,0:T(8,128)(2,1)} %pre_ref.1) | copy-start | bytes 393220
  89.1 24.1 %copy-start.3 = (bf16[256,256]{1,0:T(8,128)(2,1)S(1)}, bf16[256,256]{1,0:T(8,128)(2,1)}, u32[]{:S(2)}) copy-start(bf16[256,256]{1,0:T(8,128)(2,1)} %post_ref.1) | copy-start | bytes 393220
  89.1 33.3 %collective-permute-start.2 = (bf16[256,1024]{1,0:T(8,128)(2,1)}, bf16[256,1024]{1,0:T(8,128)(2,1)S(1)}, u32[]{:S(2)}, u32[]{:S(2)}) collective-permute-start(bf16[256,1024]{1,0:T(8,128)(2,1)} %get-tuple-element.18), channel_id=1, source_target_pairs={{0,1},{1,0},{2,3},{3,2},{4,5},{5,4},{6,7},{7,6},{8,9},{9,8},{10,11... | collective-permute-start | bytes 1572872 | tf_op jit(solution)/shard_map/ppermute | solution.py:305
  91.2 31.2 %copy-start.2 = (bf16[256,1024]{1,0:T(8,128)(2,1)S(1)}, bf16[256,1024]{1,0:T(8,128)(2,1)}, u32[]{:S(2)}) copy-start(bf16[256,1024]{1,0:T(8,128)(2,1)} %get-tuple-element.17.refs_2_) | copy-start | bytes 1572868
  94.5 18.7 %all-to-all-start.1 = ((bf16[32,8,256]{2,1,0:T(8,128)(2,1)}), bf16[32,8,256]{2,1,0:T(8,128)(2,1)S(1)}, u32[]{:S(2)}, u32[]{:S(2)}) async-start(bf16[32,8,256]{2,1,0:T(8,128)(2,1)} %bitcast.3), calls=%async_computation.1 | async-start | bytes 262144 | tf_op jit(solution)/shard_map/all_to_all | solution.py:308
  123.1 13.2 %collective-permute-start.3 = (bf16[256,256]{1,0:T(8,128)(2,1)S(1)}, bf16[256,256]{1,0:T(8,128)(2,1)S(1)}, u32[]{:S(2)}, u32[]{:S(2)}) collective-permute-start(bf16[256,256]{1,0:T(8,128)(2,1)S(1)} %get-tuple-element.19), channel_id=1, source_target_pairs={{0,10},{1,11},{2,8},{3,9},{4,14},{5,15},{6,12},{7,13},{8,2},{9,3},... | collective-permute-start | bytes 393224 | tf_op jit(solution)/shard_map/ppermute | solution.py:33
  129.6 9.9 %collective-permute-start.4 = (bf16[256,256]{1,0:T(8,128)(2,1)S(1)}, bf16[256,256]{1,0:T(8,128)(2,1)S(1)}, u32[]{:S(2)}, u32[]{:S(2)}) collective-permute-start(bf16[256,256]{1,0:T(8,128)(2,1)S(1)} %get-tuple-element.20), channel_id=1, source_target_pairs={{0,12},{1,13},{2,6},{3,7},{4,0},{5,1},{6,10},{7,11},{8,4},{9,5},{1... | collective-permute-start | bytes 393224 | tf_op jit(solution)/shard_map/ppermute | solution.py:33
  131.9 9.9 %collective-permute-start.5 = (bf16[256,256]{1,0:T(8,128)(2,1)S(1)}, bf16[256,256]{1,0:T(8,128)(2,1)S(1)}, u32[]{:S(2)}, u32[]{:S(2)}) collective-permute-start(bf16[256,256]{1,0:T(8,128)(2,1)S(1)} %get-tuple-element.21), channel_id=1, source_target_pairs={{0,14},{1,15},{2,4},{3,5},{4,2},{5,3},{6,8},{7,9},{8,6},{9,7},{10,... | collective-permute-start | bytes 393224 | tf_op jit(solution)/shard_map/ppermute | solution.py:33

commit v5 on v4

--- a/solution.py
+++ b/solution.py
@@ -66,7 +66,7 @@
             pl.BlockSpec(memory_space=pltpu.SMEM),
             pl.BlockSpec(memory_space=pltpu.HBM),
         ],
-        out_specs=[pl.BlockSpec(memory_space=pltpu.HBM)] * len(members)
+        out_specs=[pl.BlockSpec(memory_space=pltpu.VMEM)] * len(members)
         + [pl.BlockSpec(memory_space=pltpu.SMEM)],
         scratch_shapes=[pltpu.SemaphoreType.DMA((len(members) * group,))],
         compiler_params=pltpu.CompilerParams(vmem_limit_bytes=60 * MIB),

time: 143 us -> 81 us (0.57)
  Pallas kernels: 73.7 us -> 11.5 us
    pallas_call x2, Pallas kernels: 67 us -> 4.84 us  [arrange(): pl.pallas_call(lambda *refs: arrange_kernel(group, quads, width, members,...]
    ppermute x3, waiting for transfers between devices: 0.01 us -> 3.12 us  [per_device(): lax.ppermute(piece, GROUP, [(t, t ^ r) for t in range(group)])]
    all_to_all x1, waiting for transfers between devices: 8.96 us -> 5.88 us  [per_device(): lax.all_to_all(convolved, 'ctx', split_axis=0, concat_axis=0, tiled=True)]
  transfers between devices with their start and end apart: 8 -> 8, of which waited for: 3 -> 4; matrix products, arithmetic and copies ran while one was open for 0% -> 0% of each run, Pallas kernels for 49% -> 10%
where the time goes in v5:
time: 81 us; the launch traced here: 80.5 us
  starting transfers between devices  44.9 us (55%)
  waiting for transfers between devices  14.5 us (18%)
  Pallas kernels  11.5 us (14%)
  blocking collectives  9.08 us (11%)
    all_to_all x1, starting transfers between devices, per_device(): lax.all_to_all(send, 'ctx', split_axis=0, concat_axis=0, tiled=True)  13.7 us
    ppermute x3, starting transfers between devices, send_to_target(): return lax.ppermute(share, TP_AXES, pairs)  13.2 us
    all_to_all x1, starting transfers between devices, per_device(): lax.all_to_all(convolved, 'ctx', split_axis=0, concat_axis=0, tiled=True)  9.5 us
    all_gather x1, blocking collectives, per_device(): gathered = lax.all_gather(mixed, GROUP, axis=0, tiled=True)  9.08 us
    ppermute x3, starting transfers between devices, per_device(): lax.ppermute(piece, GROUP, [(t, t ^ r) for t in range(group)])  8.45 us
    all_to_all x1, waiting for transfers between devices, per_device(): lax.all_to_all(convolved, 'ctx', split_axis=0, concat_axis=0, tiled=True)  5.88 us
    ppermute x3, waiting for transfers between devices, send_to_target(): return lax.ppermute(share, TP_AXES, pairs)  5.49 us
    pallas_call x2, Pallas kernels, arrange(): pl.pallas_call(lambda *refs: arrange_kernel(group, quads, width, members,...  4.84 us
  transfers between devices with their start and end apart: 8, of which 4 were waited for; matrix products, arithmetic and copies ran while one was open for 0% of the time, Pallas kernels for 10%

profile of v5, /device:TPU:1, one launch (start us, length us, event | category | flops | bytes accessed | tf_op | source)
XLA Modules:
  0.0 80.5 jit_solution(7894793992835026418)
XLA Ops:
  0.0 1.9 %shard_map.118 = bf16[512,256]{1,0:T(8,128)(2,1)} custom-call(bf16[256,256]{1,0:T(8,128)(2,1)} %signal_ref.1, bf16[256,256]{1,0:T(8,128)(2,1)} %pre_ref.1, f32[256,256]{1,0:T(8,128)} %refs_2_.2), custom_call_target="tpu_custom_call" | custom-call | tf_op jit(solution)/shard_map/pallas_call | solution.py:249
  1.9 13.7 %all-to-all-start = ((bf16[32,16,256]{2,1,0:T(8,128)(2,1)}), bf16[32,16,256]{2,1,0:T(8,128)(2,1)S(1)}, u32[]{:S(2)}, u32[]{:S(2)}) async-start(bf16[32,16,256]{2,1,0:T(8,128)(2,1)} %bitcast.8), calls=%async_computation | async-start | bytes 524288 | tf_op jit(solution)/shard_map/all_to_all | solution.py:296
  15.6 0.0 copy-start.4
  15.6 0.0 copy-start.5
  15.6 0.0 copy-start.6
  15.6 0.0 copy-start.7
  15.7 0.0 copy-start.8
  15.7 0.0 copy-start.9
  15.7 2.5 %shard_map.119 = (bf16[256,1024]{1,0:T(8,128)(2,1)}, bf16[256,1024]{1,0:T(8,128)(2,1)}, s32[1]{0:T(128)}) custom-call(s32[1]{0:T(128)} %bitcast.refs_0_, bf16[256,4096]{1,0:T(8,128)(2,1)} %refs_1_.6), custom_call_target="tpu_custom_call" | custom-call | bytes 2097152 | tf_op jit(solution)/shard_map/pallas_call | solution.py:62
  18.2 3.2 %collective-permute-start = (bf16[256,1024]{1,0:T(8,128)(2,1)}, bf16[256,1024]{1,0:T(8,128)(2,1)S(1)}, u32[]{:S(2)}, u32[]{:S(2)}) collective-permute-start(bf16[256,1024]{1,0:T(8,128)(2,1)} %get-tuple-element.15), channel_id=1, source_target_pairs={{0,2},{1,3},{2,0},{3,1},{4,6},{5,7},{6,4},{7,5},{8,10},{9,11},{10,... | collective-permute-start | bytes 1572872 | tf_op jit(solution)/shard_map/ppermute | solution.py:305
  21.4 3.2 %collective-permute-start.1 = (bf16[256,1024]{1,0:T(8,128)(2,1)}, bf16[256,1024]{1,0:T(8,128)(2,1)S(1)}, u32[]{:S(2)}, u32[]{:S(2)}) collective-permute-start(bf16[256,1024]{1,0:T(8,128)(2,1)} %get-tuple-element.16), channel_id=1, source_target_pairs={{0,3},{1,2},{2,1},{3,0},{4,7},{5,6},{6,5},{7,4},{8,11},{9,10},{10,... | collective-permute-start | bytes 1572872 | tf_op jit(solution)/shard_map/ppermute | solution.py:305
  24.6 2.4 %shard_map.122 = (bf16[256,1024]{1,0:T(8,128)(2,1)}, bf16[256,1024]{1,0:T(8,128)(2,1)}, s32[1]{0:T(128)}) custom-call(s32[1]{0:T(128)} %bitcast.refs_0_, bf16[256,4096]{1,0:T(8,128)(2,1)} %refs_1_.6), custom_call_target="tpu_custom_call" | custom-call | bytes 2097152 | tf_op jit(solution)/shard_map/pallas_call | solution.py:62
  26.9 0.0 copy-start.10
  27.0 0.0 copy-start
  27.0 0.0 copy-start.1
  27.0 0.0 copy-start.3
  27.0 2.1 %collective-permute-start.2 = (bf16[256,1024]{1,0:T(8,128)(2,1)}, bf16[256,1024]{1,0:T(8,128)(2,1)S(1)}, u32[]{:S(2)}, u32[]{:S(2)}) collective-permute-start(bf16[256,1024]{1,0:T(8,128)(2,1)} %get-tuple-element.18), channel_id=1, source_target_pairs={{0,1},{1,0},{2,3},{3,2},{4,5},{5,4},{6,7},{7,6},{8,9},{9,8},{10,11... | collective-permute-start | bytes 1572872 | tf_op jit(solution)/shard_map/ppermute | solution.py:305
  29.1 0.0 all-to-all-done
  29.1 0.0 copy-done.4
  29.1 0.0 copy-done.5
  29.1 0.0 copy-done.6
  29.1 0.0 copy-done.7
  29.1 0.0 copy-done.8
  29.1 0.0 copy-done.9
  29.1 0.0 copy-start.2
  29.1 3.2 %shard_map.120 = bf16[256,256]{1,0:T(8,128)(2,1)} custom-call(bf16[512,256]{1,0:T(8,128)(2,1)S(1)} %bitcast.7, bf16[66,32]{1,0:T(8,128)(2,1)S(1)} %copy-done.9, bf16[256,256]{1,0:T(8,128)(2,1)S(1)} %copy-done.6, bf16[256,256]{1,0:T(8,128)(2,1)S(1)} %copy-done.5, bf16[256,528]{1,0:T(8,128)(2,1)S(1)} %copy-done.4, f32[33,256]{1,0:T(8,128)S(1)} %copy-done.8, ...), custom_call_target="tpu_custom_call" | custom-call | flops 800000000 | bytes 3000000 | tf_op jit(solution)/shard_map/pallas_call | solution.py:210
  32.3 9.5 %all-to-all-start.1 = ((bf16[32,8,256]{2,1,0:T(8,128)(2,1)}), bf16[32,8,256]{2,1,0:T(8,128)(2,1)S(1)}, u32[]{:S(2)}, u32[]{:S(2)}) async-start(bf16[32,8,256]{2,1,0:T(8,128)(2,1)} %bitcast.3), calls=%async_computation.1 | async-start | bytes 262144 | tf_op jit(solution)/shard_map/all_to_all | solution.py:308
  41.9 0.0 copy-done.10
  41.9 0.1 copy.13.gain_ref
  42.0 0.0 collective-permute-done.refs_4_
  42.0 3.1 %collective-permute-done.1.refs_5_ = bf16[256,1024]{1,0:T(8,128)(2,1)S(1)} collective-permute-done((bf16[256,1024]{1,0:T(8,128)(2,1)}, bf16[256,1024]{1,0:T(8,128)(2,1)S(1)}, u32[]{:S(2)}, u32[]{:S(2)}) %collective-permute-start.1) | collective-permute-done | bytes 524320 | tf_op jit(solution)/shard_map/ppermute | solution.py:305
  45.1 5.9 %all-to-all-done.1 = bf16[32,8,256]{2,1,0:T(8,128)(2,1)S(1)} async-done(((bf16[32,8,256]{2,1,0:T(8,128)(2,1)}), bf16[32,8,256]{2,1,0:T(8,128)(2,1)S(1)}, u32[]{:S(2)}, u32[]{:S(2)}) %all-to-all-start.1) | async-done | bytes 131104 | tf_op jit(solution)/shard_map/all_to_all | solution.py:308
  51.0 0.0 copy-done
  51.0 0.0 copy-done.1
  51.0 0.0 copy-done.3
  51.0 0.2 shard_map.121
  51.2 9.1 %all_gather.3.refs_1_ = bf16[1024,256]{1,0:T(8,128)(2,1)S(1)} all-gather(bf16[256,256]{1,0:T(8,128)(2,1)S(1)} %shard_map.121), channel_id=1, replica_groups=mesh['ctx'=32,'quad'=4,'pair'=2,'core'=2] {'pair','core'}, dimensions={0}, use_global_device_ids=true | all-gather | bytes 655360 | tf_op jit(solution)/shard_map/all_gather | solution.py:312
  60.3 0.0 collective-permute-done.2.refs_3_
  60.3 0.0 copy-done.2
  60.3 0.7 shard_map.123
  61.0 6.5 %collective-permute-start.3 = (bf16[256,256]{1,0:T(8,128)(2,1)S(1)}, bf16[256,256]{1,0:T(8,128)(2,1)S(1)}, u32[]{:S(2)}, u32[]{:S(2)}) collective-permute-start(bf16[256,256]{1,0:T(8,128)(2,1)S(1)} %get-tuple-element.19), channel_id=1, source_target_pairs={{0,10},{1,11},{2,8},{3,9},{4,14},{5,15},{6,12},{7,13},{8,2},{9,3},... | collective-permute-start | bytes 393224 | tf_op jit(solution)/shard_map/ppermute | solution.py:33
  67.5 2.3 %collective-permute-start.4 = (bf16[256,256]{1,0:T(8,128)(2,1)S(1)}, bf16[256,256]{1,0:T(8,128)(2,1)S(1)}, u32[]{:S(2)}, u32[]{:S(2)}) collective-permute-start(bf16[256,256]{1,0:T(8,128)(2,1)S(1)} %get-tuple-element.20), channel_id=1, source_target_pairs={{0,12},{1,13},{2,6},{3,7},{4,0},{5,1},{6,10},{7,11},{8,4},{9,5},{1... | collective-permute-start | bytes 393224 | tf_op jit(solution)/shard_map/ppermute | solution.py:33
  69.8 4.4 %collective-permute-start.5 = (bf16[256,256]{1,0:T(8,128)(2,1)S(1)}, bf16[256,256]{1,0:T(8,128)(2,1)S(1)}, u32[]{:S(2)}, u32[]{:S(2)}) collective-permute-start(bf16[256,256]{1,0:T(8,128)(2,1)S(1)} %get-tuple-element.21), channel_id=1, source_target_pairs={{0,14},{1,15},{2,4},{3,5},{4,2},{5,3},{6,8},{7,9},{8,6},{9,7},{10,... | collective-permute-start | bytes 393224 | tf_op jit(solution)/shard_map/ppermute | solution.py:33
  74.3 0.0 collective-permute-done.3.refs_0_
  74.3 3.1 %collective-permute-done.4.refs_1_ = bf16[256,256]{1,0:T(8,128)(2,1)S(1)} collective-permute-done((bf16[256,256]{1,0:T(8,128)(2,1)S(1)}, bf16[256,256]{1,0:T(8,128)(2,1)S(1)}, u32[]{:S(2)}, u32[]{:S(2)}) %collective-permute-start.4) | collective-permute-done | bytes 131104 | tf_op jit(solution)/shard_map/ppermute | solution.py:33
  77.4 2.4 %collective-permute-done.5.refs_2_ = bf16[256,256]{1,0:T(8,128)(2,1)S(1)} collective-permute-done((bf16[256,256]{1,0:T(8,128)(2,1)S(1)}, bf16[256,256]{1,0:T(8,128)(2,1)S(1)}, u32[]{:S(2)}, u32[]{:S(2)}) %collective-permute-start.5) | collective-permute-done | bytes 131104 | tf_op jit(solution)/shard_map/ppermute | solution.py:33
  79.8 0.8 shard_map.124
  (3 shorter events, 0.0 us)
Async XLA Ops:
  1.9 27.2 %all-to-all-start = ((bf16[32,16,256]{2,1,0:T(8,128)(2,1)}), bf16[32,16,256]{2,1,0:T(8,128)(2,1)S(1)}, u32[]{:S(2)}, u32[]{:S(2)}) async-start(bf16[32,16,256]{2,1,0:T(8,128)(2,1)} %bitcast.8), calls=%async_computation | async-start | bytes 524288 | tf_op jit(solution)/shard_map/all_to_all | solution.py:296
  15.6 13.5 %copy-start.4 = (bf16[256,528]{1,0:T(8,128)(2,1)S(1)}, bf16[256,528]{1,0:T(8,128)(2,1)}, u32[]{:S(2)}) copy-start(bf16[256,528]{1,0:T(8,128)(2,1)} %constant.30.clone.refs_4_) | copy-start | bytes 811012
  15.6 13.5 %copy-start.5 = (bf16[256,256]{1,0:T(8,128)(2,1)S(1)}, bf16[256,256]{1,0:T(8,128)(2,1)}, u32[]{:S(2)}) copy-start(bf16[256,256]{1,0:T(8,128)(2,1)} %constant.29.clone.refs_3_) | copy-start | bytes 393220
  15.6 13.5 %copy-start.6 = (bf16[256,256]{1,0:T(8,128)(2,1)S(1)}, bf16[256,256]{1,0:T(8,128)(2,1)}, u32[]{:S(2)}) copy-start(bf16[256,256]{1,0:T(8,128)(2,1)} %constant.28.clone.refs_2_) | copy-start | bytes 393220
  15.6 13.5 %copy-start.7 = (f32[33,256]{1,0:T(8,128)S(1)}, f32[33,256]{1,0:T(8,128)}, u32[]{:S(2)}) copy-start(f32[33,256]{1,0:T(8,128)} %constant.32.clone.refs_6_) | copy-start | bytes 101380
  15.7 13.5 %copy-start.8 = (f32[33,256]{1,0:T(8,128)S(1)}, f32[33,256]{1,0:T(8,128)}, u32[]{:S(2)}) copy-start(f32[33,256]{1,0:T(8,128)} %constant.31.clone.refs_5_) | copy-start | bytes 101380
  15.7 13.5 %copy-start.9 = (bf16[66,32]{1,0:T(8,128)(2,1)S(1)}, bf16[66,32]{1,0:T(8,128)(2,1)}, u32[]{:S(2)}) copy-start(bf16[66,32]{1,0:T(8,128)(2,1)} %constant.27.clone.refs_1_) | copy-start | bytes 12676
  18.2 23.9 %collective-permute-start = (bf16[256,1024]{1,0:T(8,128)(2,1)}, bf16[256,1024]{1,0:T(8,128)(2,1)S(1)}, u32[]{:S(2)}, u32[]{:S(2)}) collective-permute-start(bf16[256,1024]{1,0:T(8,128)(2,1)} %get-tuple-element.15), channel_id=1, source_target_pairs={{0,2},{1,3},{2,0},{3,1},{4,6},{5,7},{6,4},{7,5},{8,10},{9,11},{10,... | collective-permute-start | bytes 1572872 | tf_op jit(solution)/shard_map/ppermute | solution.py:305
  21.4 23.8 %collective-permute-start.1 = (bf16[256,1024]{1,0:T(8,128)(2,1)}, bf16[256,1024]{1,0:T(8,128)(2,1)S(1)}, u32[]{:S(2)}, u32[]{:S(2)}) collective-permute-start(bf16[256,1024]{1,0:T(8,128)(2,1)} %get-tuple-element.16), channel_id=1, source_target_pairs={{0,3},{1,2},{2,1},{3,0},{4,7},{5,6},{6,5},{7,4},{8,11},{9,10},{10,... | collective-permute-start | bytes 1572872 | tf_op jit(solution)/shard_map/ppermute | solution.py:305
  26.9 14.9 %copy-start.10 = (f32[256]{0:T(256)S(1)}, f32[256]{0:T(256)}, u32[]{:S(2)}) copy-start(f32[256]{0:T(256)} %param.16) | copy-start | bytes 3076
  27.0 24.1 %copy-start = (bf16[256,256]{1,0:T(8,128)(2,1)S(1)}, bf16[256,256]{1,0:T(8,128)(2,1)}, u32[]{:S(2)}) copy-start(bf16[256,256]{1,0:T(8,128)(2,1)} %signal_ref.1) | copy-start | bytes 393220
  27.0 24.1 %copy-start.1 = (bf16[256,256]{1,0:T(8,128)(2,1)S(1)}, bf16[256,256]{1,0:T(8,128)(2,1)}, u32[]{:S(2)}) copy-start(bf16[256,256]{1,0:T(8,128)(2,1)} %pre_ref.1) | copy-start | bytes 393220
  27.0 24.1 %copy-start.3 = (bf16[256,256]{1,0:T(8,128)(2,1)S(1)}, bf16[256,256]{1,0:T(8,128)(2,1)}, u32[]{:S(2)}) copy-start(bf16[256,256]{1,0:T(8,128)(2,1)} %post_ref.1) | copy-start | bytes 393220
  27.0 33.3 %collective-permute-start.2 = (bf16[256,1024]{1,0:T(8,128)(2,1)}, bf16[256,1024]{1,0:T(8,128)(2,1)S(1)}, u32[]{:S(2)}, u32[]{:S(2)}) collective-permute-start(bf16[256,1024]{1,0:T(8,128)(2,1)} %get-tuple-element.18), channel_id=1, source_target_pairs={{0,1},{1,0},{2,3},{3,2},{4,5},{5,4},{6,7},{7,6},{8,9},{9,8},{10,11... | collective-permute-start | bytes 1572872 | tf_op jit(solution)/shard_map/ppermute | solution.py:305
  29.1 31.2 %copy-start.2 = (bf16[256,1024]{1,0:T(8,128)(2,1)S(1)}, bf16[256,1024]{1,0:T(8,128)(2,1)}, u32[]{:S(2)}) copy-start(bf16[256,1024]{1,0:T(8,128)(2,1)} %get-tuple-element.17.refs_2_) | copy-start | bytes 1572868
  32.3 18.7 %all-to-all-start.1 = ((bf16[32,8,256]{2,1,0:T(8,128)(2,1)}), bf16[32,8,256]{2,1,0:T(8,128)(2,1)S(1)}, u32[]{:S(2)}, u32[]{:S(2)}) async-start(bf16[32,8,256]{2,1,0:T(8,128)(2,1)} %bitcast.3), calls=%async_computation.1 | async-start | bytes 262144 | tf_op jit(solution)/shard_map/all_to_all | solution.py:308
  61.0 13.2 %collective-permute-start.3 = (bf16[256,256]{1,0:T(8,128)(2,1)S(1)}, bf16[256,256]{1,0:T(8,128)(2,1)S(1)}, u32[]{:S(2)}, u32[]{:S(2)}) collective-permute-start(bf16[256,256]{1,0:T(8,128)(2,1)S(1)} %get-tuple-element.19), channel_id=1, source_target_pairs={{0,10},{1,11},{2,8},{3,9},{4,14},{5,15},{6,12},{7,13},{8,2},{9,3},... | collective-permute-start | bytes 393224 | tf_op jit(solution)/shard_map/ppermute | solution.py:33
  67.5 9.9 %collective-permute-start.4 = (bf16[256,256]{1,0:T(8,128)(2,1)S(1)}, bf16[256,256]{1,0:T(8,128)(2,1)S(1)}, u32[]{:S(2)}, u32[]{:S(2)}) collective-permute-start(bf16[256,256]{1,0:T(8,128)(2,1)S(1)} %get-tuple-element.20), channel_id=1, source_target_pairs={{0,12},{1,13},{2,6},{3,7},{4,0},{5,1},{6,10},{7,11},{8,4},{9,5},{1... | collective-permute-start | bytes 393224 | tf_op jit(solution)/shard_map/ppermute | solution.py:33
  69.8 9.9 %collective-permute-start.5 = (bf16[256,256]{1,0:T(8,128)(2,1)S(1)}, bf16[256,256]{1,0:T(8,128)(2,1)S(1)}, u32[]{:S(2)}, u32[]{:S(2)}) collective-permute-start(bf16[256,256]{1,0:T(8,128)(2,1)S(1)} %get-tuple-element.21), channel_id=1, source_target_pairs={{0,14},{1,15},{2,4},{3,5},{4,2},{5,3},{6,8},{7,9},{8,6},{9,7},{10,... | collective-permute-start | bytes 393224 | tf_op jit(solution)/shard_map/ppermute | solution.py:33

commit v6 on v4

--- a/solution.py
+++ b/solution.py
@@ -34,30 +34,39 @@
 
 
 def arrange_kernel(group, quads, width, members, place_ref, weight_ref, *refs):
-    out_refs, done_ref, sems = refs[: len(members)], refs[-2], refs[-1]
+    count = len(members) * group
+    out_refs, done_ref, blocks, in_sems, out_sems = refs[: len(members)], *refs[-4:]
     tp = place_ref[0]
     quad, place = tp // group, lax.rem(tp, group)
-    copies = []
+    loads, stores = [], []
     for n, r in enumerate(members):
         other = place ^ r
         for i, target in enumerate(targets_of(quad, other // 2, lax.rem(other, 2), quads)):
+            k = n * group + i
             start = pl.multiple_of(target * width, width)
-            copies.append(
+            loads.append(
                 pltpu.make_async_copy(
-                    weight_ref.at[:, pl.ds(start, width)],
-                    out_refs[n].at[:, pl.ds(i * width, width)],
-                    sems.at[n * group + i],
+                    weight_ref.at[:, pl.ds(start, width)], blocks.at[k], in_sems.at[k]
                 )
             )
-    for copy in copies:
-        copy.start()
-    for copy in copies:
-        copy.wait()
+            stores.append(
+                pltpu.make_async_copy(
+                    blocks.at[k], out_refs[n].at[:, pl.ds(i * width, width)], out_sems.at[k]
+                )
+            )
+    for load in loads:
+        load.start()
+    for k in range(count):
+        loads[k].wait()
+        stores[k].start()
+    for store in stores:
+        store.wait()
     done_ref[0] = tp
 
 
 def arrange(out_weight, place, group, quads, width, members):
     rows = out_weight.shape[0]
+    count = len(members) * group
     piece = jax.ShapeDtypeStruct((rows, group * width), out_weight.dtype)
     *pieces, done = pl.pallas_call(
         lambda *refs: arrange_kernel(group, quads, width, members, *refs),
@@ -68,54 +77,84 @@
         ],
         out_specs=[pl.BlockSpec(memory_space=pltpu.HBM)] * len(members)
         + [pl.BlockSpec(memory_space=pltpu.SMEM)],
-        scratch_shapes=[pltpu.SemaphoreType.DMA((len(members) * group,))],
+        scratch_shapes=[
+            pltpu.VMEM((count, rows, width), out_weight.dtype),
+            pltpu.SemaphoreType.DMA((count,)),
+            pltpu.SemaphoreType.DMA((count,)),
+        ],
         compiler_params=pltpu.CompilerParams(vmem_limit_bytes=60 * MIB),
         cost_estimate=pl.CostEstimate(
-            flops=0,
-            bytes_accessed=4 * rows * len(members) * group * width,
-            transcendentals=0,
+            flops=0, bytes_accessed=4 * rows * count * width, transcendentals=0
         ),
     )(place, out_weight)
     return pieces, done
 
 
-def project_kernel(group, place_ref, mixed_ref, *refs):
-    weight_refs, out_refs = refs[:group], refs[group:]
+def project_kernel(
+    group, quads, place_ref, mixed_ref, own_ref, *refs
+):
+    piece_refs, out_refs = refs[: group - 1], refs[group - 1 : 2 * group - 1]
+    blocks, totals, sems = refs[-3:]
     tokens = mixed_ref.shape[0] // group
     width = out_refs[0].shape[1]
-    place = lax.rem(place_ref[0], group)
+    tp = place_ref[0]
+    quad, place = tp // group, lax.rem(tp, group)
+    targets = targets_of(quad, place // 2, lax.rem(place, 2), quads)
+    loads = []
+    for i, target in enumerate(targets):
+        start = pl.multiple_of(target * width, width)
+        loads.append(
+            pltpu.make_async_copy(own_ref.at[:, pl.ds(start, width)], blocks.at[i], sems.at[i])
+        )
+    for load in loads:
+        load.start()
     mixed = [
         mixed_ref[pl.ds(pl.multiple_of((place ^ r) * tokens, tokens), tokens), :]
         for r in range(group)
     ]
+
+    def product(r, weights):
+        return jnp.dot(mixed[r], weights, preferred_element_type=jnp.float32)
+
     for i in range(group):
-        total = None
-        for r in range(group):
-            term = jnp.dot(
-                mixed[r],
-                weight_refs[r][:, i * width : (i + 1) * width],
-                preferred_element_type=jnp.float32,
-            )
-            total = term if total is None else total + term
+        columns = slice(i * width, (i + 1) * width)
+        total = product(1, piece_refs[0][:, columns])
+        for r in range(2, group):
+            total = total + product(r, piece_refs[r - 1][:, columns])
+        totals[i] = total
+    for i in range(group):
+        loads[i].wait()
+        total = totals[i] + product(0, blocks[i])
         out_refs[i][...] = total.astype(out_refs[i].dtype)
 
 
-def project(place, mixed, weights, width):
-    group = len(weights)
-    share = jax.ShapeDtypeStruct((mixed.shape[0] // group, width), mixed.dtype)
+def project(place, mixed, own, pieces, group, quads):
+    rows = own.shape[0]
+    width = pieces[0].shape[1] // group
+    tokens = mixed.shape[0] // group
+    share = jax.ShapeDtypeStruct((tokens, width), mixed.dtype)
     return pl.pallas_call(
-        lambda *refs: project_kernel(group, *refs),
+        lambda *refs: project_kernel(group, quads, *refs),
         out_shape=[share] * group,
-        in_specs=[pl.BlockSpec(memory_space=pltpu.SMEM)]
-        + [pl.BlockSpec(memory_space=pltpu.VMEM)] * (1 + group),
+        in_specs=[
+            pl.BlockSpec(memory_space=pltpu.SMEM),
+            pl.BlockSpec(memory_space=pltpu.VMEM),
+            pl.BlockSpec(memory_space=pltpu.HBM),
+        ]
+        + [pl.BlockSpec(memory_space=pltpu.VMEM)] * (group - 1),
         out_specs=[pl.BlockSpec(memory_space=pltpu.VMEM)] * group,
-        compiler_params=pltpu.CompilerParams(vmem_limit_bytes=10 * MIB),
+        scratch_shapes=[
+            pltpu.VMEM((group, rows, width), own.dtype),
+            pltpu.VMEM((group, tokens, width), jnp.float32),
+            pltpu.SemaphoreType.DMA((group,)),
+        ],
+        compiler_params=pltpu.CompilerParams(vmem_limit_bytes=60 * MIB),
         cost_estimate=pl.CostEstimate(
             flops=2 * mixed.size * group * width,
-            bytes_accessed=2 * (mixed.size + sum(w.size for w in weights) + group * share.size),
+            bytes_accessed=2 * (mixed.size + 4 * rows * group * width + group * share.size),
             transcendentals=0,
         ),
-    )(place, mixed, *weights)
+    )(place, mixed, own, *pieces)
 
 
 def finish_kernel(*refs):
@@ -296,8 +335,13 @@
     blocks = lax.all_to_all(send, "ctx", split_axis=0, concat_axis=0, tiled=True)
 
     place = lax.axis_index(TP_AXES).astype(jnp.int32).reshape(1)
-    crossing = [r for r in range(group) if r >= 2]
-    pieces, arranged = arrange(out_weight, place, group, quads, width, crossing)
+    members = [2, 3, 1]
+    pieces, arranged = arrange(out_weight, place, group, quads, width, members)
+    pieces = {
+        r: lax.ppermute(piece, GROUP, [(t, t ^ r) for t in range(group)])
+        for r, piece in zip(members, pieces)
+    }
+    pieces = [pieces[r] for r in range(1, group)]
     tables = dft_tables(devices, tokens_here, channels)
     convolved = convolve(blocks, channels, tables, arranged)
     inner, _ = arrange(out_weight, place, group, quads, width, [0, 1])
@@ -308,9 +352,9 @@
     convolved = lax.all_to_all(convolved, "ctx", split_axis=0, concat_axis=0, tiled=True).reshape(
         channels_here, tokens_here
     )
-    mixed = gate(post_gate, signal, pre_gate, convolved, skip_gain, weights[2:])
+    mixed = gate(post_gate, signal, pre_gate, convolved, skip_gain, pieces)
     gathered = lax.all_gather(mixed, GROUP, axis=0, tiled=True)
-    shares = project(place, gathered, weights, width)
+    shares = project(place, gathered, out_weight, pieces, group, quads)
     return finish([send_to_target(shares[step], step, quads) for step in range(3)] + [shares[3]])
 
 

time: 143 us -> 84.4 us (0.59)
  Pallas kernels: 73.7 us -> 13.3 us
    pallas_call x2 -> x1, Pallas kernels: 67 us -> 2.92 us  [arrange(): pl.pallas_call(lambda *refs: arrange_kernel(group, quads, width, members,...]
    all_to_all x1, waiting for transfers between devices: 8.96 us -> 0.12 us  [per_device(): lax.all_to_all(convolved, 'ctx', split_axis=0, concat_axis=0, tiled=True)]
    ppermute x3, waiting for transfers between devices: 0.01 us -> 8.81 us  [per_device(): lax.ppermute(piece, GROUP, [(t, t ^ r) for t in range(group)])]
    pallas_call x1, Pallas kernels: 0.7 us -> 4.34 us  [project(): pl.pallas_call(lambda *refs: project_kernel(group, quads, *refs), out_sha...]
  transfers between devices with their start and end apart: 8 -> 8, of which waited for: 3 -> 4; matrix products, arithmetic and copies ran while one was open for 0% -> 0% of each run, Pallas kernels for 49% -> 7%
where the time goes in v6:
time: 84.4 us; the launch traced here: 83.9 us
  starting transfers between devices  44.9 us (53%)
  waiting for transfers between devices  14.6 us (17%)
  Pallas kernels  13.3 us (16%)
  blocking collectives  9.65 us (11%)
  local copies, waits for them, and re-layouts  1.11 us (1%)
    all_to_all x1, starting transfers between devices, per_device(): lax.all_to_all(send, 'ctx', split_axis=0, concat_axis=0, tiled=True)  13.7 us
    ppermute x3, starting transfers between devices, send_to_target(): return lax.ppermute(share, TP_AXES, pairs)  13.2 us
    all_gather x1, blocking collectives, per_device(): gathered = lax.all_gather(mixed, GROUP, axis=0, tiled=True)  9.65 us
    all_to_all x1, starting transfers between devices, per_device(): lax.all_to_all(convolved, 'ctx', split_axis=0, concat_axis=0, tiled=True)  9.5 us
    ppermute x3, waiting for transfers between devices, per_device(): lax.ppermute(piece, GROUP, [(t, t ^ r) for t in range(group)])  8.81 us
    ppermute x3, starting transfers between devices, per_device(): lax.ppermute(piece, GROUP, [(t, t ^ r) for t in range(group)])  8.45 us
    ppermute x3, waiting for transfers between devices, send_to_target(): return lax.ppermute(share, TP_AXES, pairs)  5.69 us
    pallas_call x1, Pallas kernels, project(): pl.pallas_call(lambda *refs: project_kernel(group, quads, *refs), out_sha...  4.34 us
  transfers between devices with their start and end apart: 8, of which 4 were waited for; matrix products, arithmetic and copies ran while one was open for 0% of the time, Pallas kernels for 7%

profile of v6, /device:TPU:1, one launch (start us, length us, event | category | flops | bytes accessed | tf_op | source)
XLA Modules:
  0.0 83.9 jit_solution(3277252456126014147)
XLA Ops:
  0.0 0.0 copy-start.7
  0.0 0.0 copy-start.5
  0.0 0.0 copy-start.6
  0.0 0.0 copy-start.9
  0.0 1.9 %shard_map.118 = bf16[512,256]{1,0:T(8,128)(2,1)} custom-call(bf16[256,256]{1,0:T(8,128)(2,1)} %signal_ref.1, bf16[256,256]{1,0:T(8,128)(2,1)} %pre_ref.1, f32[256,256]{1,0:T(8,128)} %refs_2_.3), custom_call_target="tpu_custom_call" | custom-call | tf_op jit(solution)/shard_map/pallas_call | solution.py:288
  2.0 13.7 %all-to-all-start = ((bf16[32,16,256]{2,1,0:T(8,128)(2,1)}), bf16[32,16,256]{2,1,0:T(8,128)(2,1)S(1)}, u32[]{:S(2)}, u32[]{:S(2)}) async-start(bf16[32,16,256]{2,1,0:T(8,128)(2,1)} %bitcast.8), calls=%async_computation | async-start | bytes 524288 | tf_op jit(solution)/shard_map/all_to_all | solution.py:335
  15.7 2.9 %shard_map.119 = (bf16[256,1024]{1,0:T(8,128)(2,1)}, bf16[256,1024]{1,0:T(8,128)(2,1)}, bf16[256,1024]{1,0:T(8,128)(2,1)}, s32[1]{0:T(128)}) custom-call(s32[1]{0:T(128)} %bitcast.refs_0_, bf16[256,4096]{1,0:T(8,128)(2,1)} %refs_2_.4), custom_call_target="tpu_custom_call" | custom-call | bytes 3145728 | tf_op jit(solution)/shard_map/pallas_call | solution.py:71
  18.6 0.0 copy-start.13
  18.6 0.0 copy-start
  18.7 0.0 copy-start.1
  18.7 0.0 copy-start.2
  18.7 3.0 %collective-permute-start = (bf16[256,1024]{1,0:T(8,128)(2,1)}, bf16[256,1024]{1,0:T(8,128)(2,1)S(1)}, u32[]{:S(2)}, u32[]{:S(2)}) collective-permute-start(bf16[256,1024]{1,0:T(8,128)(2,1)} %get-tuple-element.14), channel_id=1, source_target_pairs={{0,1},{1,0},{2,3},{3,2},{4,5},{5,4},{6,7},{7,6},{8,9},{9,8},{10,11... | collective-permute-start | bytes 1572872 | tf_op jit(solution)/shard_map/ppermute | solution.py:341
  21.7 3.2 %collective-permute-start.1 = (bf16[256,1024]{1,0:T(8,128)(2,1)}, bf16[256,1024]{1,0:T(8,128)(2,1)S(1)}, u32[]{:S(2)}, u32[]{:S(2)}) collective-permute-start(bf16[256,1024]{1,0:T(8,128)(2,1)} %get-tuple-element.15), channel_id=1, source_target_pairs={{0,2},{1,3},{2,0},{3,1},{4,6},{5,7},{6,4},{7,5},{8,10},{9,11},{10,... | collective-permute-start | bytes 1572872 | tf_op jit(solution)/shard_map/ppermute | solution.py:341
  24.9 2.3 %collective-permute-start.2 = (bf16[256,1024]{1,0:T(8,128)(2,1)}, bf16[256,1024]{1,0:T(8,128)(2,1)S(1)}, u32[]{:S(2)}, u32[]{:S(2)}) collective-permute-start(bf16[256,1024]{1,0:T(8,128)(2,1)} %get-tuple-element.16), channel_id=1, source_target_pairs={{0,3},{1,2},{2,1},{3,0},{4,7},{5,6},{6,5},{7,4},{8,11},{9,10},{10,... | collective-permute-start | bytes 1572872 | tf_op jit(solution)/shard_map/ppermute | solution.py:341
  27.2 0.0 all-to-all-done
  27.2 0.0 copy-done.7
  27.2 0.0 copy-done.8
  27.2 0.0 copy-done.4
  27.2 0.0 copy-done.5
  27.2 0.0 copy-done.6
  27.2 0.0 copy-done.9
  27.2 3.2 %shard_map.120 = bf16[256,256]{1,0:T(8,128)(2,1)} custom-call(bf16[512,256]{1,0:T(8,128)(2,1)S(1)} %bitcast.7, bf16[66,32]{1,0:T(8,128)(2,1)S(1)} %copy-done.9, bf16[256,256]{1,0:T(8,128)(2,1)S(1)} %copy-done.6, bf16[256,256]{1,0:T(8,128)(2,1)S(1)} %copy-done.5, bf16[256,528]{1,0:T(8,128)(2,1)S(1)} %copy-done.4, f32[33,256]{1,0:T(8,128)S(1)} %copy-done.8, ...), custom_call_target="tpu_custom_call" | custom-call | flops 800000000 | bytes 3000000 | tf_op jit(solution)/shard_map/pallas_call | solution.py:249
  30.4 9.5 %all-to-all-start.1 = ((bf16[32,8,256]{2,1,0:T(8,128)(2,1)}), bf16[32,8,256]{2,1,0:T(8,128)(2,1)S(1)}, u32[]{:S(2)}, u32[]{:S(2)}) async-start(bf16[32,8,256]{2,1,0:T(8,128)(2,1)} %bitcast.3), calls=%async_computation.1 | async-start | bytes 262144 | tf_op jit(solution)/shard_map/all_to_all | solution.py:352
  39.9 0.0 copy-done.13
  40.0 0.1 copy.13.gain_ref
  40.1 0.0 collective-permute-done.refs_3_
  40.1 0.0 copy-start.10
  40.1 0.0 collective-permute-done.1.refs_4_
  40.1 0.0 copy-start.11
  40.2 8.8 %collective-permute-done.2.refs_5_ = bf16[256,1024]{1,0:T(8,128)(2,1)S(1)} collective-permute-done((bf16[256,1024]{1,0:T(8,128)(2,1)}, bf16[256,1024]{1,0:T(8,128)(2,1)S(1)}, u32[]{:S(2)}, u32[]{:S(2)}) %collective-permute-start.2) | collective-permute-done | bytes 524320 | tf_op jit(solution)/shard_map/ppermute | solution.py:341
  49.0 0.1 all-to-all-done.1
  49.1 0.0 copy-done
  49.1 0.0 copy-done.1
  49.1 0.0 copy-done.2
  49.1 0.2 shard_map.121
  49.3 9.6 %all_gather.3.refs_1_ = bf16[1024,256]{1,0:T(8,128)(2,1)} all-gather(bf16[256,256]{1,0:T(8,128)(2,1)S(1)} %shard_map.121), channel_id=1, replica_groups=mesh['ctx'=32,'quad'=4,'pair'=2,'core'=2] {'pair','core'}, dimensions={0}, use_global_device_ids=true | all-gather | bytes 655360 | tf_op jit(solution)/shard_map/all_gather | solution.py:356
  58.9 0.0 copy-done.10
  58.9 0.0 copy-done.11
  58.9 0.0 copy-done.12
  58.9 4.3 %shard_map.122 = (bf16[256,256]{1,0:T(8,128)(2,1)}, bf16[256,256]{1,0:T(8,128)(2,1)}, bf16[256,256]{1,0:T(8,128)(2,1)}, bf16[256,256]{1,0:T(8,128)(2,1)}) custom-call(s32[1]{0:T(128)} %bitcast.refs_0_, bf16[1024,256]{1,0:T(8,128)(2,1)} %all_gather.3.refs_1_, bf16[256,4096]{1,0:T(8,128)(2,1)} %refs_2_.4, bf16[256,1024]{1,0:T(8,128)(2,1)} %copy-done.10, ...), custom_call_target="tpu_custom_call" | custom-call | flops 536870912 | bytes 3145728 | tf_op jit(solution)/shard_map/pallas_call | solution.py:136
  63.3 6.4 %collective-permute-start.3 = (bf16[256,256]{1,0:T(8,128)(2,1)}, bf16[256,256]{1,0:T(8,128)(2,1)S(1)}, u32[]{:S(2)}, u32[]{:S(2)}) collective-permute-start(bf16[256,256]{1,0:T(8,128)(2,1)} %get-tuple-element.17), channel_id=1, source_target_pairs={{0,10},{1,11},{2,8},{3,9},{4,14},{5,15},{6,12},{7,13},{8,2},{9,3},... | collective-permute-start | bytes 393224 | tf_op jit(solution)/shard_map/ppermute | solution.py:33
  69.7 2.3 %collective-permute-start.4 = (bf16[256,256]{1,0:T(8,128)(2,1)}, bf16[256,256]{1,0:T(8,128)(2,1)S(1)}, u32[]{:S(2)}, u32[]{:S(2)}) collective-permute-start(bf16[256,256]{1,0:T(8,128)(2,1)} %get-tuple-element.18), channel_id=1, source_target_pairs={{0,12},{1,13},{2,6},{3,7},{4,0},{5,1},{6,10},{7,11},{8,4},{9,5},{1... | collective-permute-start | bytes 393224 | tf_op jit(solution)/shard_map/ppermute | solution.py:33
  72.1 4.4 %collective-permute-start.5 = (bf16[256,256]{1,0:T(8,128)(2,1)}, bf16[256,256]{1,0:T(8,128)(2,1)S(1)}, u32[]{:S(2)}, u32[]{:S(2)}) collective-permute-start(bf16[256,256]{1,0:T(8,128)(2,1)} %get-tuple-element.19), channel_id=1, source_target_pairs={{0,14},{1,15},{2,4},{3,5},{4,2},{5,3},{6,8},{7,9},{8,6},{9,7},{10,... | collective-permute-start | bytes 393224 | tf_op jit(solution)/shard_map/ppermute | solution.py:33
  76.5 0.0 collective-permute-done.3.refs_0_
  76.5 3.3 %collective-permute-done.4.refs_1_ = bf16[256,256]{1,0:T(8,128)(2,1)S(1)} collective-permute-done((bf16[256,256]{1,0:T(8,128)(2,1)}, bf16[256,256]{1,0:T(8,128)(2,1)S(1)}, u32[]{:S(2)}, u32[]{:S(2)}) %collective-permute-start.4) | collective-permute-done | bytes 131104 | tf_op jit(solution)/shard_map/ppermute | solution.py:33
  79.8 2.4 %collective-permute-done.5.refs_2_ = bf16[256,256]{1,0:T(8,128)(2,1)S(1)} collective-permute-done((bf16[256,256]{1,0:T(8,128)(2,1)}, bf16[256,256]{1,0:T(8,128)(2,1)S(1)}, u32[]{:S(2)}, u32[]{:S(2)}) %collective-permute-start.5) | collective-permute-done | bytes 131104 | tf_op jit(solution)/shard_map/ppermute | solution.py:33
  82.2 0.9 %copy-done.3 = bf16[256,256]{1,0:T(8,128)(2,1)S(1)} copy-done((bf16[256,256]{1,0:T(8,128)(2,1)S(1)}, bf16[256,256]{1,0:T(8,128)(2,1)}, u32[]{:S(2)}) %copy-start.3) | copy-done | bytes 131096
  83.1 0.8 shard_map.123
  (8 shorter events, 0.0 us)
Async XLA Ops:
  0.0 27.2 %copy-start.7 = (f32[33,256]{1,0:T(8,128)S(1)}, f32[33,256]{1,0:T(8,128)}, u32[]{:S(2)}) copy-start(f32[33,256]{1,0:T(8,128)} %constant.32.clone.refs_6_) | copy-start | bytes 101380
  0.0 27.2 %copy-start.8 = (f32[33,256]{1,0:T(8,128)S(1)}, f32[33,256]{1,0:T(8,128)}, u32[]{:S(2)}) copy-start(f32[33,256]{1,0:T(8,128)} %constant.31.clone.refs_5_) | copy-start | bytes 101380
  0.0 27.2 %copy-start.4 = (bf16[256,528]{1,0:T(8,128)(2,1)S(1)}, bf16[256,528]{1,0:T(8,128)(2,1)}, u32[]{:S(2)}) copy-start(bf16[256,528]{1,0:T(8,128)(2,1)} %constant.30.clone.refs_4_) | copy-start | bytes 811012
  0.0 27.2 %copy-start.5 = (bf16[256,256]{1,0:T(8,128)(2,1)S(1)}, bf16[256,256]{1,0:T(8,128)(2,1)}, u32[]{:S(2)}) copy-start(bf16[256,256]{1,0:T(8,128)(2,1)} %constant.29.clone.refs_3_) | copy-start | bytes 393220
  0.0 27.2 %copy-start.6 = (bf16[256,256]{1,0:T(8,128)(2,1)S(1)}, bf16[256,256]{1,0:T(8,128)(2,1)}, u32[]{:S(2)}) copy-start(bf16[256,256]{1,0:T(8,128)(2,1)} %constant.28.clone.refs_2_) | copy-start | bytes 393220
  0.0 27.2 %copy-start.9 = (bf16[66,32]{1,0:T(8,128)(2,1)S(1)}, bf16[66,32]{1,0:T(8,128)(2,1)}, u32[]{:S(2)}) copy-start(bf16[66,32]{1,0:T(8,128)(2,1)} %constant.27.clone.refs_1_) | copy-start | bytes 12676
  2.0 25.2 %all-to-all-start = ((bf16[32,16,256]{2,1,0:T(8,128)(2,1)}), bf16[32,16,256]{2,1,0:T(8,128)(2,1)S(1)}, u32[]{:S(2)}, u32[]{:S(2)}) async-start(bf16[32,16,256]{2,1,0:T(8,128)(2,1)} %bitcast.8), calls=%async_computation | async-start | bytes 524288 | tf_op jit(solution)/shard_map/all_to_all | solution.py:335
  18.6 21.3 %copy-start.13 = (f32[256]{0:T(256)S(1)}, f32[256]{0:T(256)}, u32[]{:S(2)}) copy-start(f32[256]{0:T(256)} %param.16) | copy-start | bytes 3076
  18.6 30.5 %copy-start = (bf16[256,256]{1,0:T(8,128)(2,1)S(1)}, bf16[256,256]{1,0:T(8,128)(2,1)}, u32[]{:S(2)}) copy-start(bf16[256,256]{1,0:T(8,128)(2,1)} %signal_ref.1) | copy-start | bytes 393220
  18.7 30.4 %copy-start.1 = (bf16[256,256]{1,0:T(8,128)(2,1)S(1)}, bf16[256,256]{1,0:T(8,128)(2,1)}, u32[]{:S(2)}) copy-start(bf16[256,256]{1,0:T(8,128)(2,1)} %pre_ref.1) | copy-start | bytes 393220
  18.7 30.4 %copy-start.2 = (bf16[256,256]{1,0:T(8,128)(2,1)S(1)}, bf16[256,256]{1,0:T(8,128)(2,1)}, u32[]{:S(2)}) copy-start(bf16[256,256]{1,0:T(8,128)(2,1)} %post_ref.1) | copy-start | bytes 393220
  18.7 21.4 %collective-permute-start = (bf16[256,1024]{1,0:T(8,128)(2,1)}, bf16[256,1024]{1,0:T(8,128)(2,1)S(1)}, u32[]{:S(2)}, u32[]{:S(2)}) collective-permute-start(bf16[256,1024]{1,0:T(8,128)(2,1)} %get-tuple-element.14), channel_id=1, source_target_pairs={{0,1},{1,0},{2,3},{3,2},{4,5},{5,4},{6,7},{7,6},{8,9},{9,8},{10,11... | collective-permute-start | bytes 1572872 | tf_op jit(solution)/shard_map/ppermute | solution.py:341
  21.7 18.4 %collective-permute-start.1 = (bf16[256,1024]{1,0:T(8,128)(2,1)}, bf16[256,1024]{1,0:T(8,128)(2,1)S(1)}, u32[]{:S(2)}, u32[]{:S(2)}) collective-permute-start(bf16[256,1024]{1,0:T(8,128)(2,1)} %get-tuple-element.15), channel_id=1, source_target_pairs={{0,2},{1,3},{2,0},{3,1},{4,6},{5,7},{6,4},{7,5},{8,10},{9,11},{10,... | collective-permute-start | bytes 1572872 | tf_op jit(solution)/shard_map/ppermute | solution.py:341
  24.9 24.1 %collective-permute-start.2 = (bf16[256,1024]{1,0:T(8,128)(2,1)}, bf16[256,1024]{1,0:T(8,128)(2,1)S(1)}, u32[]{:S(2)}, u32[]{:S(2)}) collective-permute-start(bf16[256,1024]{1,0:T(8,128)(2,1)} %get-tuple-element.16), channel_id=1, source_target_pairs={{0,3},{1,2},{2,1},{3,0},{4,7},{5,6},{6,5},{7,4},{8,11},{9,10},{10,... | collective-permute-start | bytes 1572872 | tf_op jit(solution)/shard_map/ppermute | solution.py:341
  30.4 18.7 %all-to-all-start.1 = ((bf16[32,8,256]{2,1,0:T(8,128)(2,1)}), bf16[32,8,256]{2,1,0:T(8,128)(2,1)S(1)}, u32[]{:S(2)}, u32[]{:S(2)}) async-start(bf16[32,8,256]{2,1,0:T(8,128)(2,1)} %bitcast.3), calls=%async_computation.1 | async-start | bytes 262144 | tf_op jit(solution)/shard_map/all_to_all | solution.py:352
  40.1 18.8 %copy-start.10 = (bf16[256,1024]{1,0:T(8,128)(2,1)}, bf16[256,1024]{1,0:T(8,128)(2,1)S(1)}, u32[]{:S(2)}) copy-start(bf16[256,1024]{1,0:T(8,128)(2,1)S(1)} %collective-permute-done.refs_3_) | copy-start | bytes 1572868
  40.1 18.8 %copy-start.11 = (bf16[256,1024]{1,0:T(8,128)(2,1)}, bf16[256,1024]{1,0:T(8,128)(2,1)S(1)}, u32[]{:S(2)}) copy-start(bf16[256,1024]{1,0:T(8,128)(2,1)S(1)} %collective-permute-done.1.refs_4_) | copy-start | bytes 1572868
  49.0 10.0 %copy-start.12 = (bf16[256,1024]{1,0:T(8,128)(2,1)}, bf16[256,1024]{1,0:T(8,128)(2,1)S(1)}, u32[]{:S(2)}) copy-start(bf16[256,1024]{1,0:T(8,128)(2,1)S(1)} %collective-permute-done.2.refs_5_) | copy-start | bytes 1572868
  63.3 13.2 %collective-permute-start.3 = (bf16[256,256]{1,0:T(8,128)(2,1)}, bf16[256,256]{1,0:T(8,128)(2,1)S(1)}, u32[]{:S(2)}, u32[]{:S(2)}) collective-permute-start(bf16[256,256]{1,0:T(8,128)(2,1)} %get-tuple-element.17), channel_id=1, source_target_pairs={{0,10},{1,11},{2,8},{3,9},{4,14},{5,15},{6,12},{7,13},{8,2},{9,3},... | collective-permute-start | bytes 393224 | tf_op jit(solution)/shard_map/ppermute | solution.py:33
  69.7 10.1 %collective-permute-start.4 = (bf16[256,256]{1,0:T(8,128)(2,1)}, bf16[256,256]{1,0:T(8,128)(2,1)S(1)}, u32[]{:S(2)}, u32[]{:S(2)}) collective-permute-start(bf16[256,256]{1,0:T(8,128)(2,1)} %get-tuple-element.18), channel_id=1, source_target_pairs={{0,12},{1,13},{2,6},{3,7},{4,0},{5,1},{6,10},{7,11},{8,4},{9,5},{1... | collective-permute-start | bytes 393224 | tf_op jit(solution)/shard_map/ppermute | solution.py:33
  72.1 10.1 %collective-permute-start.5 = (bf16[256,256]{1,0:T(8,128)(2,1)}, bf16[256,256]{1,0:T(8,128)(2,1)S(1)}, u32[]{:S(2)}, u32[]{:S(2)}) collective-permute-start(bf16[256,256]{1,0:T(8,128)(2,1)} %get-tuple-element.19), channel_id=1, source_target_pairs={{0,14},{1,15},{2,4},{3,5},{4,2},{5,3},{6,8},{7,9},{8,6},{9,7},{10,... | collective-permute-start | bytes 393224 | tf_op jit(solution)/shard_map/ppermute | solution.py:33
  82.2 0.9 %copy-start.3 = (bf16[256,256]{1,0:T(8,128)(2,1)S(1)}, bf16[256,256]{1,0:T(8,128)(2,1)}, u32[]{:S(2)}) copy-start(bf16[256,256]{1,0:T(8,128)(2,1)} %get-tuple-element.20.refs_3_) | copy-start | bytes 393220

commit v7 on v4

--- a/solution.py
+++ b/solution.py
@@ -34,30 +34,39 @@
 
 
 def arrange_kernel(group, quads, width, members, place_ref, weight_ref, *refs):
-    out_refs, done_ref, sems = refs[: len(members)], refs[-2], refs[-1]
+    count = len(members) * group
+    out_refs, done_ref, blocks, in_sems, out_sems = refs[: len(members)], *refs[-4:]
     tp = place_ref[0]
     quad, place = tp // group, lax.rem(tp, group)
-    copies = []
+    loads, stores = [], []
     for n, r in enumerate(members):
         other = place ^ r
         for i, target in enumerate(targets_of(quad, other // 2, lax.rem(other, 2), quads)):
+            k = n * group + i
             start = pl.multiple_of(target * width, width)
-            copies.append(
+            loads.append(
                 pltpu.make_async_copy(
-                    weight_ref.at[:, pl.ds(start, width)],
-                    out_refs[n].at[:, pl.ds(i * width, width)],
-                    sems.at[n * group + i],
+                    weight_ref.at[:, pl.ds(start, width)], blocks.at[k], in_sems.at[k]
                 )
             )
-    for copy in copies:
-        copy.start()
-    for copy in copies:
-        copy.wait()
+            stores.append(
+                pltpu.make_async_copy(
+                    blocks.at[k], out_refs[n].at[:, pl.ds(i * width, width)], out_sems.at[k]
+                )
+            )
+    for load in loads:
+        load.start()
+    for k in range(count):
+        loads[k].wait()
+        stores[k].start()
+    for store in stores:
+        store.wait()
     done_ref[0] = tp
 
 
 def arrange(out_weight, place, group, quads, width, members):
     rows = out_weight.shape[0]
+    count = len(members) * group
     piece = jax.ShapeDtypeStruct((rows, group * width), out_weight.dtype)
     *pieces, done = pl.pallas_call(
         lambda *refs: arrange_kernel(group, quads, width, members, *refs),
@@ -68,15 +77,54 @@
         ],
         out_specs=[pl.BlockSpec(memory_space=pltpu.HBM)] * len(members)
         + [pl.BlockSpec(memory_space=pltpu.SMEM)],
-        scratch_shapes=[pltpu.SemaphoreType.DMA((len(members) * group,))],
+        scratch_shapes=[
+            pltpu.VMEM((count, rows, width), out_weight.dtype),
+            pltpu.SemaphoreType.DMA((count,)),
+            pltpu.SemaphoreType.DMA((count,)),
+        ],
         compiler_params=pltpu.CompilerParams(vmem_limit_bytes=60 * MIB),
         cost_estimate=pl.CostEstimate(
-            flops=0,
-            bytes_accessed=4 * rows * len(members) * group * width,
-            transcendentals=0,
+            flops=0, bytes_accessed=4 * rows * count * width, transcendentals=0
         ),
     )(place, out_weight)
     return pieces, done
+
+
+def own_columns_kernel(group, quads, width, place_ref, weight_ref, out_ref, sems):
+    tp = place_ref[0]
+    quad, place = tp // group, lax.rem(tp, group)
+    copies = []
+    for i, target in enumerate(targets_of(quad, place // 2, lax.rem(place, 2), quads)):
+        start = pl.multiple_of(target * width, width)
+        copies.append(
+            pltpu.make_async_copy(
+                weight_ref.at[:, pl.ds(start, width)],
+                out_ref.at[:, pl.ds(i * width, width)],
+                sems.at[i],
+            )
+        )
+    for copy in copies:
+        copy.start()
+    for copy in copies:
+        copy.wait()
+
+
+def own_columns(out_weight, place, group, quads, width):
+    rows = out_weight.shape[0]
+    return pl.pallas_call(
+        lambda *refs: own_columns_kernel(group, quads, width, *refs),
+        out_shape=jax.ShapeDtypeStruct((rows, group * width), out_weight.dtype),
+        in_specs=[
+            pl.BlockSpec(memory_space=pltpu.SMEM),
+            pl.BlockSpec(memory_space=pltpu.HBM),
+        ],
+        out_specs=pl.BlockSpec(memory_space=pltpu.VMEM),
+        scratch_shapes=[pltpu.SemaphoreType.DMA((group,))],
+        compiler_params=pltpu.CompilerParams(vmem_limit_bytes=60 * MIB),
+        cost_estimate=pl.CostEstimate(
+            flops=0, bytes_accessed=4 * rows * group * width, transcendentals=0
+        ),
+    )(place, out_weight)
 
 
 def project_kernel(group, place_ref, mixed_ref, *refs):
@@ -296,8 +344,14 @@
     blocks = lax.all_to_all(send, "ctx", split_axis=0, concat_axis=0, tiled=True)
 
     place = lax.axis_index(TP_AXES).astype(jnp.int32).reshape(1)
-    crossing = [r for r in range(group) if r >= 2]
-    pieces, arranged = arrange(out_weight, place, group, quads, width, crossing)
+    members = [2, 3, 1]
+    pieces, arranged = arrange(out_weight, place, group, quads, width, members)
+    pieces = {
+        r: lax.ppermute(piece, GROUP, [(t, t ^ r) for t in range(group)])
+        for r, piece in zip(members, pieces)
+    }
+    pieces = [pieces[r] for r in range(1, group)]
+    own = own_columns(out_weight, place, group, quads, width)
     tables = dft_tables(devices, tokens_here, channels)
     convolved = convolve(blocks, channels, tables, arranged)
     inner, _ = arrange(out_weight, place, group, quads, width, [0, 1])
@@ -308,9 +362,9 @@
     convolved = lax.all_to_all(convolved, "ctx", split_axis=0, concat_axis=0, tiled=True).reshape(
         channels_here, tokens_here
     )
-    mixed = gate(post_gate, signal, pre_gate, convolved, skip_gain, weights[2:])
+    mixed = gate(post_gate, signal, pre_gate, convolved, skip_gain, pieces)
     gathered = lax.all_gather(mixed, GROUP, axis=0, tiled=True)
-    shares = project(place, gathered, weights, width)
+    shares = project(place, gathered, [own] + pieces, width)
     return finish([send_to_target(shares[step], step, quads) for step in range(3)] + [shares[3]])
 
 

time: 143 us -> 80.3 us (0.56)
  Pallas kernels: 73.7 us -> 11.7 us
  waiting for transfers between devices: 14.5 us -> 12.5 us
    pallas_call x2 -> x1, Pallas kernels: 67 us -> 2.93 us  [arrange(): pl.pallas_call(lambda *refs: arrange_kernel(group, quads, width, members,...]
    all_to_all x1, waiting for transfers between devices: 8.96 us -> 0.33 us  [per_device(): lax.all_to_all(convolved, 'ctx', split_axis=0, concat_axis=0, tiled=True)]
    ppermute x3, waiting for transfers between devices: 0.01 us -> 6.64 us  [per_device(): lax.ppermute(piece, GROUP, [(t, t ^ r) for t in range(group)])]
    pallas_call x0 -> x1, Pallas kernels: none -> 1.97 us  [own_columns(): pl.pallas_call(lambda *refs: own_columns_kernel(group, quads, width, *ref...]
  transfers between devices with their start and end apart: 8 -> 8, of which waited for: 3 -> 4; matrix products, arithmetic and copies ran while one was open for 0% -> 0% of each run, Pallas kernels for 49% -> 10%
where the time goes in v7:
time: 80.3 us; the launch traced here: 79.8 us
  starting transfers between devices  44.9 us (56%)
  waiting for transfers between devices  12.5 us (16%)
  Pallas kernels  11.7 us (15%)
  blocking collectives  9.2 us (11%)
  local copies, waits for them, and re-layouts  1.23 us (2%)
    all_to_all x1, starting transfers between devices, per_device(): lax.all_to_all(send, 'ctx', split_axis=0, concat_axis=0, tiled=True)  13.7 us
    ppermute x3, starting transfers between devices, send_to_target(): return lax.ppermute(share, TP_AXES, pairs)  13.2 us
    all_to_all x1, starting transfers between devices, per_device(): lax.all_to_all(convolved, 'ctx', split_axis=0, concat_axis=0, tiled=True)  9.65 us
    all_gather x1, blocking collectives, per_device(): gathered = lax.all_gather(mixed, GROUP, axis=0, tiled=True)  9.2 us
    ppermute x3, starting transfers between devices, per_device(): lax.ppermute(piece, GROUP, [(t, t ^ r) for t in range(group)])  8.32 us
    ppermute x3, waiting for transfers between devices, per_device(): lax.ppermute(piece, GROUP, [(t, t ^ r) for t in range(group)])  6.64 us
    ppermute x3, waiting for transfers between devices, send_to_target(): return lax.ppermute(share, TP_AXES, pairs)  5.48 us
    pallas_call x1, Pallas kernels, convolve(): pl.pallas_call(lambda *refs: convolve_kernel(channels, *refs), out_shape=...  3.26 us
  transfers between devices with their start and end apart: 8, of which 4 were waited for; matrix products, arithmetic and copies ran while one was open for 0% of the time, Pallas kernels for 10%

profile of v7, /device:TPU:1, one launch (start us, length us, event | category | flops | bytes accessed | tf_op | source)
XLA Modules:
  0.0 79.8 jit_solution(6765828531648901294)
XLA Ops:
  0.0 0.0 copy-start.7
  0.0 0.0 copy-start.8
  0.0 0.0 copy-start.4
  0.0 0.0 copy-start.5
  0.0 0.0 copy-start.6
  0.0 0.0 copy-start.9
  0.0 1.9 %shard_map.118 = bf16[512,256]{1,0:T(8,128)(2,1)} custom-call(bf16[256,256]{1,0:T(8,128)(2,1)} %signal_ref.1, bf16[256,256]{1,0:T(8,128)(2,1)} %pre_ref.1, f32[256,256]{1,0:T(8,128)} %refs_2_.2), custom_call_target="tpu_custom_call" | custom-call | tf_op jit(solution)/shard_map/pallas_call | solution.py:297
  2.0 13.7 %all-to-all-start = ((bf16[32,16,256]{2,1,0:T(8,128)(2,1)}), bf16[32,16,256]{2,1,0:T(8,128)(2,1)S(1)}, u32[]{:S(2)}, u32[]{:S(2)}) async-start(bf16[32,16,256]{2,1,0:T(8,128)(2,1)} %bitcast.8), calls=%async_computation | async-start | bytes 524288 | tf_op jit(solution)/shard_map/all_to_all | solution.py:344
  15.7 2.9 %shard_map.119 = (bf16[256,1024]{1,0:T(8,128)(2,1)}, bf16[256,1024]{1,0:T(8,128)(2,1)}, bf16[256,1024]{1,0:T(8,128)(2,1)}, s32[1]{0:T(128)}) custom-call(s32[1]{0:T(128)} %bitcast.refs_0_, bf16[256,4096]{1,0:T(8,128)(2,1)} %refs_1_.6), custom_call_target="tpu_custom_call" | custom-call | bytes 3145728 | tf_op jit(solution)/shard_map/pallas_call | solution.py:71
  18.6 2.9 %collective-permute-start = (bf16[256,1024]{1,0:T(8,128)(2,1)}, bf16[256,1024]{1,0:T(8,128)(2,1)S(1)}, u32[]{:S(2)}, u32[]{:S(2)}) collective-permute-start(bf16[256,1024]{1,0:T(8,128)(2,1)} %get-tuple-element.14), channel_id=1, source_target_pairs={{0,1},{1,0},{2,3},{3,2},{4,5},{5,4},{6,7},{7,6},{8,9},{9,8},{10,11... | collective-permute-start | bytes 1572872 | tf_op jit(solution)/shard_map/ppermute | solution.py:350
  21.5 3.2 %collective-permute-start.1 = (bf16[256,1024]{1,0:T(8,128)(2,1)}, bf16[256,1024]{1,0:T(8,128)(2,1)S(1)}, u32[]{:S(2)}, u32[]{:S(2)}) collective-permute-start(bf16[256,1024]{1,0:T(8,128)(2,1)} %get-tuple-element.15), channel_id=1, source_target_pairs={{0,2},{1,3},{2,0},{3,1},{4,6},{5,7},{6,4},{7,5},{8,10},{9,11},{10,... | collective-permute-start | bytes 1572872 | tf_op jit(solution)/shard_map/ppermute | solution.py:350
  24.7 2.3 %collective-permute-start.2 = (bf16[256,1024]{1,0:T(8,128)(2,1)}, bf16[256,1024]{1,0:T(8,128)(2,1)S(1)}, u32[]{:S(2)}, u32[]{:S(2)}) collective-permute-start(bf16[256,1024]{1,0:T(8,128)(2,1)} %get-tuple-element.16), channel_id=1, source_target_pairs={{0,3},{1,2},{2,1},{3,0},{4,7},{5,6},{6,5},{7,4},{8,11},{9,10},{10,... | collective-permute-start | bytes 1572872 | tf_op jit(solution)/shard_map/ppermute | solution.py:350
  27.0 0.0 all-to-all-done
  27.0 0.0 copy-done.7
  27.0 0.0 copy-done.8
  27.0 0.0 copy-done.4
  27.0 0.0 copy-done.5
  27.0 0.0 copy-done.6
  27.1 0.0 copy-done.9
  27.1 3.3 %shard_map.120 = bf16[256,256]{1,0:T(8,128)(2,1)} custom-call(bf16[512,256]{1,0:T(8,128)(2,1)S(1)} %bitcast.7, bf16[66,32]{1,0:T(8,128)(2,1)S(1)} %copy-done.9, bf16[256,256]{1,0:T(8,128)(2,1)S(1)} %copy-done.6, bf16[256,256]{1,0:T(8,128)(2,1)S(1)} %copy-done.5, bf16[256,528]{1,0:T(8,128)(2,1)S(1)} %copy-done.4, f32[33,256]{1,0:T(8,128)S(1)} %copy-done.8, ...), custom_call_target="tpu_custom_call" | custom-call | flops 800000000 | bytes 3000000 | tf_op jit(solution)/shard_map/pallas_call | solution.py:258
  30.3 0.0 copy-start.10
  30.3 0.0 copy-start.1
  30.3 0.0 copy-start.2
  30.3 0.0 copy-start.3
  30.3 9.6 %all-to-all-start.1 = ((bf16[32,8,256]{2,1,0:T(8,128)(2,1)}), bf16[32,8,256]{2,1,0:T(8,128)(2,1)S(1)}, u32[]{:S(2)}, u32[]{:S(2)}) async-start(bf16[32,8,256]{2,1,0:T(8,128)(2,1)} %bitcast.3), calls=%async_computation.1 | async-start | bytes 262144 | tf_op jit(solution)/shard_map/all_to_all | solution.py:362
  40.0 2.0 %shard_map.122.refs_2_ = bf16[256,1024]{1,0:T(8,128)(2,1)} custom-call(s32[1]{0:T(128)} %bitcast.refs_0_, bf16[256,4096]{1,0:T(8,128)(2,1)} %refs_1_.6), custom_call_target="tpu_custom_call" | custom-call | bytes 1048576 | tf_op jit(solution)/shard_map/pallas_call | solution.py:114
  42.0 0.0 copy-done.10
  42.0 0.1 copy.13.gain_ref
  42.1 0.0 collective-permute-done.refs_3_
  42.1 0.0 collective-permute-done.1.refs_4_
  42.2 6.6 %collective-permute-done.2.refs_5_ = bf16[256,1024]{1,0:T(8,128)(2,1)S(1)} collective-permute-done((bf16[256,1024]{1,0:T(8,128)(2,1)}, bf16[256,1024]{1,0:T(8,128)(2,1)S(1)}, u32[]{:S(2)}, u32[]{:S(2)}) %collective-permute-start.2) | collective-permute-done | bytes 524320 | tf_op jit(solution)/shard_map/ppermute | solution.py:350
  48.8 0.3 all-to-all-done.1
  49.1 0.0 copy-done.1
  49.1 0.0 copy-done.2
  49.1 0.0 copy-done.3
  49.1 0.2 shard_map.121
  49.3 9.2 %all_gather.3.refs_1_ = bf16[1024,256]{1,0:T(8,128)(2,1)S(1)} all-gather(bf16[256,256]{1,0:T(8,128)(2,1)S(1)} %shard_map.121), channel_id=1, replica_groups=mesh['ctx'=32,'quad'=4,'pair'=2,'core'=2] {'pair','core'}, dimensions={0}, use_global_device_ids=true | all-gather | bytes 655360 | tf_op jit(solution)/shard_map/all_gather | solution.py:366
  58.5 0.0 copy-start
  58.5 1.0 %copy-done = bf16[256,1024]{1,0:T(8,128)(2,1)S(1)} copy-done((bf16[256,1024]{1,0:T(8,128)(2,1)S(1)}, bf16[256,1024]{1,0:T(8,128)(2,1)}, u32[]{:S(2)}) %copy-start) | copy-done | bytes 524312
  59.6 0.7 shard_map.123
  60.3 6.4 %collective-permute-start.3 = (bf16[256,256]{1,0:T(8,128)(2,1)S(1)}, bf16[256,256]{1,0:T(8,128)(2,1)S(1)}, u32[]{:S(2)}, u32[]{:S(2)}) collective-permute-start(bf16[256,256]{1,0:T(8,128)(2,1)S(1)} %get-tuple-element.17), channel_id=1, source_target_pairs={{0,10},{1,11},{2,8},{3,9},{4,14},{5,15},{6,12},{7,13},{8,2},{9,3},... | collective-permute-start | bytes 393224 | tf_op jit(solution)/shard_map/ppermute | solution.py:33
  66.8 2.3 %collective-permute-start.4 = (bf16[256,256]{1,0:T(8,128)(2,1)S(1)}, bf16[256,256]{1,0:T(8,128)(2,1)S(1)}, u32[]{:S(2)}, u32[]{:S(2)}) collective-permute-start(bf16[256,256]{1,0:T(8,128)(2,1)S(1)} %get-tuple-element.18), channel_id=1, source_target_pairs={{0,12},{1,13},{2,6},{3,7},{4,0},{5,1},{6,10},{7,11},{8,4},{9,5},{1... | collective-permute-start | bytes 393224 | tf_op jit(solution)/shard_map/ppermute | solution.py:33
  69.1 4.4 %collective-permute-start.5 = (bf16[256,256]{1,0:T(8,128)(2,1)S(1)}, bf16[256,256]{1,0:T(8,128)(2,1)S(1)}, u32[]{:S(2)}, u32[]{:S(2)}) collective-permute-start(bf16[256,256]{1,0:T(8,128)(2,1)S(1)} %get-tuple-element.19), channel_id=1, source_target_pairs={{0,14},{1,15},{2,4},{3,5},{4,2},{5,3},{6,8},{7,9},{8,6},{9,7},{10,... | collective-permute-start | bytes 393224 | tf_op jit(solution)/shard_map/ppermute | solution.py:33
  73.5 0.0 collective-permute-done.3.refs_0_
  73.5 3.1 %collective-permute-done.4.refs_1_ = bf16[256,256]{1,0:T(8,128)(2,1)S(1)} collective-permute-done((bf16[256,256]{1,0:T(8,128)(2,1)S(1)}, bf16[256,256]{1,0:T(8,128)(2,1)S(1)}, u32[]{:S(2)}, u32[]{:S(2)}) %collective-permute-start.4) | collective-permute-done | bytes 131104 | tf_op jit(solution)/shard_map/ppermute | solution.py:33
  76.6 2.4 %collective-permute-done.5.refs_2_ = bf16[256,256]{1,0:T(8,128)(2,1)S(1)} collective-permute-done((bf16[256,256]{1,0:T(8,128)(2,1)S(1)}, bf16[256,256]{1,0:T(8,128)(2,1)S(1)}, u32[]{:S(2)}, u32[]{:S(2)}) %collective-permute-start.5) | collective-permute-done | bytes 131104 | tf_op jit(solution)/shard_map/ppermute | solution.py:33
  79.0 0.8 shard_map.124
  (4 shorter events, 0.0 us)
Async XLA Ops:
  0.0 27.0 %copy-start.7 = (f32[33,256]{1,0:T(8,128)S(1)}, f32[33,256]{1,0:T(8,128)}, u32[]{:S(2)}) copy-start(f32[33,256]{1,0:T(8,128)} %constant.32.clone.refs_6_) | copy-start | bytes 101380
  0.0 27.0 %copy-start.8 = (f32[33,256]{1,0:T(8,128)S(1)}, f32[33,256]{1,0:T(8,128)}, u32[]{:S(2)}) copy-start(f32[33,256]{1,0:T(8,128)} %constant.31.clone.refs_5_) | copy-start | bytes 101380
  0.0 27.0 %copy-start.4 = (bf16[256,528]{1,0:T(8,128)(2,1)S(1)}, bf16[256,528]{1,0:T(8,128)(2,1)}, u32[]{:S(2)}) copy-start(bf16[256,528]{1,0:T(8,128)(2,1)} %constant.30.clone.refs_4_) | copy-start | bytes 811012
  0.0 27.0 %copy-start.5 = (bf16[256,256]{1,0:T(8,128)(2,1)S(1)}, bf16[256,256]{1,0:T(8,128)(2,1)}, u32[]{:S(2)}) copy-start(bf16[256,256]{1,0:T(8,128)(2,1)} %constant.29.clone.refs_3_) | copy-start | bytes 393220
  0.0 27.0 %copy-start.6 = (bf16[256,256]{1,0:T(8,128)(2,1)S(1)}, bf16[256,256]{1,0:T(8,128)(2,1)}, u32[]{:S(2)}) copy-start(bf16[256,256]{1,0:T(8,128)(2,1)} %constant.28.clone.refs_2_) | copy-start | bytes 393220
  0.0 27.0 %copy-start.9 = (bf16[66,32]{1,0:T(8,128)(2,1)S(1)}, bf16[66,32]{1,0:T(8,128)(2,1)}, u32[]{:S(2)}) copy-start(bf16[66,32]{1,0:T(8,128)(2,1)} %constant.27.clone.refs_1_) | copy-start | bytes 12676
  2.0 25.0 %all-to-all-start = ((bf16[32,16,256]{2,1,0:T(8,128)(2,1)}), bf16[32,16,256]{2,1,0:T(8,128)(2,1)S(1)}, u32[]{:S(2)}, u32[]{:S(2)}) async-start(bf16[32,16,256]{2,1,0:T(8,128)(2,1)} %bitcast.8), calls=%async_computation | async-start | bytes 524288 | tf_op jit(solution)/shard_map/all_to_all | solution.py:344
  18.6 23.5 %collective-permute-start = (bf16[256,1024]{1,0:T(8,128)(2,1)}, bf16[256,1024]{1,0:T(8,128)(2,1)S(1)}, u32[]{:S(2)}, u32[]{:S(2)}) collective-permute-start(bf16[256,1024]{1,0:T(8,128)(2,1)} %get-tuple-element.14), channel_id=1, source_target_pairs={{0,1},{1,0},{2,3},{3,2},{4,5},{5,4},{6,7},{7,6},{8,9},{9,8},{10,11... | collective-permute-start | bytes 1572872 | tf_op jit(solution)/shard_map/ppermute | solution.py:350
  21.5 20.6 %collective-permute-start.1 = (bf16[256,1024]{1,0:T(8,128)(2,1)}, bf16[256,1024]{1,0:T(8,128)(2,1)S(1)}, u32[]{:S(2)}, u32[]{:S(2)}) collective-permute-start(bf16[256,1024]{1,0:T(8,128)(2,1)} %get-tuple-element.15), channel_id=1, source_target_pairs={{0,2},{1,3},{2,0},{3,1},{4,6},{5,7},{6,4},{7,5},{8,10},{9,11},{10,... | collective-permute-start | bytes 1572872 | tf_op jit(solution)/shard_map/ppermute | solution.py:350
  24.7 24.1 %collective-permute-start.2 = (bf16[256,1024]{1,0:T(8,128)(2,1)}, bf16[256,1024]{1,0:T(8,128)(2,1)S(1)}, u32[]{:S(2)}, u32[]{:S(2)}) collective-permute-start(bf16[256,1024]{1,0:T(8,128)(2,1)} %get-tuple-element.16), channel_id=1, source_target_pairs={{0,3},{1,2},{2,1},{3,0},{4,7},{5,6},{6,5},{7,4},{8,11},{9,10},{10,... | collective-permute-start | bytes 1572872 | tf_op jit(solution)/shard_map/ppermute | solution.py:350
  30.3 11.6 %copy-start.10 = (f32[256]{0:T(256)S(1)}, f32[256]{0:T(256)}, u32[]{:S(2)}) copy-start(f32[256]{0:T(256)} %param.16) | copy-start | bytes 3076
  30.3 18.8 %copy-start.1 = (bf16[256,256]{1,0:T(8,128)(2,1)S(1)}, bf16[256,256]{1,0:T(8,128)(2,1)}, u32[]{:S(2)}) copy-start(bf16[256,256]{1,0:T(8,128)(2,1)} %signal_ref.1) | copy-start | bytes 393220
  30.3 18.8 %copy-start.2 = (bf16[256,256]{1,0:T(8,128)(2,1)S(1)}, bf16[256,256]{1,0:T(8,128)(2,1)}, u32[]{:S(2)}) copy-start(bf16[256,256]{1,0:T(8,128)(2,1)} %pre_ref.1) | copy-start | bytes 393220
  30.3 18.8 %copy-start.3 = (bf16[256,256]{1,0:T(8,128)(2,1)S(1)}, bf16[256,256]{1,0:T(8,128)(2,1)}, u32[]{:S(2)}) copy-start(bf16[256,256]{1,0:T(8,128)(2,1)} %post_ref.1) | copy-start | bytes 393220
  30.3 18.8 %all-to-all-start.1 = ((bf16[32,8,256]{2,1,0:T(8,128)(2,1)}), bf16[32,8,256]{2,1,0:T(8,128)(2,1)S(1)}, u32[]{:S(2)}, u32[]{:S(2)}) async-start(bf16[32,8,256]{2,1,0:T(8,128)(2,1)} %bitcast.3), calls=%async_computation.1 | async-start | bytes 262144 | tf_op jit(solution)/shard_map/all_to_all | solution.py:362
  58.5 1.0 %copy-start = (bf16[256,1024]{1,0:T(8,128)(2,1)S(1)}, bf16[256,1024]{1,0:T(8,128)(2,1)}, u32[]{:S(2)}) copy-start(bf16[256,1024]{1,0:T(8,128)(2,1)} %shard_map.122.refs_2_) | copy-start | bytes 1572868
  60.3 13.2 %collective-permute-start.3 = (bf16[256,256]{1,0:T(8,128)(2,1)S(1)}, bf16[256,256]{1,0:T(8,128)(2,1)S(1)}, u32[]{:S(2)}, u32[]{:S(2)}) collective-permute-start(bf16[256,256]{1,0:T(8,128)(2,1)S(1)} %get-tuple-element.17), channel_id=1, source_target_pairs={{0,10},{1,11},{2,8},{3,9},{4,14},{5,15},{6,12},{7,13},{8,2},{9,3},... | collective-permute-start | bytes 393224 | tf_op jit(solution)/shard_map/ppermute | solution.py:33
  66.8 9.9 %collective-permute-start.4 = (bf16[256,256]{1,0:T(8,128)(2,1)S(1)}, bf16[256,256]{1,0:T(8,128)(2,1)S(1)}, u32[]{:S(2)}, u32[]{:S(2)}) collective-permute-start(bf16[256,256]{1,0:T(8,128)(2,1)S(1)} %get-tuple-element.18), channel_id=1, source_target_pairs={{0,12},{1,13},{2,6},{3,7},{4,0},{5,1},{6,10},{7,11},{8,4},{9,5},{1... | collective-permute-start | bytes 393224 | tf_op jit(solution)/shard_map/ppermute | solution.py:33
  69.1 9.9 %collective-permute-start.5 = (bf16[256,256]{1,0:T(8,128)(2,1)S(1)}, bf16[256,256]{1,0:T(8,128)(2,1)S(1)}, u32[]{:S(2)}, u32[]{:S(2)}) collective-permute-start(bf16[256,256]{1,0:T(8,128)(2,1)S(1)} %get-tuple-element.19), channel_id=1, source_target_pairs={{0,14},{1,15},{2,4},{3,5},{4,2},{5,3},{6,8},{7,9},{8,6},{9,7},{10,... | collective-permute-start | bytes 393224 | tf_op jit(solution)/shard_map/ppermute | solution.py:33

commit v8 on v7

--- a/solution.py
+++ b/solution.py
@@ -10,6 +10,8 @@
 from jax.sharding import PartitionSpec as P
 
 TP_AXES = ("quad", "pair", "core")
+REMOTE = 3
+TARGETS = 5
 GROUP = ("pair", "core")
 MIB = 1 << 20
 
@@ -18,7 +20,7 @@
     onward = 2 * pair - 1
     far = lax.rem(quad + 2 * onward + quads, quads)
     near = lax.rem(quad + onward + quads, quads)
-    chips = [(far, 1 - pair), (near, pair), (near, 1 - pair), (quad, pair)]
+    chips = [(far, 1 - pair), (near, pair), (near, 1 - pair), (quad, 1 - pair), (quad, pair)]
     return [(q * 2 + p) * 2 + core for q, p in chips]
 
 
@@ -27,22 +29,22 @@
     for quad in range(quads):
         for pair in range(2):
             onward = 1 if pair == 1 else -1
-            q = (quad + (2 * onward if step == 0 else onward)) % quads
+            q = (quad + (2 * onward, onward, onward, 0)[step]) % quads
             p = pair if step == 1 else 1 - pair
             pairs += [((quad * 2 + pair) * 2 + c, (q * 2 + p) * 2 + c) for c in range(2)]
     return lax.ppermute(share, TP_AXES, pairs)
 
 
 def arrange_kernel(group, quads, width, members, place_ref, weight_ref, *refs):
-    count = len(members) * group
     out_refs, done_ref, blocks, in_sems, out_sems = refs[: len(members)], *refs[-4:]
     tp = place_ref[0]
     quad, place = tp // group, lax.rem(tp, group)
     loads, stores = [], []
     for n, r in enumerate(members):
         other = place ^ r
-        for i, target in enumerate(targets_of(quad, other // 2, lax.rem(other, 2), quads)):
-            k = n * group + i
+        targets = targets_of(quad, other // 2, lax.rem(other, 2), quads)
+        for i, target in enumerate(targets[: out_refs[n].shape[1] // width]):
+            k = len(loads)
             start = pl.multiple_of(target * width, width)
             loads.append(
                 pltpu.make_async_copy(
@@ -56,9 +58,9 @@
             )
     for load in loads:
         load.start()
-    for k in range(count):
-        loads[k].wait()
-        stores[k].start()
+    for load, store in zip(loads, stores):
+        load.wait()
+        store.start()
     for store in stores:
         store.wait()
     done_ref[0] = tp
@@ -66,11 +68,11 @@
 
 def arrange(out_weight, place, group, quads, width, members):
     rows = out_weight.shape[0]
-    count = len(members) * group
-    piece = jax.ShapeDtypeStruct((rows, group * width), out_weight.dtype)
+    counts = [TARGETS if r < 2 else REMOTE for r in members]
     *pieces, done = pl.pallas_call(
         lambda *refs: arrange_kernel(group, quads, width, members, *refs),
-        out_shape=[piece] * len(members) + [jax.ShapeDtypeStruct((1,), jnp.int32)],
+        out_shape=[jax.ShapeDtypeStruct((rows, n * width), out_weight.dtype) for n in counts]
+        + [jax.ShapeDtypeStruct((1,), jnp.int32)],
         in_specs=[
             pl.BlockSpec(memory_space=pltpu.SMEM),
             pl.BlockSpec(memory_space=pltpu.HBM),
@@ -78,13 +80,13 @@
         out_specs=[pl.BlockSpec(memory_space=pltpu.HBM)] * len(members)
         + [pl.BlockSpec(memory_space=pltpu.SMEM)],
         scratch_shapes=[
-            pltpu.VMEM((count, rows, width), out_weight.dtype),
-            pltpu.SemaphoreType.DMA((count,)),
-            pltpu.SemaphoreType.DMA((count,)),
+            pltpu.VMEM((sum(counts), rows, width), out_weight.dtype),
+            pltpu.SemaphoreType.DMA((sum(counts),)),
+            pltpu.SemaphoreType.DMA((sum(counts),)),
         ],
         compiler_params=pltpu.CompilerParams(vmem_limit_bytes=60 * MIB),
         cost_estimate=pl.CostEstimate(
-            flops=0, bytes_accessed=4 * rows * count * width, transcendentals=0
+            flops=0, bytes_accessed=4 * rows * sum(counts) * width, transcendentals=0
         ),
     )(place, out_weight)
     return pieces, done
@@ -113,16 +115,16 @@
     rows = out_weight.shape[0]
     return pl.pallas_call(
         lambda *refs: own_columns_kernel(group, quads, width, *refs),
-        out_shape=jax.ShapeDtypeStruct((rows, group * width), out_weight.dtype),
+        out_shape=jax.ShapeDtypeStruct((rows, TARGETS * width), out_weight.dtype),
         in_specs=[
             pl.BlockSpec(memory_space=pltpu.SMEM),
             pl.BlockSpec(memory_space=pltpu.HBM),
         ],
         out_specs=pl.BlockSpec(memory_space=pltpu.VMEM),
-        scratch_shapes=[pltpu.SemaphoreType.DMA((group,))],
+        scratch_shapes=[pltpu.SemaphoreType.DMA((TARGETS,))],
         compiler_params=pltpu.CompilerParams(vmem_limit_bytes=60 * MIB),
         cost_estimate=pl.CostEstimate(
-            flops=0, bytes_accessed=4 * rows * group * width, transcendentals=0
+            flops=0, bytes_accessed=4 * rows * TARGETS * width, transcendentals=0
         ),
     )(place, out_weight)
 
@@ -136,9 +138,9 @@
         mixed_ref[pl.ds(pl.multiple_of((place ^ r) * tokens, tokens), tokens), :]
         for r in range(group)
     ]
-    for i in range(group):
+    for i in range(TARGETS):
         total = None
-        for r in range(group):
+        for r in range(group if i < REMOTE else 2):
             term = jnp.dot(
                 mixed[r],
                 weight_refs[r][:, i * width : (i + 1) * width],
@@ -153,14 +155,14 @@
     share = jax.ShapeDtypeStruct((mixed.shape[0] // group, width), mixed.dtype)
     return pl.pallas_call(
         lambda *refs: project_kernel(group, *refs),
-        out_shape=[share] * group,
+        out_shape=[share] * TARGETS,
         in_specs=[pl.BlockSpec(memory_space=pltpu.SMEM)]
         + [pl.BlockSpec(memory_space=pltpu.VMEM)] * (1 + group),
-        out_specs=[pl.BlockSpec(memory_space=pltpu.VMEM)] * group,
+        out_specs=[pl.BlockSpec(memory_space=pltpu.VMEM)] * TARGETS,
         compiler_params=pltpu.CompilerParams(vmem_limit_bytes=10 * MIB),
         cost_estimate=pl.CostEstimate(
-            flops=2 * mixed.size * group * width,
-            bytes_accessed=2 * (mixed.size + sum(w.size for w in weights) + group * share.size),
+            flops=2 * mixed.size * 4 * width,
+            bytes_accessed=2 * (mixed.size + sum(w.size for w in weights) + TARGETS * share.size),
             transcendentals=0,
         ),
     )(place, mixed, *weights)
@@ -362,10 +364,11 @@
     convolved = lax.all_to_all(convolved, "ctx", split_axis=0, concat_axis=0, tiled=True).reshape(
         channels_here, tokens_here
     )
-    mixed = gate(post_gate, signal, pre_gate, convolved, skip_gain, pieces)
+    mixed = gate(post_gate, signal, pre_gate, convolved, skip_gain, pieces[1:] + pieces[:1])
     gathered = lax.all_gather(mixed, GROUP, axis=0, tiled=True)
     shares = project(place, gathered, [own] + pieces, width)
-    return finish([send_to_target(shares[step], step, quads) for step in range(3)] + [shares[3]])
+    received = [send_to_target(shares[step], step, quads) for step in range(TARGETS - 1)]
+    return finish(received + [shares[-1]])
 
 
 def solution(mesh):

time: 80.3 us -> 80.6 us (level)
  waiting for transfers between devices: 12.5 us -> 10.6 us
  starting transfers between devices: 44.9 us -> 46.8 us
    ppermute x3, waiting for transfers between devices: 6.64 us -> 0.68 us  [per_device(): lax.ppermute(piece, GROUP, [(t, t ^ r) for t in range(group)])]
    all_to_all x1, waiting for transfers between devices: 0.33 us -> 6.18 us  [per_device(): lax.all_to_all(convolved, 'ctx', split_axis=0, concat_axis=0, tiled=True)]
    ppermute x3 -> x4, starting transfers between devices: 13.2 us -> 15.1 us  [send_to_target(): return lax.ppermute(share, TP_AXES, pairs)]
    ppermute x3 -> x4, waiting for transfers between devices: 5.48 us -> 3.77 us  [send_to_target(): return lax.ppermute(share, TP_AXES, pairs)]
  transfers between devices with their start and end apart: 8 -> 9, of which waited for: 4 -> 5; matrix products, arithmetic and copies ran while one was open for 0% -> 0% of each run, Pallas kernels for 10% -> 10%
where the time goes in v8:
time: 80.6 us; the launch traced here: 80 us
  starting transfers between devices  46.8 us (58%)
  Pallas kernels  11.8 us (15%)
  waiting for transfers between devices  10.6 us (13%)
  blocking collectives  9.2 us (11%)
  local copies, waits for them, and re-layouts  1.27 us (2%)
    ppermute x4, starting transfers between devices, send_to_target(): return lax.ppermute(share, TP_AXES, pairs)  15.1 us
    all_to_all x1, starting transfers between devices, per_device(): lax.all_to_all(send, 'ctx', split_axis=0, concat_axis=0, tiled=True)  13.7 us
    all_to_all x1, starting transfers between devices, per_device(): lax.all_to_all(convolved, 'ctx', split_axis=0, concat_axis=0, tiled=True)  9.65 us
    all_gather x1, blocking collectives, per_device(): gathered = lax.all_gather(mixed, GROUP, axis=0, tiled=True)  9.2 us
    ppermute x3, starting transfers between devices, per_device(): lax.ppermute(piece, GROUP, [(t, t ^ r) for t in range(group)])  8.32 us
    all_to_all x1, waiting for transfers between devices, per_device(): lax.all_to_all(convolved, 'ctx', split_axis=0, concat_axis=0, tiled=True)  6.18 us
    ppermute x4, waiting for transfers between devices, send_to_target(): return lax.ppermute(share, TP_AXES, pairs)  3.77 us
    pallas_call x1, Pallas kernels, convolve(): pl.pallas_call(lambda *refs: convolve_kernel(channels, *refs), out_shape=...  3.21 us
  transfers between devices with their start and end apart: 9, of which 5 were waited for; matrix products, arithmetic and copies ran while one was open for 0% of the time, Pallas kernels for 10%

profile of v8, /device:TPU:1, one launch (start us, length us, event | category | flops | bytes accessed | tf_op | source)
XLA Modules:
  0.0 80.0 jit_solution(17516826991613766423)
XLA Ops:
  0.0 0.0 copy-start.7
  0.0 0.0 copy-start.8
  0.0 0.0 copy-start.4
  0.0 0.0 copy-start.5
  0.0 0.0 copy-start.6
  0.0 0.0 copy-start.9
  0.0 1.9 %shard_map.118 = bf16[512,256]{1,0:T(8,128)(2,1)} custom-call(bf16[256,256]{1,0:T(8,128)(2,1)} %signal_ref.1, bf16[256,256]{1,0:T(8,128)(2,1)} %pre_ref.1, f32[256,256]{1,0:T(8,128)} %refs_2_.2), custom_call_target="tpu_custom_call" | custom-call | tf_op jit(solution)/shard_map/pallas_call | solution.py:299
  2.0 13.7 %all-to-all-start = ((bf16[32,16,256]{2,1,0:T(8,128)(2,1)}), bf16[32,16,256]{2,1,0:T(8,128)(2,1)S(1)}, u32[]{:S(2)}, u32[]{:S(2)}) async-start(bf16[32,16,256]{2,1,0:T(8,128)(2,1)} %bitcast.8), calls=%async_computation | async-start | bytes 524288 | tf_op jit(solution)/shard_map/all_to_all | solution.py:346
  15.7 2.9 %shard_map.119 = (bf16[256,768]{1,0:T(8,128)(2,1)}, bf16[256,768]{1,0:T(8,128)(2,1)}, bf16[256,1280]{1,0:T(8,128)(2,1)}, s32[1]{0:T(128)}) custom-call(s32[1]{0:T(128)} %bitcast.refs_0_, bf16[256,4096]{1,0:T(8,128)(2,1)} %refs_1_.6), custom_call_target="tpu_custom_call" | custom-call | bytes 2883584 | tf_op jit(solution)/shard_map/pallas_call | solution.py:72
  18.6 2.9 %collective-permute-start.2 = (bf16[256,1280]{1,0:T(8,128)(2,1)}, bf16[256,1280]{1,0:T(8,128)(2,1)S(1)}, u32[]{:S(2)}, u32[]{:S(2)}) collective-permute-start(bf16[256,1280]{1,0:T(8,128)(2,1)} %get-tuple-element.17), channel_id=1, source_target_pairs={{0,1},{1,0},{2,3},{3,2},{4,5},{5,4},{6,7},{7,6},{8,9},{9,8},{10,11... | collective-permute-start | bytes 1966088 | tf_op jit(solution)/shard_map/ppermute | solution.py:352
  21.5 3.2 %collective-permute-start = (bf16[256,768]{1,0:T(8,128)(2,1)}, bf16[256,768]{1,0:T(8,128)(2,1)S(1)}, u32[]{:S(2)}, u32[]{:S(2)}) collective-permute-start(bf16[256,768]{1,0:T(8,128)(2,1)} %get-tuple-element.15), channel_id=1, source_target_pairs={{0,2},{1,3},{2,0},{3,1},{4,6},{5,7},{6,4},{7,5},{8,10},{9,11},{10,... | collective-permute-start | bytes 1179656 | tf_op jit(solution)/shard_map/ppermute | solution.py:352
  24.7 2.3 %collective-permute-start.1 = (bf16[256,768]{1,0:T(8,128)(2,1)}, bf16[256,768]{1,0:T(8,128)(2,1)S(1)}, u32[]{:S(2)}, u32[]{:S(2)}) collective-permute-start(bf16[256,768]{1,0:T(8,128)(2,1)} %get-tuple-element.16), channel_id=1, source_target_pairs={{0,3},{1,2},{2,1},{3,0},{4,7},{5,6},{6,5},{7,4},{8,11},{9,10},{10,... | collective-permute-start | bytes 1179656 | tf_op jit(solution)/shard_map/ppermute | solution.py:352
  27.0 0.0 all-to-all-done
  27.0 0.0 copy-done.7
  27.0 0.0 copy-done.8
  27.0 0.0 copy-done.4
  27.0 0.0 copy-done.5
  27.0 0.0 copy-done.6
  27.0 0.0 copy-done.9
  27.0 3.2 %shard_map.120 = bf16[256,256]{1,0:T(8,128)(2,1)} custom-call(bf16[512,256]{1,0:T(8,128)(2,1)S(1)} %bitcast.7, bf16[66,32]{1,0:T(8,128)(2,1)S(1)} %copy-done.9, bf16[256,256]{1,0:T(8,128)(2,1)S(1)} %copy-done.6, bf16[256,256]{1,0:T(8,128)(2,1)S(1)} %copy-done.5, bf16[256,528]{1,0:T(8,128)(2,1)S(1)} %copy-done.4, f32[33,256]{1,0:T(8,128)S(1)} %copy-done.8, ...), custom_call_target="tpu_custom_call" | custom-call | flops 800000000 | bytes 3000000 | tf_op jit(solution)/shard_map/pallas_call | solution.py:260
  30.2 0.0 copy-start.1
  30.2 0.0 copy-start.2
  30.2 0.0 copy-start.3
  30.2 9.6 %all-to-all-start.1 = ((bf16[32,8,256]{2,1,0:T(8,128)(2,1)}), bf16[32,8,256]{2,1,0:T(8,128)(2,1)S(1)}, u32[]{:S(2)}, u32[]{:S(2)}) async-start(bf16[32,8,256]{2,1,0:T(8,128)(2,1)} %bitcast.3), calls=%async_computation.1 | async-start | bytes 262144 | tf_op jit(solution)/shard_map/all_to_all | solution.py:364
  39.9 2.1 %shard_map.122.refs_2_ = bf16[256,1280]{1,0:T(8,128)(2,1)} custom-call(s32[1]{0:T(128)} %bitcast.refs_0_, bf16[256,4096]{1,0:T(8,128)(2,1)} %refs_1_.6), custom_call_target="tpu_custom_call" | custom-call | bytes 1310720 | tf_op jit(solution)/shard_map/pallas_call | solution.py:116
  42.0 0.0 copy-done.10
  42.0 0.1 copy.13.gain_ref
  42.2 0.0 collective-permute-done.refs_4_
  42.2 0.7 collective-permute-done.1.refs_5_
  42.9 0.0 collective-permute-done.2.refs_3_
  42.9 6.2 %all-to-all-done.1 = bf16[32,8,256]{2,1,0:T(8,128)(2,1)S(1)} async-done(((bf16[32,8,256]{2,1,0:T(8,128)(2,1)}), bf16[32,8,256]{2,1,0:T(8,128)(2,1)S(1)}, u32[]{:S(2)}, u32[]{:S(2)}) %all-to-all-start.1) | async-done | bytes 131104 | tf_op jit(solution)/shard_map/all_to_all | solution.py:364
  49.1 0.0 copy-done.1
  49.1 0.0 copy-done.2
  49.1 0.0 copy-done.3
  49.1 0.2 shard_map.121
  49.3 9.2 %all_gather.3.refs_1_ = bf16[1024,256]{1,0:T(8,128)(2,1)S(1)} all-gather(bf16[256,256]{1,0:T(8,128)(2,1)S(1)} %shard_map.121), channel_id=1, replica_groups=mesh['ctx'=32,'quad'=4,'pair'=2,'core'=2] {'pair','core'}, dimensions={0}, use_global_device_ids=true | all-gather | bytes 655360 | tf_op jit(solution)/shard_map/all_gather | solution.py:368
  58.5 0.0 copy-start
  58.5 1.1 %copy-done = bf16[256,1280]{1,0:T(8,128)(2,1)S(1)} copy-done((bf16[256,1280]{1,0:T(8,128)(2,1)S(1)}, bf16[256,1280]{1,0:T(8,128)(2,1)}, u32[]{:S(2)}) %copy-start) | copy-done | bytes 655384
  59.5 0.7 shard_map.123
  60.3 6.4 %collective-permute-start.3 = (bf16[256,256]{1,0:T(8,128)(2,1)S(1)}, bf16[256,256]{1,0:T(8,128)(2,1)S(1)}, u32[]{:S(2)}, u32[]{:S(2)}) collective-permute-start(bf16[256,256]{1,0:T(8,128)(2,1)S(1)} %get-tuple-element.18), channel_id=1, source_target_pairs={{0,10},{1,11},{2,8},{3,9},{4,14},{5,15},{6,12},{7,13},{8,2},{9,3},... | collective-permute-start | bytes 393224 | tf_op jit(solution)/shard_map/ppermute | solution.py:35
  66.7 2.3 %collective-permute-start.4 = (bf16[256,256]{1,0:T(8,128)(2,1)S(1)}, bf16[256,256]{1,0:T(8,128)(2,1)S(1)}, u32[]{:S(2)}, u32[]{:S(2)}) collective-permute-start(bf16[256,256]{1,0:T(8,128)(2,1)S(1)} %get-tuple-element.19), channel_id=1, source_target_pairs={{0,12},{1,13},{2,6},{3,7},{4,0},{5,1},{6,10},{7,11},{8,4},{9,5},{1... | collective-permute-start | bytes 393224 | tf_op jit(solution)/shard_map/ppermute | solution.py:35
  69.1 4.4 %collective-permute-start.5 = (bf16[256,256]{1,0:T(8,128)(2,1)S(1)}, bf16[256,256]{1,0:T(8,128)(2,1)S(1)}, u32[]{:S(2)}, u32[]{:S(2)}) collective-permute-start(bf16[256,256]{1,0:T(8,128)(2,1)S(1)} %get-tuple-element.20), channel_id=1, source_target_pairs={{0,14},{1,15},{2,4},{3,5},{4,2},{5,3},{6,8},{7,9},{8,6},{9,7},{10,... | collective-permute-start | bytes 393224 | tf_op jit(solution)/shard_map/ppermute | solution.py:35
  73.5 1.9 %collective-permute-start.6 = (bf16[256,256]{1,0:T(8,128)(2,1)S(1)}, bf16[256,256]{1,0:T(8,128)(2,1)S(1)}, u32[]{:S(2)}, u32[]{:S(2)}) collective-permute-start(bf16[256,256]{1,0:T(8,128)(2,1)S(1)} %get-tuple-element.21), channel_id=1, source_target_pairs={{0,2},{1,3},{2,0},{3,1},{4,6},{5,7},{6,4},{7,5},{8,10},{9,11},{10,... | collective-permute-start | bytes 393224 | tf_op jit(solution)/shard_map/ppermute | solution.py:35
  75.4 0.0 collective-permute-done.3.refs_0_
  75.4 1.2 %collective-permute-done.4.refs_1_ = bf16[256,256]{1,0:T(8,128)(2,1)S(1)} collective-permute-done((bf16[256,256]{1,0:T(8,128)(2,1)S(1)}, bf16[256,256]{1,0:T(8,128)(2,1)S(1)}, u32[]{:S(2)}, u32[]{:S(2)}) %collective-permute-start.4) | collective-permute-done | bytes 131104 | tf_op jit(solution)/shard_map/ppermute | solution.py:35
  76.6 2.4 %collective-permute-done.5.refs_2_ = bf16[256,256]{1,0:T(8,128)(2,1)S(1)} collective-permute-done((bf16[256,256]{1,0:T(8,128)(2,1)S(1)}, bf16[256,256]{1,0:T(8,128)(2,1)S(1)}, u32[]{:S(2)}, u32[]{:S(2)}) %collective-permute-start.5) | collective-permute-done | bytes 131104 | tf_op jit(solution)/shard_map/ppermute | solution.py:35
  79.0 0.2 collective-permute-done.6.refs_3_
  79.2 0.8 shard_map.124
  (5 shorter events, 0.0 us)
Async XLA Ops:
  0.0 27.0 %copy-start.7 = (f32[33,256]{1,0:T(8,128)S(1)}, f32[33,256]{1,0:T(8,128)}, u32[]{:S(2)}) copy-start(f32[33,256]{1,0:T(8,128)} %constant.32.clone.refs_6_) | copy-start | bytes 101380
  0.0 27.0 %copy-start.8 = (f32[33,256]{1,0:T(8,128)S(1)}, f32[33,256]{1,0:T(8,128)}, u32[]{:S(2)}) copy-start(f32[33,256]{1,0:T(8,128)} %constant.31.clone.refs_5_) | copy-start | bytes 101380
  0.0 27.0 %copy-start.4 = (bf16[256,528]{1,0:T(8,128)(2,1)S(1)}, bf16[256,528]{1,0:T(8,128)(2,1)}, u32[]{:S(2)}) copy-start(bf16[256,528]{1,0:T(8,128)(2,1)} %constant.30.clone.refs_4_) | copy-start | bytes 811012
  0.0 27.0 %copy-start.5 = (bf16[256,256]{1,0:T(8,128)(2,1)S(1)}, bf16[256,256]{1,0:T(8,128)(2,1)}, u32[]{:S(2)}) copy-start(bf16[256,256]{1,0:T(8,128)(2,1)} %constant.29.clone.refs_3_) | copy-start | bytes 393220
  0.0 27.0 %copy-start.6 = (bf16[256,256]{1,0:T(8,128)(2,1)S(1)}, bf16[256,256]{1,0:T(8,128)(2,1)}, u32[]{:S(2)}) copy-start(bf16[256,256]{1,0:T(8,128)(2,1)} %constant.28.clone.refs_2_) | copy-start | bytes 393220
  0.0 27.0 %copy-start.9 = (bf16[66,32]{1,0:T(8,128)(2,1)S(1)}, bf16[66,32]{1,0:T(8,128)(2,1)}, u32[]{:S(2)}) copy-start(bf16[66,32]{1,0:T(8,128)(2,1)} %constant.27.clone.refs_1_) | copy-start | bytes 12676
  2.0 25.0 %all-to-all-start = ((bf16[32,16,256]{2,1,0:T(8,128)(2,1)}), bf16[32,16,256]{2,1,0:T(8,128)(2,1)S(1)}, u32[]{:S(2)}, u32[]{:S(2)}) async-start(bf16[32,16,256]{2,1,0:T(8,128)(2,1)} %bitcast.8), calls=%async_computation | async-start | bytes 524288 | tf_op jit(solution)/shard_map/all_to_all | solution.py:346
  18.6 24.2 %collective-permute-start.2 = (bf16[256,1280]{1,0:T(8,128)(2,1)}, bf16[256,1280]{1,0:T(8,128)(2,1)S(1)}, u32[]{:S(2)}, u32[]{:S(2)}) collective-permute-start(bf16[256,1280]{1,0:T(8,128)(2,1)} %get-tuple-element.17), channel_id=1, source_target_pairs={{0,1},{1,0},{2,3},{3,2},{4,5},{5,4},{6,7},{7,6},{8,9},{9,8},{10,11... | collective-permute-start | bytes 1966088 | tf_op jit(solution)/shard_map/ppermute | solution.py:352
  21.5 20.7 %collective-permute-start = (bf16[256,768]{1,0:T(8,128)(2,1)}, bf16[256,768]{1,0:T(8,128)(2,1)S(1)}, u32[]{:S(2)}, u32[]{:S(2)}) collective-permute-start(bf16[256,768]{1,0:T(8,128)(2,1)} %get-tuple-element.15), channel_id=1, source_target_pairs={{0,2},{1,3},{2,0},{3,1},{4,6},{5,7},{6,4},{7,5},{8,10},{9,11},{10,... | collective-permute-start | bytes 1179656 | tf_op jit(solution)/shard_map/ppermute | solution.py:352
  24.7 18.2 %collective-permute-start.1 = (bf16[256,768]{1,0:T(8,128)(2,1)}, bf16[256,768]{1,0:T(8,128)(2,1)S(1)}, u32[]{:S(2)}, u32[]{:S(2)}) collective-permute-start(bf16[256,768]{1,0:T(8,128)(2,1)} %get-tuple-element.16), channel_id=1, source_target_pairs={{0,3},{1,2},{2,1},{3,0},{4,7},{5,6},{6,5},{7,4},{8,11},{9,10},{10,... | collective-permute-start | bytes 1179656 | tf_op jit(solution)/shard_map/ppermute | solution.py:352
  30.2 11.8 %copy-start.10 = (f32[256]{0:T(256)S(1)}, f32[256]{0:T(256)}, u32[]{:S(2)}) copy-start(f32[256]{0:T(256)} %param.16) | copy-start | bytes 3076
  30.2 18.8 %copy-start.1 = (bf16[256,256]{1,0:T(8,128)(2,1)S(1)}, bf16[256,256]{1,0:T(8,128)(2,1)}, u32[]{:S(2)}) copy-start(bf16[256,256]{1,0:T(8,128)(2,1)} %signal_ref.1) | copy-start | bytes 393220
  30.2 18.8 %copy-start.2 = (bf16[256,256]{1,0:T(8,128)(2,1)S(1)}, bf16[256,256]{1,0:T(8,128)(2,1)}, u32[]{:S(2)}) copy-start(bf16[256,256]{1,0:T(8,128)(2,1)} %pre_ref.1) | copy-start | bytes 393220
  30.2 18.8 %copy-start.3 = (bf16[256,256]{1,0:T(8,128)(2,1)S(1)}, bf16[256,256]{1,0:T(8,128)(2,1)}, u32[]{:S(2)}) copy-start(bf16[256,256]{1,0:T(8,128)(2,1)} %post_ref.1) | copy-start | bytes 393220
  30.2 18.8 %all-to-all-start.1 = ((bf16[32,8,256]{2,1,0:T(8,128)(2,1)}), bf16[32,8,256]{2,1,0:T(8,128)(2,1)S(1)}, u32[]{:S(2)}, u32[]{:S(2)}) async-start(bf16[32,8,256]{2,1,0:T(8,128)(2,1)} %bitcast.3), calls=%async_computation.1 | async-start | bytes 262144 | tf_op jit(solution)/shard_map/all_to_all | solution.py:364
  58.5 1.1 %copy-start = (bf16[256,1280]{1,0:T(8,128)(2,1)S(1)}, bf16[256,1280]{1,0:T(8,128)(2,1)}, u32[]{:S(2)}) copy-start(bf16[256,1280]{1,0:T(8,128)(2,1)} %shard_map.122.refs_2_) | copy-start | bytes 1966084
  60.3 15.2 %collective-permute-start.3 = (bf16[256,256]{1,0:T(8,128)(2,1)S(1)}, bf16[256,256]{1,0:T(8,128)(2,1)S(1)}, u32[]{:S(2)}, u32[]{:S(2)}) collective-permute-start(bf16[256,256]{1,0:T(8,128)(2,1)S(1)} %get-tuple-element.18), channel_id=1, source_target_pairs={{0,10},{1,11},{2,8},{3,9},{4,14},{5,15},{6,12},{7,13},{8,2},{9,3},... | collective-permute-start | bytes 393224 | tf_op jit(solution)/shard_map/ppermute | solution.py:35
  66.7 9.9 %collective-permute-start.4 = (bf16[256,256]{1,0:T(8,128)(2,1)S(1)}, bf16[256,256]{1,0:T(8,128)(2,1)S(1)}, u32[]{:S(2)}, u32[]{:S(2)}) collective-permute-start(bf16[256,256]{1,0:T(8,128)(2,1)S(1)} %get-tuple-element.19), channel_id=1, source_target_pairs={{0,12},{1,13},{2,6},{3,7},{4,0},{5,1},{6,10},{7,11},{8,4},{9,5},{1... | collective-permute-start | bytes 393224 | tf_op jit(solution)/shard_map/ppermute | solution.py:35
  69.1 9.9 %collective-permute-start.5 = (bf16[256,256]{1,0:T(8,128)(2,1)S(1)}, bf16[256,256]{1,0:T(8,128)(2,1)S(1)}, u32[]{:S(2)}, u32[]{:S(2)}) collective-permute-start(bf16[256,256]{1,0:T(8,128)(2,1)S(1)} %get-tuple-element.20), channel_id=1, source_target_pairs={{0,14},{1,15},{2,4},{3,5},{4,2},{5,3},{6,8},{7,9},{8,6},{9,7},{10,... | collective-permute-start | bytes 393224 | tf_op jit(solution)/shard_map/ppermute | solution.py:35
  73.5 5.7 %collective-permute-start.6 = (bf16[256,256]{1,0:T(8,128)(2,1)S(1)}, bf16[256,256]{1,0:T(8,128)(2,1)S(1)}, u32[]{:S(2)}, u32[]{:S(2)}) collective-permute-start(bf16[256,256]{1,0:T(8,128)(2,1)S(1)} %get-tuple-element.21), channel_id=1, source_target_pairs={{0,2},{1,3},{2,0},{3,1},{4,6},{5,7},{6,4},{7,5},{8,10},{9,11},{10,... | collective-permute-start | bytes 393224 | tf_op jit(solution)/shard_map/ppermute | solution.py:35

commit v9 on v7

--- a/solution.py
+++ b/solution.py
@@ -127,8 +127,11 @@
     )(place, out_weight)
 
 
-def project_kernel(group, place_ref, mixed_ref, *refs):
-    weight_refs, out_refs = refs[:group], refs[group:]
+def project_kernel(group, place_ref, mixed_ref, own_hbm, *refs):
+    out_refs, own_ref, sem = refs[group - 1 : -2], refs[-2], refs[-1]
+    load = pltpu.make_async_copy(own_hbm, own_ref, sem)
+    load.start()
+    weight_refs = (own_ref,) + refs[: group - 1]
     tokens = mixed_ref.shape[0] // group
     width = out_refs[0].shape[1]
     place = lax.rem(place_ref[0], group)
@@ -136,16 +139,15 @@
         mixed_ref[pl.ds(pl.multiple_of((place ^ r) * tokens, tokens), tokens), :]
         for r in range(group)
     ]
+
+    def product(r, i):
+        weights = weight_refs[r][:, i * width : (i + 1) * width]
+        return jnp.dot(mixed[r], weights, preferred_element_type=jnp.float32)
+
+    totals = [sum(product(r, i) for r in range(1, group)) for i in range(group)]
+    load.wait()
     for i in range(group):
-        total = None
-        for r in range(group):
-            term = jnp.dot(
-                mixed[r],
-                weight_refs[r][:, i * width : (i + 1) * width],
-                preferred_element_type=jnp.float32,
-            )
-            total = term if total is None else total + term
-        out_refs[i][...] = total.astype(out_refs[i].dtype)
+        out_refs[i][...] = (totals[i] + product(0, i)).astype(out_refs[i].dtype)
 
 
 def project(place, mixed, weights, width):
@@ -155,15 +157,20 @@
         lambda *refs: project_kernel(group, *refs),
         out_shape=[share] * group,
         in_specs=[pl.BlockSpec(memory_space=pltpu.SMEM)]
-        + [pl.BlockSpec(memory_space=pltpu.VMEM)] * (1 + group),
+        + [pl.BlockSpec(memory_space=pltpu.VMEM), pl.BlockSpec(memory_space=pltpu.HBM)]
+        + [pl.BlockSpec(memory_space=pltpu.VMEM)] * (group - 1),
         out_specs=[pl.BlockSpec(memory_space=pltpu.VMEM)] * group,
+        scratch_shapes=[
+            pltpu.VMEM(weights[0].shape, weights[0].dtype),
+            pltpu.SemaphoreType.DMA,
+        ],
         compiler_params=pltpu.CompilerParams(vmem_limit_bytes=10 * MIB),
         cost_estimate=pl.CostEstimate(
             flops=2 * mixed.size * group * width,
             bytes_accessed=2 * (mixed.size + sum(w.size for w in weights) + group * share.size),
             transcendentals=0,
         ),
-    )(place, mixed, *weights)
+    )(place, mixed, pltpu.with_memory_space_constraint(weights[0], pltpu.HBM), *weights[1:])
 
 
 def finish_kernel(*refs):
@@ -213,44 +220,47 @@
 
 
 def convolve_kernel(
-    channels, in_ref, front_ref, square_cos_ref, square_sin_ref, back_ref, cos_ref, sin_ref, after_ref, out_ref
+    channels, in_ref, front_ref, square_cos_ref, square_sin_ref, back_ref, cos_ref, sin_ref, after_ref, out_ref, rows_ref
 ):
     del after_ref
     low, tokens = cos_ref.shape
     both = 2 * channels
-    turn_cos = cos_ref[...].reshape(low, 1, tokens)
-    turn_sin = sin_ref[...].reshape(low, 1, tokens)
     blocks = front_ref.shape[1]
     width = blocks * both
     repeat = lax.broadcasted_iota(jnp.int32, (blocks, width), 1) // both
     repeat = (repeat == lax.broadcasted_iota(jnp.int32, (blocks, width), 0)).astype(jnp.bfloat16)
     agree = lax.broadcasted_iota(jnp.int32, (both, width), 1) % both
-    agree = agree == lax.broadcasted_iota(jnp.int32, (both, width), 0)
-    entries = matmul(front_ref[...], repeat).reshape(2 * low, 1, width)
-    front = jnp.where(agree[None], entries, 0.0).reshape(2 * low * both, width)
-    spread = matmul(front.astype(jnp.bfloat16), in_ref[...])
-    real = spread[: low * both].reshape(low, both, tokens)
-    imag = spread[low * both :].reshape(low, both, tokens)
-    turned_real = (real * turn_cos + imag * turn_sin).reshape(low * both, tokens).astype(jnp.bfloat16)
-    turned_imag = (imag * turn_cos - real * turn_sin).reshape(low * both, tokens).astype(jnp.bfloat16)
+    agree = (agree == lax.broadcasted_iota(jnp.int32, (both, width), 0))[None]
+    entries = matmul(front_ref[...], repeat)
+    turn_cos = cos_ref[...].reshape(low, 1, tokens)
+    turn_sin = sin_ref[...].reshape(low, 1, tokens)
+
+    def spread(part):
+        part = jnp.where(agree, part.reshape(low, 1, width), 0.0)
+        part = part.reshape(low * both, width).astype(jnp.bfloat16)
+        return matmul(part, in_ref[...]).reshape(low, both, tokens)
+
+    def flat(array):
+        return array.reshape(-1, tokens).astype(jnp.bfloat16)
+
+    real, imag = spread(entries[:low]), spread(entries[low:])
+    turned_real = flat(real * turn_cos + imag * turn_sin)
+    turned_imag = flat(imag * turn_cos - real * turn_sin)
     square_cos, square_sin = square_cos_ref[...], square_sin_ref[...]
-    real = (matmul(turned_real, square_cos) + matmul(turned_imag, square_sin)).reshape(low, both, tokens)
-    imag = (matmul(turned_imag, square_cos) - matmul(turned_real, square_sin)).reshape(low, both, tokens)
+    real = matmul(turned_real, square_cos) + matmul(turned_imag, square_sin)
+    imag = matmul(turned_imag, square_cos) - matmul(turned_real, square_sin)
+    real, imag = real.reshape(low, both, tokens), imag.reshape(low, both, tokens)
     sig_real, tap_real = real[:, :channels], real[:, channels:]
     sig_imag, tap_imag = imag[:, :channels], imag[:, channels:]
-    prod_real = sig_real * tap_real - sig_imag * tap_imag
-    prod_imag = sig_real * tap_imag + sig_imag * tap_real
-    prod_real = prod_real.reshape(low * channels, tokens).astype(jnp.bfloat16)
-    prod_imag = prod_imag.reshape(low * channels, tokens).astype(jnp.bfloat16)
+    prod_real = flat(sig_real * tap_real - sig_imag * tap_imag)
+    prod_imag = flat(sig_real * tap_imag + sig_imag * tap_real)
     real = matmul(prod_real, square_cos) - matmul(prod_imag, square_sin)
     imag = matmul(prod_imag, square_cos) + matmul(prod_real, square_sin)
     real, imag = real.reshape(low, channels, tokens), imag.reshape(low, channels, tokens)
-    rows = jnp.concatenate(
-        [real * turn_cos - imag * turn_sin, real * turn_sin + imag * turn_cos], axis=0
-    )
-    out_ref[...] = matmul(
-        back_ref[...], rows.reshape(2 * low * channels, tokens).astype(jnp.bfloat16)
-    ).astype(out_ref.dtype)
+    half = low * channels
+    rows_ref[:half, :] = (real * turn_cos - imag * turn_sin).reshape(half, tokens)
+    rows_ref[half:, :] = (real * turn_sin + imag * turn_cos).reshape(half, tokens)
+    out_ref[...] = matmul(back_ref[...], rows_ref[...].astype(jnp.bfloat16)).astype(out_ref.dtype)
 
 
 def convolve(blocks_in, channels, tables, after):
@@ -261,6 +271,7 @@
         in_specs=[pl.BlockSpec(memory_space=pltpu.VMEM)] * (1 + len(tables))
         + [pl.BlockSpec(memory_space=pltpu.SMEM)],
         out_specs=pl.BlockSpec(memory_space=pltpu.VMEM),
+        scratch_shapes=[pltpu.VMEM((2 * tables[-1].shape[0] * channels, tokens), jnp.float32)],
         compiler_params=pltpu.CompilerParams(vmem_limit_bytes=32 * MIB),
         cost_estimate=pl.CostEstimate(
             flops=800_000_000, bytes_accessed=3_000_000, transcendentals=0

time: 80.3 us -> 79.7 us (level)
  local copies, waits for them, and re-layouts: 1.23 us -> 0.19 us
    unnamed x22 -> x20, local copies, waits for them, and re-layouts: 1.09 us -> 0.05 us
    pallas_call x1, Pallas kernels: 0.71 us -> 1.71 us  [project(): pl.pallas_call(lambda *refs: project_kernel(group, *refs), out_shape=[sha...]
  transfers between devices with their start and end apart: 8 -> 8, of which waited for: 4 -> 3; matrix products, arithmetic and copies ran while one was open for 0% -> 0% of each run, Pallas kernels for 10% -> 10%
where the time goes in v9:
time: 79.7 us; the launch traced here: 79.2 us
  starting transfers between devices  44.9 us (56%)
  waiting for transfers between devices  12.8 us (16%)
  Pallas kernels  12.1 us (15%)
  blocking collectives  8.89 us (11%)
    all_to_all x1, starting transfers between devices, per_device(): lax.all_to_all(send, 'ctx', split_axis=0, concat_axis=0, tiled=True)  13.7 us
    ppermute x3, starting transfers between devices, send_to_target(): return lax.ppermute(share, TP_AXES, pairs)  13.2 us
    all_to_all x1, starting transfers between devices, per_device(): lax.all_to_all(convolved, 'ctx', split_axis=0, concat_axis=0, tiled=True)  9.65 us
    all_gather x1, blocking collectives, per_device(): gathered = lax.all_gather(mixed, GROUP, axis=0, tiled=True)  8.89 us
    ppermute x3, starting transfers between devices, per_device(): lax.ppermute(piece, GROUP, [(t, t ^ r) for t in range(group)])  8.32 us
    ppermute x3, waiting for transfers between devices, per_device(): lax.ppermute(piece, GROUP, [(t, t ^ r) for t in range(group)])  7.26 us
    ppermute x3, waiting for transfers between devices, send_to_target(): return lax.ppermute(share, TP_AXES, pairs)  5.49 us
    pallas_call x1, Pallas kernels, arrange(): pl.pallas_call(lambda *refs: arrange_kernel(group, quads, width, members,...  2.96 us
  transfers between devices with their start and end apart: 8, of which 3 were waited for; matrix products, arithmetic and copies ran while one was open for 0% of the time, Pallas kernels for 10%

profile of v9, /device:TPU:1, one launch (start us, length us, event | category | flops | bytes accessed | tf_op | source)
XLA Modules:
  0.0 79.2 jit_solution(11450663068300070389)
XLA Ops:
  0.0 0.0 copy-start.6
  0.0 0.0 copy-start.7
  0.0 0.0 copy-start.3
  0.0 0.0 copy-start.4
  0.0 0.0 copy-start.5
  0.0 0.0 copy-start.8
  0.0 1.9 %shard_map.118 = bf16[512,256]{1,0:T(8,128)(2,1)} custom-call(bf16[256,256]{1,0:T(8,128)(2,1)} %signal_ref.1, bf16[256,256]{1,0:T(8,128)(2,1)} %pre_ref.1, f32[256,256]{1,0:T(8,128)} %refs_2_.2), custom_call_target="tpu_custom_call" | custom-call | tf_op jit(solution)/shard_map/pallas_call | solution.py:308
  1.9 13.7 %all-to-all-start = ((bf16[32,16,256]{2,1,0:T(8,128)(2,1)}), bf16[32,16,256]{2,1,0:T(8,128)(2,1)S(1)}, u32[]{:S(2)}, u32[]{:S(2)}) async-start(bf16[32,16,256]{2,1,0:T(8,128)(2,1)} %bitcast.8), calls=%async_computation | async-start | bytes 524288 | tf_op jit(solution)/shard_map/all_to_all | solution.py:355
  15.7 3.0 %shard_map.119 = (bf16[256,1024]{1,0:T(8,128)(2,1)}, bf16[256,1024]{1,0:T(8,128)(2,1)}, bf16[256,1024]{1,0:T(8,128)(2,1)}, s32[1]{0:T(128)}) custom-call(s32[1]{0:T(128)} %bitcast.refs_0_, bf16[256,4096]{1,0:T(8,128)(2,1)} %refs_1_.6), custom_call_target="tpu_custom_call" | custom-call | bytes 3145728 | tf_op jit(solution)/shard_map/pallas_call | solution.py:71
  18.7 2.9 %collective-permute-start = (bf16[256,1024]{1,0:T(8,128)(2,1)}, bf16[256,1024]{1,0:T(8,128)(2,1)S(1)}, u32[]{:S(2)}, u32[]{:S(2)}) collective-permute-start(bf16[256,1024]{1,0:T(8,128)(2,1)} %get-tuple-element.14), channel_id=1, source_target_pairs={{0,1},{1,0},{2,3},{3,2},{4,5},{5,4},{6,7},{7,6},{8,9},{9,8},{10,11... | collective-permute-start | bytes 1572872 | tf_op jit(solution)/shard_map/ppermute | solution.py:361
  21.5 3.2 %collective-permute-start.1 = (bf16[256,1024]{1,0:T(8,128)(2,1)}, bf16[256,1024]{1,0:T(8,128)(2,1)S(1)}, u32[]{:S(2)}, u32[]{:S(2)}) collective-permute-start(bf16[256,1024]{1,0:T(8,128)(2,1)} %get-tuple-element.15), channel_id=1, source_target_pairs={{0,2},{1,3},{2,0},{3,1},{4,6},{5,7},{6,4},{7,5},{8,10},{9,11},{10,... | collective-permute-start | bytes 1572872 | tf_op jit(solution)/shard_map/ppermute | solution.py:361
  24.7 2.3 %collective-permute-start.2 = (bf16[256,1024]{1,0:T(8,128)(2,1)}, bf16[256,1024]{1,0:T(8,128)(2,1)S(1)}, u32[]{:S(2)}, u32[]{:S(2)}) collective-permute-start(bf16[256,1024]{1,0:T(8,128)(2,1)} %get-tuple-element.16), channel_id=1, source_target_pairs={{0,3},{1,2},{2,1},{3,0},{4,7},{5,6},{6,5},{7,4},{8,11},{9,10},{10,... | collective-permute-start | bytes 1572872 | tf_op jit(solution)/shard_map/ppermute | solution.py:361
  27.0 0.0 all-to-all-done
  27.0 0.0 copy-done.6
  27.0 0.0 copy-done.7
  27.0 0.0 copy-done.3
  27.0 0.0 copy-done.4
  27.1 0.0 copy-done.5
  27.1 0.0 copy-done.8
  27.1 2.6 %shard_map.120 = bf16[256,256]{1,0:T(8,128)(2,1)} custom-call(bf16[512,256]{1,0:T(8,128)(2,1)S(1)} %bitcast.7, bf16[66,32]{1,0:T(8,128)(2,1)S(1)} %copy-done.8, bf16[256,256]{1,0:T(8,128)(2,1)S(1)} %copy-done.5, bf16[256,256]{1,0:T(8,128)(2,1)S(1)} %copy-done.4, bf16[256,528]{1,0:T(8,128)(2,1)S(1)} %copy-done.3, f32[33,256]{1,0:T(8,128)S(1)} %copy-done.7, ...), custom_call_target="tpu_custom_call" | custom-call | flops 800000000 | bytes 3000000 | tf_op jit(solution)/shard_map/pallas_call | solution.py:268
  29.7 0.0 copy-start.9
  29.7 0.0 copy-start
  29.7 0.0 copy-start.1
  29.7 0.0 copy-start.2
  29.7 9.7 %all-to-all-start.1 = ((bf16[32,8,256]{2,1,0:T(8,128)(2,1)}), bf16[32,8,256]{2,1,0:T(8,128)(2,1)S(1)}, u32[]{:S(2)}, u32[]{:S(2)}) async-start(bf16[32,8,256]{2,1,0:T(8,128)(2,1)} %bitcast.3), calls=%async_computation.1 | async-start | bytes 262144 | tf_op jit(solution)/shard_map/all_to_all | solution.py:373
  39.4 2.0 %shard_map.122.refs_2_ = bf16[256,1024]{1,0:T(8,128)(2,1)} custom-call(s32[1]{0:T(128)} %bitcast.refs_0_, bf16[256,4096]{1,0:T(8,128)(2,1)} %refs_1_.6), custom_call_target="tpu_custom_call" | custom-call | bytes 1048576 | tf_op jit(solution)/shard_map/pallas_call | solution.py:114
  41.4 0.0 copy-done.9
  41.4 0.1 copy.13.gain_ref
  41.5 0.0 collective-permute-done.refs_3_
  41.5 0.0 collective-permute-done.1.refs_4_
  41.6 7.3 %collective-permute-done.2.refs_5_ = bf16[256,1024]{1,0:T(8,128)(2,1)S(1)} collective-permute-done((bf16[256,1024]{1,0:T(8,128)(2,1)}, bf16[256,1024]{1,0:T(8,128)(2,1)S(1)}, u32[]{:S(2)}, u32[]{:S(2)}) %collective-permute-start.2) | collective-permute-done | bytes 524320 | tf_op jit(solution)/shard_map/ppermute | solution.py:361
  48.8 0.0 all-to-all-done.1
  48.8 0.0 copy-done
  48.8 0.0 copy-done.1
  48.8 0.0 copy-done.2
  48.9 0.2 shard_map.121
  49.0 8.9 %all_gather.3.refs_1_ = bf16[1024,256]{1,0:T(8,128)(2,1)S(1)} all-gather(bf16[256,256]{1,0:T(8,128)(2,1)S(1)} %shard_map.121), channel_id=1, replica_groups=mesh['ctx'=32,'quad'=4,'pair'=2,'core'=2] {'pair','core'}, dimensions={0}, use_global_device_ids=true | all-gather | bytes 655360 | tf_op jit(solution)/shard_map/all_gather | solution.py:377
  57.9 1.7 %shard_map.123 = (bf16[256,256]{1,0:T(8,128)(2,1)S(1)}, bf16[256,256]{1,0:T(8,128)(2,1)S(1)}, bf16[256,256]{1,0:T(8,128)(2,1)S(1)}, bf16[256,256]{1,0:T(8,128)(2,1)S(1)}) custom-call(s32[1]{0:T(128)} %bitcast.refs_0_, bf16[1024,256]{1,0:T(8,128)(2,1)S(1)} %all_gather.3.refs_1_, bf16[256,1024]{1,0:T(8,128)(2,1)} %shard_map.122.refs_2_, ...), custom_call_target="tpu_custom_call" | custom-call | flops 536870912 | bytes 3145728 | tf_op jit(solution)/shard_map/pallas_call | solution.py:156
  59.6 6.4 %collective-permute-start.3 = (bf16[256,256]{1,0:T(8,128)(2,1)S(1)}, bf16[256,256]{1,0:T(8,128)(2,1)S(1)}, u32[]{:S(2)}, u32[]{:S(2)}) collective-permute-start(bf16[256,256]{1,0:T(8,128)(2,1)S(1)} %get-tuple-element.17), channel_id=1, source_target_pairs={{0,10},{1,11},{2,8},{3,9},{4,14},{5,15},{6,12},{7,13},{8,2},{9,3},... | collective-permute-start | bytes 393224 | tf_op jit(solution)/shard_map/ppermute | solution.py:33
  66.1 2.3 %collective-permute-start.4 = (bf16[256,256]{1,0:T(8,128)(2,1)S(1)}, bf16[256,256]{1,0:T(8,128)(2,1)S(1)}, u32[]{:S(2)}, u32[]{:S(2)}) collective-permute-start(bf16[256,256]{1,0:T(8,128)(2,1)S(1)} %get-tuple-element.18), channel_id=1, source_target_pairs={{0,12},{1,13},{2,6},{3,7},{4,0},{5,1},{6,10},{7,11},{8,4},{9,5},{1... | collective-permute-start | bytes 393224 | tf_op jit(solution)/shard_map/ppermute | solution.py:33
  68.4 4.4 %collective-permute-start.5 = (bf16[256,256]{1,0:T(8,128)(2,1)S(1)}, bf16[256,256]{1,0:T(8,128)(2,1)S(1)}, u32[]{:S(2)}, u32[]{:S(2)}) collective-permute-start(bf16[256,256]{1,0:T(8,128)(2,1)S(1)} %get-tuple-element.19), channel_id=1, source_target_pairs={{0,14},{1,15},{2,4},{3,5},{4,2},{5,3},{6,8},{7,9},{8,6},{9,7},{10,... | collective-permute-start | bytes 393224 | tf_op jit(solution)/shard_map/ppermute | solution.py:33
  72.9 0.0 collective-permute-done.3.refs_0_
  72.9 3.1 %collective-permute-done.4.refs_1_ = bf16[256,256]{1,0:T(8,128)(2,1)S(1)} collective-permute-done((bf16[256,256]{1,0:T(8,128)(2,1)S(1)}, bf16[256,256]{1,0:T(8,128)(2,1)S(1)}, u32[]{:S(2)}, u32[]{:S(2)}) %collective-permute-start.4) | collective-permute-done | bytes 131104 | tf_op jit(solution)/shard_map/ppermute | solution.py:33
  76.0 2.4 %collective-permute-done.5.refs_2_ = bf16[256,256]{1,0:T(8,128)(2,1)S(1)} collective-permute-done((bf16[256,256]{1,0:T(8,128)(2,1)S(1)}, bf16[256,256]{1,0:T(8,128)(2,1)S(1)}, u32[]{:S(2)}, u32[]{:S(2)}) %collective-permute-start.5) | collective-permute-done | bytes 131104 | tf_op jit(solution)/shard_map/ppermute | solution.py:33
  78.4 0.8 shard_map.124
  (4 shorter events, 0.0 us)
Async XLA Ops:
  0.0 27.0 %copy-start.6 = (f32[33,256]{1,0:T(8,128)S(1)}, f32[33,256]{1,0:T(8,128)}, u32[]{:S(2)}) copy-start(f32[33,256]{1,0:T(8,128)} %constant.32.clone.refs_6_) | copy-start | bytes 101380
  0.0 27.0 %copy-start.7 = (f32[33,256]{1,0:T(8,128)S(1)}, f32[33,256]{1,0:T(8,128)}, u32[]{:S(2)}) copy-start(f32[33,256]{1,0:T(8,128)} %constant.31.clone.refs_5_) | copy-start | bytes 101380
  0.0 27.0 %copy-start.3 = (bf16[256,528]{1,0:T(8,128)(2,1)S(1)}, bf16[256,528]{1,0:T(8,128)(2,1)}, u32[]{:S(2)}) copy-start(bf16[256,528]{1,0:T(8,128)(2,1)} %constant.30.clone.refs_4_) | copy-start | bytes 811012
  0.0 27.0 %copy-start.4 = (bf16[256,256]{1,0:T(8,128)(2,1)S(1)}, bf16[256,256]{1,0:T(8,128)(2,1)}, u32[]{:S(2)}) copy-start(bf16[256,256]{1,0:T(8,128)(2,1)} %constant.29.clone.refs_3_) | copy-start | bytes 393220
  0.0 27.0 %copy-start.5 = (bf16[256,256]{1,0:T(8,128)(2,1)S(1)}, bf16[256,256]{1,0:T(8,128)(2,1)}, u32[]{:S(2)}) copy-start(bf16[256,256]{1,0:T(8,128)(2,1)} %constant.28.clone.refs_2_) | copy-start | bytes 393220
  0.0 27.0 %copy-start.8 = (bf16[66,32]{1,0:T(8,128)(2,1)S(1)}, bf16[66,32]{1,0:T(8,128)(2,1)}, u32[]{:S(2)}) copy-start(bf16[66,32]{1,0:T(8,128)(2,1)} %constant.27.clone.refs_1_) | copy-start | bytes 12676
  1.9 25.1 %all-to-all-start = ((bf16[32,16,256]{2,1,0:T(8,128)(2,1)}), bf16[32,16,256]{2,1,0:T(8,128)(2,1)S(1)}, u32[]{:S(2)}, u32[]{:S(2)}) async-start(bf16[32,16,256]{2,1,0:T(8,128)(2,1)} %bitcast.8), calls=%async_computation | async-start | bytes 524288 | tf_op jit(solution)/shard_map/all_to_all | solution.py:355
  18.7 22.9 %collective-permute-start = (bf16[256,1024]{1,0:T(8,128)(2,1)}, bf16[256,1024]{1,0:T(8,128)(2,1)S(1)}, u32[]{:S(2)}, u32[]{:S(2)}) collective-permute-start(bf16[256,1024]{1,0:T(8,128)(2,1)} %get-tuple-element.14), channel_id=1, source_target_pairs={{0,1},{1,0},{2,3},{3,2},{4,5},{5,4},{6,7},{7,6},{8,9},{9,8},{10,11... | collective-permute-start | bytes 1572872 | tf_op jit(solution)/shard_map/ppermute | solution.py:361
  21.5 20.0 %collective-permute-start.1 = (bf16[256,1024]{1,0:T(8,128)(2,1)}, bf16[256,1024]{1,0:T(8,128)(2,1)S(1)}, u32[]{:S(2)}, u32[]{:S(2)}) collective-permute-start(bf16[256,1024]{1,0:T(8,128)(2,1)} %get-tuple-element.15), channel_id=1, source_target_pairs={{0,2},{1,3},{2,0},{3,1},{4,6},{5,7},{6,4},{7,5},{8,10},{9,11},{10,... | collective-permute-start | bytes 1572872 | tf_op jit(solution)/shard_map/ppermute | solution.py:361
  24.7 24.1 %collective-permute-start.2 = (bf16[256,1024]{1,0:T(8,128)(2,1)}, bf16[256,1024]{1,0:T(8,128)(2,1)S(1)}, u32[]{:S(2)}, u32[]{:S(2)}) collective-permute-start(bf16[256,1024]{1,0:T(8,128)(2,1)} %get-tuple-element.16), channel_id=1, source_target_pairs={{0,3},{1,2},{2,1},{3,0},{4,7},{5,6},{6,5},{7,4},{8,11},{9,10},{10,... | collective-permute-start | bytes 1572872 | tf_op jit(solution)/shard_map/ppermute | solution.py:361
  29.7 11.7 %copy-start.9 = (f32[256]{0:T(256)S(1)}, f32[256]{0:T(256)}, u32[]{:S(2)}) copy-start(f32[256]{0:T(256)} %param.16) | copy-start | bytes 3076
  29.7 19.1 %copy-start = (bf16[256,256]{1,0:T(8,128)(2,1)S(1)}, bf16[256,256]{1,0:T(8,128)(2,1)}, u32[]{:S(2)}) copy-start(bf16[256,256]{1,0:T(8,128)(2,1)} %signal_ref.1) | copy-start | bytes 393220
  29.7 19.1 %copy-start.1 = (bf16[256,256]{1,0:T(8,128)(2,1)S(1)}, bf16[256,256]{1,0:T(8,128)(2,1)}, u32[]{:S(2)}) copy-start(bf16[256,256]{1,0:T(8,128)(2,1)} %pre_ref.1) | copy-start | bytes 393220
  29.7 19.1 %copy-start.2 = (bf16[256,256]{1,0:T(8,128)(2,1)S(1)}, bf16[256,256]{1,0:T(8,128)(2,1)}, u32[]{:S(2)}) copy-start(bf16[256,256]{1,0:T(8,128)(2,1)} %post_ref.1) | copy-start | bytes 393220
  29.7 19.1 %all-to-all-start.1 = ((bf16[32,8,256]{2,1,0:T(8,128)(2,1)}), bf16[32,8,256]{2,1,0:T(8,128)(2,1)S(1)}, u32[]{:S(2)}, u32[]{:S(2)}) async-start(bf16[32,8,256]{2,1,0:T(8,128)(2,1)} %bitcast.3), calls=%async_computation.1 | async-start | bytes 262144 | tf_op jit(solution)/shard_map/all_to_all | solution.py:373
  59.6 13.2 %collective-permute-start.3 = (bf16[256,256]{1,0:T(8,128)(2,1)S(1)}, bf16[256,256]{1,0:T(8,128)(2,1)S(1)}, u32[]{:S(2)}, u32[]{:S(2)}) collective-permute-start(bf16[256,256]{1,0:T(8,128)(2,1)S(1)} %get-tuple-element.17), channel_id=1, source_target_pairs={{0,10},{1,11},{2,8},{3,9},{4,14},{5,15},{6,12},{7,13},{8,2},{9,3},... | collective-permute-start | bytes 393224 | tf_op jit(solution)/shard_map/ppermute | solution.py:33
  66.1 9.9 %collective-permute-start.4 = (bf16[256,256]{1,0:T(8,128)(2,1)S(1)}, bf16[256,256]{1,0:T(8,128)(2,1)S(1)}, u32[]{:S(2)}, u32[]{:S(2)}) collective-permute-start(bf16[256,256]{1,0:T(8,128)(2,1)S(1)} %get-tuple-element.18), channel_id=1, source_target_pairs={{0,12},{1,13},{2,6},{3,7},{4,0},{5,1},{6,10},{7,11},{8,4},{9,5},{1... | collective-permute-start | bytes 393224 | tf_op jit(solution)/shard_map/ppermute | solution.py:33
  68.4 9.9 %collective-permute-start.5 = (bf16[256,256]{1,0:T(8,128)(2,1)S(1)}, bf16[256,256]{1,0:T(8,128)(2,1)S(1)}, u32[]{:S(2)}, u32[]{:S(2)}) collective-permute-start(bf16[256,256]{1,0:T(8,128)(2,1)S(1)} %get-tuple-element.19), channel_id=1, source_target_pairs={{0,14},{1,15},{2,4},{3,5},{4,2},{5,3},{6,8},{7,9},{8,6},{9,7},{10,... | collective-permute-start | bytes 393224 | tf_op jit(solution)/shard_map/ppermute | solution.py:33

commit v10 on v9

--- a/solution.py
+++ b/solution.py
@@ -196,7 +196,7 @@
     total = period * tokens
     low = blocks + 1
     k1 = np.arange(low)
-    i = np.arange(blocks)
+    i = np.arange(blocks)[::-1]
     s = np.arange(tokens)
     first = 2 * np.pi * (np.outer(k1, i) % period) / period
     turn = 2 * np.pi * (np.outer(k1, s) % total) / total
@@ -342,6 +342,13 @@
     )(post_gate, signal, pre_gate, convolved, skip_gain[:, None], corners)
 
 
+def exchange(parts, devices):
+    backwards = [list(range(devices))[::-1]]
+    return lax.all_to_all(
+        parts, "ctx", split_axis=0, concat_axis=0, axis_index_groups=backwards, tiled=True
+    )
+
+
 def per_device(signal, pre_gate, post_gate, filter_taps, skip_gain, out_weight):
     channels_here, tokens_here = signal.shape
     devices = lax.axis_size("ctx")
@@ -352,7 +359,7 @@
     width = features // (quads * group)
 
     send = outgoing(signal, pre_gate, filter_taps, devices)
-    blocks = lax.all_to_all(send, "ctx", split_axis=0, concat_axis=0, tiled=True)
+    blocks = exchange(send, devices)
 
     place = lax.axis_index(TP_AXES).astype(jnp.int32).reshape(1)
     members = [2, 3, 1]
@@ -365,14 +372,7 @@
     own = own_columns(out_weight, place, group, quads, width)
     tables = dft_tables(devices, tokens_here, channels)
     convolved = convolve(blocks, channels, tables, arranged)
-    inner, _ = arrange(out_weight, place, group, quads, width, [0, 1])
-    weights = [inner[0]] + [
-        lax.ppermute(piece, GROUP, [(t, t ^ r) for t in range(group)])
-        for r, piece in zip(range(1, group), [inner[1]] + pieces)
-    ]
-    convolved = lax.all_to_all(convolved, "ctx", split_axis=0, concat_axis=0, tiled=True).reshape(
-        channels_here, tokens_here
-    )
+    convolved = exchange(convolved, devices).reshape(channels_here, tokens_here)
     mixed = gate(post_gate, signal, pre_gate, convolved, skip_gain, pieces)
     gathered = lax.all_gather(mixed, GROUP, axis=0, tiled=True)
     shares = project(place, gathered, [own] + pieces, width)

time: 79.7 us -> 79.3 us (level)
  starting transfers between devices: 44.9 us -> 47.1 us
  blocking collectives: 8.89 us -> 7.38 us
  waiting for transfers between devices: 12.8 us -> 11.7 us
    all_to_all x2, starting transfers between devices: 23.4 us -> 24.9 us  [exchange(): lax.all_to_all(parts, 'ctx', split_axis=0, concat_axis=0, axis_index_grou...]
    all_gather x1, blocking collectives: 8.89 us -> 7.38 us  [per_device(): gathered = lax.all_gather(mixed, GROUP, axis=0, tiled=True)]
    ppermute x3, waiting for transfers between devices: 5.49 us -> 4.44 us  [send_to_target(): return lax.ppermute(share, TP_AXES, pairs)]
where the time goes in v10:
time: 79.3 us; the launch traced here: 78.8 us
  starting transfers between devices  47.1 us (59%)
  Pallas kernels  12.1 us (15%)
  waiting for transfers between devices  11.7 us (15%)
  blocking collectives  7.38 us (9%)
    all_to_all x2, starting transfers between devices, exchange(): lax.all_to_all(parts, 'ctx', split_axis=0, concat_axis=0, axis_index_grou...  24.9 us
    ppermute x3, starting transfers between devices, send_to_target(): return lax.ppermute(share, TP_AXES, pairs)  13.9 us
    ppermute x3, starting transfers between devices, per_device(): lax.ppermute(piece, GROUP, [(t, t ^ r) for t in range(group)])  8.32 us
    all_gather x1, blocking collectives, per_device(): gathered = lax.all_gather(mixed, GROUP, axis=0, tiled=True)  7.38 us
    ppermute x3, waiting for transfers between devices, per_device(): lax.ppermute(piece, GROUP, [(t, t ^ r) for t in range(group)])  7.24 us
    ppermute x3, waiting for transfers between devices, send_to_target(): return lax.ppermute(share, TP_AXES, pairs)  4.44 us
    pallas_call x1, Pallas kernels, arrange(): pl.pallas_call(lambda *refs: arrange_kernel(group, quads, width, members,...  2.96 us
    pallas_call x1, Pallas kernels, convolve(): pl.pallas_call(lambda *refs: convolve_kernel(channels, *refs), out_shape=...  2.63 us
  transfers between devices with their start and end apart: 8, of which 3 were waited for; matrix products, arithmetic and copies ran while one was open for 0% of the time, Pallas kernels for 10%

profile of v10, /device:TPU:1, one launch (start us, length us, event | category | flops | bytes accessed | tf_op | source)
XLA Modules:
  0.0 78.8 jit_solution(6312415231612327432)
XLA Ops:
  0.0 0.0 copy-start.6
  0.0 0.0 copy-start.7
  0.0 0.0 copy-start.3
  0.0 0.0 copy-start.4
  0.0 0.0 copy-start.5
  0.0 0.0 copy-start.8
  0.0 1.9 %shard_map.118 = bf16[512,256]{1,0:T(8,128)(2,1)} custom-call(bf16[256,256]{1,0:T(8,128)(2,1)} %signal_ref.1, bf16[256,256]{1,0:T(8,128)(2,1)} %pre_ref.1, f32[256,256]{1,0:T(8,128)} %refs_2_.2), custom_call_target="tpu_custom_call" | custom-call | tf_op jit(solution)/shard_map/pallas_call | solution.py:308
  1.9 15.5 %all-to-all-start = ((bf16[32,16,256]{2,1,0:T(8,128)(2,1)}), bf16[32,16,256]{2,1,0:T(8,128)(2,1)S(1)}, u32[]{:S(2)}, u32[]{:S(2)}) async-start(bf16[32,16,256]{2,1,0:T(8,128)(2,1)} %bitcast.8), calls=%async_computation | async-start | bytes 524288 | tf_op jit(solution)/shard_map/all_to_all | solution.py:347
  17.5 3.0 %shard_map.119 = (bf16[256,1024]{1,0:T(8,128)(2,1)}, bf16[256,1024]{1,0:T(8,128)(2,1)}, bf16[256,1024]{1,0:T(8,128)(2,1)}, s32[1]{0:T(128)}) custom-call(s32[1]{0:T(128)} %bitcast.refs_0_, bf16[256,4096]{1,0:T(8,128)(2,1)} %refs_1_.6), custom_call_target="tpu_custom_call" | custom-call | bytes 3145728 | tf_op jit(solution)/shard_map/pallas_call | solution.py:71
  20.4 2.9 %collective-permute-start = (bf16[256,1024]{1,0:T(8,128)(2,1)}, bf16[256,1024]{1,0:T(8,128)(2,1)S(1)}, u32[]{:S(2)}, u32[]{:S(2)}) collective-permute-start(bf16[256,1024]{1,0:T(8,128)(2,1)} %get-tuple-element.14), channel_id=1, source_target_pairs={{0,1},{1,0},{2,3},{3,2},{4,5},{5,4},{6,7},{7,6},{8,9},{9,8},{10,11... | collective-permute-start | bytes 1572872 | tf_op jit(solution)/shard_map/ppermute | solution.py:368
  23.3 3.2 %collective-permute-start.1 = (bf16[256,1024]{1,0:T(8,128)(2,1)}, bf16[256,1024]{1,0:T(8,128)(2,1)S(1)}, u32[]{:S(2)}, u32[]{:S(2)}) collective-permute-start(bf16[256,1024]{1,0:T(8,128)(2,1)} %get-tuple-element.15), channel_id=1, source_target_pairs={{0,2},{1,3},{2,0},{3,1},{4,6},{5,7},{6,4},{7,5},{8,10},{9,11},{10,... | collective-permute-start | bytes 1572872 | tf_op jit(solution)/shard_map/ppermute | solution.py:368
  26.5 2.3 %collective-permute-start.2 = (bf16[256,1024]{1,0:T(8,128)(2,1)}, bf16[256,1024]{1,0:T(8,128)(2,1)S(1)}, u32[]{:S(2)}, u32[]{:S(2)}) collective-permute-start(bf16[256,1024]{1,0:T(8,128)(2,1)} %get-tuple-element.16), channel_id=1, source_target_pairs={{0,3},{1,2},{2,1},{3,0},{4,7},{5,6},{6,5},{7,4},{8,11},{9,10},{10,... | collective-permute-start | bytes 1572872 | tf_op jit(solution)/shard_map/ppermute | solution.py:368
  28.8 0.0 all-to-all-done
  28.8 0.0 copy-done.6
  28.8 0.0 copy-done.7
  28.8 0.0 copy-done.3
  28.8 0.0 copy-done.4
  28.8 0.0 copy-done.5
  28.9 0.0 copy-done.8
  28.9 2.6 %shard_map.120 = bf16[256,256]{1,0:T(8,128)(2,1)} custom-call(bf16[512,256]{1,0:T(8,128)(2,1)S(1)} %bitcast.7, bf16[66,32]{1,0:T(8,128)(2,1)S(1)} %copy-done.8, bf16[256,256]{1,0:T(8,128)(2,1)S(1)} %copy-done.5, bf16[256,256]{1,0:T(8,128)(2,1)S(1)} %copy-done.4, bf16[256,528]{1,0:T(8,128)(2,1)S(1)} %copy-done.3, f32[33,256]{1,0:T(8,128)S(1)} %copy-done.7, ...), custom_call_target="tpu_custom_call" | custom-call | flops 800000000 | bytes 3000000 | tf_op jit(solution)/shard_map/pallas_call | solution.py:268
  31.5 0.0 copy-start.9
  31.5 0.0 copy-start
  31.5 0.0 copy-start.1
  31.5 0.0 copy-start.2
  31.5 9.4 %all-to-all-start.1 = ((bf16[32,8,256]{2,1,0:T(8,128)(2,1)}), bf16[32,8,256]{2,1,0:T(8,128)(2,1)S(1)}, u32[]{:S(2)}, u32[]{:S(2)}) async-start(bf16[32,8,256]{2,1,0:T(8,128)(2,1)} %bitcast.3), calls=%async_computation.1 | async-start | bytes 262144 | tf_op jit(solution)/shard_map/all_to_all | solution.py:347
  40.9 2.0 %shard_map.122.refs_2_ = bf16[256,1024]{1,0:T(8,128)(2,1)} custom-call(s32[1]{0:T(128)} %bitcast.refs_0_, bf16[256,4096]{1,0:T(8,128)(2,1)} %refs_1_.6), custom_call_target="tpu_custom_call" | custom-call | bytes 1048576 | tf_op jit(solution)/shard_map/pallas_call | solution.py:114
  42.9 0.0 copy-done.9
  42.9 0.1 copy.13.gain_ref
  43.0 0.0 collective-permute-done.refs_3_
  43.0 0.0 collective-permute-done.1.refs_4_
  43.1 7.2 %collective-permute-done.2.refs_5_ = bf16[256,1024]{1,0:T(8,128)(2,1)S(1)} collective-permute-done((bf16[256,1024]{1,0:T(8,128)(2,1)}, bf16[256,1024]{1,0:T(8,128)(2,1)S(1)}, u32[]{:S(2)}, u32[]{:S(2)}) %collective-permute-start.2) | collective-permute-done | bytes 524320 | tf_op jit(solution)/shard_map/ppermute | solution.py:368
  50.3 0.0 all-to-all-done.1
  50.3 0.0 copy-done
  50.3 0.0 copy-done.1
  50.3 0.0 copy-done.2
  50.3 0.2 shard_map.121
  50.5 7.4 %all_gather.3.refs_1_ = bf16[1024,256]{1,0:T(8,128)(2,1)S(1)} all-gather(bf16[256,256]{1,0:T(8,128)(2,1)S(1)} %shard_map.121), channel_id=1, replica_groups=mesh['ctx'=32,'quad'=4,'pair'=2,'core'=2] {'pair','core'}, dimensions={0}, use_global_device_ids=true | all-gather | bytes 655360 | tf_op jit(solution)/shard_map/all_gather | solution.py:377
  57.9 1.7 %shard_map.123 = (bf16[256,256]{1,0:T(8,128)(2,1)S(1)}, bf16[256,256]{1,0:T(8,128)(2,1)S(1)}, bf16[256,256]{1,0:T(8,128)(2,1)S(1)}, bf16[256,256]{1,0:T(8,128)(2,1)S(1)}) custom-call(s32[1]{0:T(128)} %bitcast.refs_0_, bf16[1024,256]{1,0:T(8,128)(2,1)S(1)} %all_gather.3.refs_1_, bf16[256,1024]{1,0:T(8,128)(2,1)} %shard_map.122.refs_2_, ...), custom_call_target="tpu_custom_call" | custom-call | flops 536870912 | bytes 3145728 | tf_op jit(solution)/shard_map/pallas_call | solution.py:156
  59.6 6.6 %collective-permute-start.3 = (bf16[256,256]{1,0:T(8,128)(2,1)S(1)}, bf16[256,256]{1,0:T(8,128)(2,1)S(1)}, u32[]{:S(2)}, u32[]{:S(2)}) collective-permute-start(bf16[256,256]{1,0:T(8,128)(2,1)S(1)} %get-tuple-element.17), channel_id=1, source_target_pairs={{0,10},{1,11},{2,8},{3,9},{4,14},{5,15},{6,12},{7,13},{8,2},{9,3},... | collective-permute-start | bytes 393224 | tf_op jit(solution)/shard_map/ppermute | solution.py:33
  66.2 2.9 %collective-permute-start.4 = (bf16[256,256]{1,0:T(8,128)(2,1)S(1)}, bf16[256,256]{1,0:T(8,128)(2,1)S(1)}, u32[]{:S(2)}, u32[]{:S(2)}) collective-permute-start(bf16[256,256]{1,0:T(8,128)(2,1)S(1)} %get-tuple-element.18), channel_id=1, source_target_pairs={{0,12},{1,13},{2,6},{3,7},{4,0},{5,1},{6,10},{7,11},{8,4},{9,5},{1... | collective-permute-start | bytes 393224 | tf_op jit(solution)/shard_map/ppermute | solution.py:33
  69.1 4.4 %collective-permute-start.5 = (bf16[256,256]{1,0:T(8,128)(2,1)S(1)}, bf16[256,256]{1,0:T(8,128)(2,1)S(1)}, u32[]{:S(2)}, u32[]{:S(2)}) collective-permute-start(bf16[256,256]{1,0:T(8,128)(2,1)S(1)} %get-tuple-element.19), channel_id=1, source_target_pairs={{0,14},{1,15},{2,4},{3,5},{4,2},{5,3},{6,8},{7,9},{8,6},{9,7},{10,... | collective-permute-start | bytes 393224 | tf_op jit(solution)/shard_map/ppermute | solution.py:33
  73.5 0.0 collective-permute-done.3.refs_0_
  73.5 2.5 %collective-permute-done.4.refs_1_ = bf16[256,256]{1,0:T(8,128)(2,1)S(1)} collective-permute-done((bf16[256,256]{1,0:T(8,128)(2,1)S(1)}, bf16[256,256]{1,0:T(8,128)(2,1)S(1)}, u32[]{:S(2)}, u32[]{:S(2)}) %collective-permute-start.4) | collective-permute-done | bytes 131104 | tf_op jit(solution)/shard_map/ppermute | solution.py:33
  76.1 1.9 %collective-permute-done.5.refs_2_ = bf16[256,256]{1,0:T(8,128)(2,1)S(1)} collective-permute-done((bf16[256,256]{1,0:T(8,128)(2,1)S(1)}, bf16[256,256]{1,0:T(8,128)(2,1)S(1)}, u32[]{:S(2)}, u32[]{:S(2)}) %collective-permute-start.5) | collective-permute-done | bytes 131104 | tf_op jit(solution)/shard_map/ppermute | solution.py:33
  78.0 0.8 shard_map.124
  (4 shorter events, 0.0 us)
Async XLA Ops:
  0.0 28.8 %copy-start.6 = (f32[33,256]{1,0:T(8,128)S(1)}, f32[33,256]{1,0:T(8,128)}, u32[]{:S(2)}) copy-start(f32[33,256]{1,0:T(8,128)} %constant.32.clone.refs_6_) | copy-start | bytes 101380
  0.0 28.8 %copy-start.7 = (f32[33,256]{1,0:T(8,128)S(1)}, f32[33,256]{1,0:T(8,128)}, u32[]{:S(2)}) copy-start(f32[33,256]{1,0:T(8,128)} %constant.31.clone.refs_5_) | copy-start | bytes 101380
  0.0 28.8 %copy-start.3 = (bf16[256,528]{1,0:T(8,128)(2,1)S(1)}, bf16[256,528]{1,0:T(8,128)(2,1)}, u32[]{:S(2)}) copy-start(bf16[256,528]{1,0:T(8,128)(2,1)} %constant.30.clone.refs_4_) | copy-start | bytes 811012
  0.0 28.8 %copy-start.4 = (bf16[256,256]{1,0:T(8,128)(2,1)S(1)}, bf16[256,256]{1,0:T(8,128)(2,1)}, u32[]{:S(2)}) copy-start(bf16[256,256]{1,0:T(8,128)(2,1)} %constant.29.clone.refs_3_) | copy-start | bytes 393220
  0.0 28.8 %copy-start.5 = (bf16[256,256]{1,0:T(8,128)(2,1)S(1)}, bf16[256,256]{1,0:T(8,128)(2,1)}, u32[]{:S(2)}) copy-start(bf16[256,256]{1,0:T(8,128)(2,1)} %constant.28.clone.refs_2_) | copy-start | bytes 393220
  0.0 28.8 %copy-start.8 = (bf16[66,32]{1,0:T(8,128)(2,1)S(1)}, bf16[66,32]{1,0:T(8,128)(2,1)}, u32[]{:S(2)}) copy-start(bf16[66,32]{1,0:T(8,128)(2,1)} %constant.27.clone.refs_1_) | copy-start | bytes 12676
  1.9 26.8 %all-to-all-start = ((bf16[32,16,256]{2,1,0:T(8,128)(2,1)}), bf16[32,16,256]{2,1,0:T(8,128)(2,1)S(1)}, u32[]{:S(2)}, u32[]{:S(2)}) async-start(bf16[32,16,256]{2,1,0:T(8,128)(2,1)} %bitcast.8), calls=%async_computation | async-start | bytes 524288 | tf_op jit(solution)/shard_map/all_to_all | solution.py:347
  20.4 22.6 %collective-permute-start = (bf16[256,1024]{1,0:T(8,128)(2,1)}, bf16[256,1024]{1,0:T(8,128)(2,1)S(1)}, u32[]{:S(2)}, u32[]{:S(2)}) collective-permute-start(bf16[256,1024]{1,0:T(8,128)(2,1)} %get-tuple-element.14), channel_id=1, source_target_pairs={{0,1},{1,0},{2,3},{3,2},{4,5},{5,4},{6,7},{7,6},{8,9},{9,8},{10,11... | collective-permute-start | bytes 1572872 | tf_op jit(solution)/shard_map/ppermute | solution.py:368
  23.3 19.7 %collective-permute-start.1 = (bf16[256,1024]{1,0:T(8,128)(2,1)}, bf16[256,1024]{1,0:T(8,128)(2,1)S(1)}, u32[]{:S(2)}, u32[]{:S(2)}) collective-permute-start(bf16[256,1024]{1,0:T(8,128)(2,1)} %get-tuple-element.15), channel_id=1, source_target_pairs={{0,2},{1,3},{2,0},{3,1},{4,6},{5,7},{6,4},{7,5},{8,10},{9,11},{10,... | collective-permute-start | bytes 1572872 | tf_op jit(solution)/shard_map/ppermute | solution.py:368
  26.5 23.8 %collective-permute-start.2 = (bf16[256,1024]{1,0:T(8,128)(2,1)}, bf16[256,1024]{1,0:T(8,128)(2,1)S(1)}, u32[]{:S(2)}, u32[]{:S(2)}) collective-permute-start(bf16[256,1024]{1,0:T(8,128)(2,1)} %get-tuple-element.16), channel_id=1, source_target_pairs={{0,3},{1,2},{2,1},{3,0},{4,7},{5,6},{6,5},{7,4},{8,11},{9,10},{10,... | collective-permute-start | bytes 1572872 | tf_op jit(solution)/shard_map/ppermute | solution.py:368
  31.5 11.4 %copy-start.9 = (f32[256]{0:T(256)S(1)}, f32[256]{0:T(256)}, u32[]{:S(2)}) copy-start(f32[256]{0:T(256)} %param.16) | copy-start | bytes 3076
  31.5 18.8 %copy-start = (bf16[256,256]{1,0:T(8,128)(2,1)S(1)}, bf16[256,256]{1,0:T(8,128)(2,1)}, u32[]{:S(2)}) copy-start(bf16[256,256]{1,0:T(8,128)(2,1)} %signal_ref.1) | copy-start | bytes 393220
  31.5 18.8 %copy-start.1 = (bf16[256,256]{1,0:T(8,128)(2,1)S(1)}, bf16[256,256]{1,0:T(8,128)(2,1)}, u32[]{:S(2)}) copy-start(bf16[256,256]{1,0:T(8,128)(2,1)} %pre_ref.1) | copy-start | bytes 393220
  31.5 18.8 %copy-start.2 = (bf16[256,256]{1,0:T(8,128)(2,1)S(1)}, bf16[256,256]{1,0:T(8,128)(2,1)}, u32[]{:S(2)}) copy-start(bf16[256,256]{1,0:T(8,128)(2,1)} %post_ref.1) | copy-start | bytes 393220
  31.5 18.8 %all-to-all-start.1 = ((bf16[32,8,256]{2,1,0:T(8,128)(2,1)}), bf16[32,8,256]{2,1,0:T(8,128)(2,1)S(1)}, u32[]{:S(2)}, u32[]{:S(2)}) async-start(bf16[32,8,256]{2,1,0:T(8,128)(2,1)} %bitcast.3), calls=%async_computation.1 | async-start | bytes 262144 | tf_op jit(solution)/shard_map/all_to_all | solution.py:347
  59.6 13.9 %collective-permute-start.3 = (bf16[256,256]{1,0:T(8,128)(2,1)S(1)}, bf16[256,256]{1,0:T(8,128)(2,1)S(1)}, u32[]{:S(2)}, u32[]{:S(2)}) collective-permute-start(bf16[256,256]{1,0:T(8,128)(2,1)S(1)} %get-tuple-element.17), channel_id=1, source_target_pairs={{0,10},{1,11},{2,8},{3,9},{4,14},{5,15},{6,12},{7,13},{8,2},{9,3},... | collective-permute-start | bytes 393224 | tf_op jit(solution)/shard_map/ppermute | solution.py:33
  66.2 9.8 %collective-permute-start.4 = (bf16[256,256]{1,0:T(8,128)(2,1)S(1)}, bf16[256,256]{1,0:T(8,128)(2,1)S(1)}, u32[]{:S(2)}, u32[]{:S(2)}) collective-permute-start(bf16[256,256]{1,0:T(8,128)(2,1)S(1)} %get-tuple-element.18), channel_id=1, source_target_pairs={{0,12},{1,13},{2,6},{3,7},{4,0},{5,1},{6,10},{7,11},{8,4},{9,5},{1... | collective-permute-start | bytes 393224 | tf_op jit(solution)/shard_map/ppermute | solution.py:33
  69.1 8.9 %collective-permute-start.5 = (bf16[256,256]{1,0:T(8,128)(2,1)S(1)}, bf16[256,256]{1,0:T(8,128)(2,1)S(1)}, u32[]{:S(2)}, u32[]{:S(2)}) collective-permute-start(bf16[256,256]{1,0:T(8,128)(2,1)S(1)} %get-tuple-element.19), channel_id=1, source_target_pairs={{0,14},{1,15},{2,4},{3,5},{4,2},{5,3},{6,8},{7,9},{8,6},{9,7},{10,... | collective-permute-start | bytes 393224 | tf_op jit(solution)/shard_map/ppermute | solution.py:33

commit v11 on v10

--- a/solution.py
+++ b/solution.py
@@ -373,7 +373,7 @@
     tables = dft_tables(devices, tokens_here, channels)
     convolved = convolve(blocks, channels, tables, arranged)
     convolved = exchange(convolved, devices).reshape(channels_here, tokens_here)
-    mixed = gate(post_gate, signal, pre_gate, convolved, skip_gain, pieces)
+    mixed = gate(post_gate, signal, pre_gate, convolved, skip_gain, pieces[1:] + pieces[:1])
     gathered = lax.all_gather(mixed, GROUP, axis=0, tiled=True)
     shares = project(place, gathered, [own] + pieces, width)
     return finish([send_to_target(shares[step], step, quads) for step in range(3)] + [shares[3]])

time: 79.3 us -> 77 us (0.971)
  waiting for transfers between devices: 11.7 us -> 9.37 us
    ppermute x3, waiting for transfers between devices: 7.24 us -> 4.69 us  [per_device(): lax.ppermute(piece, GROUP, [(t, t ^ r) for t in range(group)])]
where the time goes in v11:
time: 77 us; the launch traced here: 76.4 us
  starting transfers between devices  46.8 us (61%)
  Pallas kernels  12.1 us (16%)
  waiting for transfers between devices  9.37 us (12%)
  blocking collectives  7.63 us (10%)
    all_to_all x2, starting transfers between devices, exchange(): lax.all_to_all(parts, 'ctx', split_axis=0, concat_axis=0, axis_index_grou...  24.9 us
    ppermute x3, starting transfers between devices, send_to_target(): return lax.ppermute(share, TP_AXES, pairs)  13.6 us
    ppermute x3, starting transfers between devices, per_device(): lax.ppermute(piece, GROUP, [(t, t ^ r) for t in range(group)])  8.32 us
    all_gather x1, blocking collectives, per_device(): gathered = lax.all_gather(mixed, GROUP, axis=0, tiled=True)  7.63 us
    ppermute x3, waiting for transfers between devices, per_device(): lax.ppermute(piece, GROUP, [(t, t ^ r) for t in range(group)])  4.69 us
    ppermute x3, waiting for transfers between devices, send_to_target(): return lax.ppermute(share, TP_AXES, pairs)  4.68 us
    pallas_call x1, Pallas kernels, arrange(): pl.pallas_call(lambda *refs: arrange_kernel(group, quads, width, members,...  2.96 us
    pallas_call x1, Pallas kernels, convolve(): pl.pallas_call(lambda *refs: convolve_kernel(channels, *refs), out_shape=...  2.63 us
  transfers between devices with their start and end apart: 8, of which 3 were waited for; matrix products, arithmetic and copies ran while one was open for 0% of the time, Pallas kernels for 10%

profile of v11, /device:TPU:1, one launch (start us, length us, event | category | flops | bytes accessed | tf_op | source)
XLA Modules:
  0.0 76.4 jit_solution(15095816615064934180)
XLA Ops:
  0.0 0.0 copy-start.6
  0.0 0.0 copy-start.7
  0.0 0.0 copy-start.3
  0.0 0.0 copy-start.4
  0.0 0.0 copy-start.5
  0.0 0.0 copy-start.8
  0.0 1.9 %shard_map.118 = bf16[512,256]{1,0:T(8,128)(2,1)} custom-call(bf16[256,256]{1,0:T(8,128)(2,1)} %signal_ref.1, bf16[256,256]{1,0:T(8,128)(2,1)} %pre_ref.1, f32[256,256]{1,0:T(8,128)} %refs_2_.2), custom_call_target="tpu_custom_call" | custom-call | tf_op jit(solution)/shard_map/pallas_call | solution.py:308
  1.9 15.5 %all-to-all-start = ((bf16[32,16,256]{2,1,0:T(8,128)(2,1)}), bf16[32,16,256]{2,1,0:T(8,128)(2,1)S(1)}, u32[]{:S(2)}, u32[]{:S(2)}) async-start(bf16[32,16,256]{2,1,0:T(8,128)(2,1)} %bitcast.8), calls=%async_computation | async-start | bytes 524288 | tf_op jit(solution)/shard_map/all_to_all | solution.py:347
  17.5 3.0 %shard_map.119 = (bf16[256,1024]{1,0:T(8,128)(2,1)}, bf16[256,1024]{1,0:T(8,128)(2,1)}, bf16[256,1024]{1,0:T(8,128)(2,1)}, s32[1]{0:T(128)}) custom-call(s32[1]{0:T(128)} %bitcast.refs_0_, bf16[256,4096]{1,0:T(8,128)(2,1)} %refs_1_.6), custom_call_target="tpu_custom_call" | custom-call | bytes 3145728 | tf_op jit(solution)/shard_map/pallas_call | solution.py:71
  20.4 3.2 %collective-permute-start = (bf16[256,1024]{1,0:T(8,128)(2,1)}, bf16[256,1024]{1,0:T(8,128)(2,1)S(1)}, u32[]{:S(2)}, u32[]{:S(2)}) collective-permute-start(bf16[256,1024]{1,0:T(8,128)(2,1)} %get-tuple-element.14), channel_id=1, source_target_pairs={{0,2},{1,3},{2,0},{3,1},{4,6},{5,7},{6,4},{7,5},{8,10},{9,11},{10,... | collective-permute-start | bytes 1572872 | tf_op jit(solution)/shard_map/ppermute | solution.py:368
  23.7 3.2 %collective-permute-start.1 = (bf16[256,1024]{1,0:T(8,128)(2,1)}, bf16[256,1024]{1,0:T(8,128)(2,1)S(1)}, u32[]{:S(2)}, u32[]{:S(2)}) collective-permute-start(bf16[256,1024]{1,0:T(8,128)(2,1)} %get-tuple-element.15), channel_id=1, source_target_pairs={{0,3},{1,2},{2,1},{3,0},{4,7},{5,6},{6,5},{7,4},{8,11},{9,10},{10,... | collective-permute-start | bytes 1572872 | tf_op jit(solution)/shard_map/ppermute | solution.py:368
  26.9 1.9 %collective-permute-start.2 = (bf16[256,1024]{1,0:T(8,128)(2,1)}, bf16[256,1024]{1,0:T(8,128)(2,1)S(1)}, u32[]{:S(2)}, u32[]{:S(2)}) collective-permute-start(bf16[256,1024]{1,0:T(8,128)(2,1)} %get-tuple-element.16), channel_id=1, source_target_pairs={{0,1},{1,0},{2,3},{3,2},{4,5},{5,4},{6,7},{7,6},{8,9},{9,8},{10,11... | collective-permute-start | bytes 1572872 | tf_op jit(solution)/shard_map/ppermute | solution.py:368
  28.8 0.0 all-to-all-done
  28.8 0.0 copy-done.6
  28.8 0.0 copy-done.7
  28.8 0.0 copy-done.3
  28.8 0.0 copy-done.4
  28.8 0.0 copy-done.5
  28.9 0.0 copy-done.8
  28.9 2.6 %shard_map.120 = bf16[256,256]{1,0:T(8,128)(2,1)} custom-call(bf16[512,256]{1,0:T(8,128)(2,1)S(1)} %bitcast.7, bf16[66,32]{1,0:T(8,128)(2,1)S(1)} %copy-done.8, bf16[256,256]{1,0:T(8,128)(2,1)S(1)} %copy-done.5, bf16[256,256]{1,0:T(8,128)(2,1)S(1)} %copy-done.4, bf16[256,528]{1,0:T(8,128)(2,1)S(1)} %copy-done.3, f32[33,256]{1,0:T(8,128)S(1)} %copy-done.7, ...), custom_call_target="tpu_custom_call" | custom-call | flops 800000000 | bytes 3000000 | tf_op jit(solution)/shard_map/pallas_call | solution.py:268
  31.5 0.0 copy-start.9
  31.5 0.0 copy-start
  31.5 0.0 copy-start.1
  31.5 0.0 copy-start.2
  31.5 9.4 %all-to-all-start.1 = ((bf16[32,8,256]{2,1,0:T(8,128)(2,1)}), bf16[32,8,256]{2,1,0:T(8,128)(2,1)S(1)}, u32[]{:S(2)}, u32[]{:S(2)}) async-start(bf16[32,8,256]{2,1,0:T(8,128)(2,1)} %bitcast.3), calls=%async_computation.1 | async-start | bytes 262144 | tf_op jit(solution)/shard_map/all_to_all | solution.py:347
  40.9 2.0 %shard_map.122.refs_2_ = bf16[256,1024]{1,0:T(8,128)(2,1)} custom-call(s32[1]{0:T(128)} %bitcast.refs_0_, bf16[256,4096]{1,0:T(8,128)(2,1)} %refs_1_.6), custom_call_target="tpu_custom_call" | custom-call | bytes 1048576 | tf_op jit(solution)/shard_map/pallas_call | solution.py:114
  42.9 0.0 copy-done.9
  42.9 0.1 copy.13.gain_ref
  43.0 0.0 collective-permute-done.refs_4_
  43.0 4.7 %collective-permute-done.1.refs_5_ = bf16[256,1024]{1,0:T(8,128)(2,1)S(1)} collective-permute-done((bf16[256,1024]{1,0:T(8,128)(2,1)}, bf16[256,1024]{1,0:T(8,128)(2,1)S(1)}, u32[]{:S(2)}, u32[]{:S(2)}) %collective-permute-start.1) | collective-permute-done | bytes 524320 | tf_op jit(solution)/shard_map/ppermute | solution.py:368
  47.7 0.0 collective-permute-done.2.refs_3_
  47.8 0.0 all-to-all-done.1
  47.8 0.0 copy-done
  47.8 0.0 copy-done.1
  47.8 0.0 copy-done.2
  47.8 0.2 shard_map.121
  48.0 7.6 %all_gather.3.refs_1_ = bf16[1024,256]{1,0:T(8,128)(2,1)S(1)} all-gather(bf16[256,256]{1,0:T(8,128)(2,1)S(1)} %shard_map.121), channel_id=1, replica_groups=mesh['ctx'=32,'quad'=4,'pair'=2,'core'=2] {'pair','core'}, dimensions={0}, use_global_device_ids=true | all-gather | bytes 655360 | tf_op jit(solution)/shard_map/all_gather | solution.py:377
  55.6 1.7 %shard_map.123 = (bf16[256,256]{1,0:T(8,128)(2,1)S(1)}, bf16[256,256]{1,0:T(8,128)(2,1)S(1)}, bf16[256,256]{1,0:T(8,128)(2,1)S(1)}, bf16[256,256]{1,0:T(8,128)(2,1)S(1)}) custom-call(s32[1]{0:T(128)} %bitcast.refs_0_, bf16[1024,256]{1,0:T(8,128)(2,1)S(1)} %all_gather.3.refs_1_, bf16[256,1024]{1,0:T(8,128)(2,1)} %shard_map.122.refs_2_, ...), custom_call_target="tpu_custom_call" | custom-call | flops 536870912 | bytes 3145728 | tf_op jit(solution)/shard_map/pallas_call | solution.py:156
  57.3 6.4 %collective-permute-start.3 = (bf16[256,256]{1,0:T(8,128)(2,1)S(1)}, bf16[256,256]{1,0:T(8,128)(2,1)S(1)}, u32[]{:S(2)}, u32[]{:S(2)}) collective-permute-start(bf16[256,256]{1,0:T(8,128)(2,1)S(1)} %get-tuple-element.17), channel_id=1, source_target_pairs={{0,10},{1,11},{2,8},{3,9},{4,14},{5,15},{6,12},{7,13},{8,2},{9,3},... | collective-permute-start | bytes 393224 | tf_op jit(solution)/shard_map/ppermute | solution.py:33
  63.8 2.7 %collective-permute-start.4 = (bf16[256,256]{1,0:T(8,128)(2,1)S(1)}, bf16[256,256]{1,0:T(8,128)(2,1)S(1)}, u32[]{:S(2)}, u32[]{:S(2)}) collective-permute-start(bf16[256,256]{1,0:T(8,128)(2,1)S(1)} %get-tuple-element.18), channel_id=1, source_target_pairs={{0,12},{1,13},{2,6},{3,7},{4,0},{5,1},{6,10},{7,11},{8,4},{9,5},{1... | collective-permute-start | bytes 393224 | tf_op jit(solution)/shard_map/ppermute | solution.py:33
  66.5 4.4 %collective-permute-start.5 = (bf16[256,256]{1,0:T(8,128)(2,1)S(1)}, bf16[256,256]{1,0:T(8,128)(2,1)S(1)}, u32[]{:S(2)}, u32[]{:S(2)}) collective-permute-start(bf16[256,256]{1,0:T(8,128)(2,1)S(1)} %get-tuple-element.19), channel_id=1, source_target_pairs={{0,14},{1,15},{2,4},{3,5},{4,2},{5,3},{6,8},{7,9},{8,6},{9,7},{10,... | collective-permute-start | bytes 393224 | tf_op jit(solution)/shard_map/ppermute | solution.py:33
  71.0 0.0 collective-permute-done.3.refs_0_
  71.0 2.7 %collective-permute-done.4.refs_1_ = bf16[256,256]{1,0:T(8,128)(2,1)S(1)} collective-permute-done((bf16[256,256]{1,0:T(8,128)(2,1)S(1)}, bf16[256,256]{1,0:T(8,128)(2,1)S(1)}, u32[]{:S(2)}, u32[]{:S(2)}) %collective-permute-start.4) | collective-permute-done | bytes 131104 | tf_op jit(solution)/shard_map/ppermute | solution.py:33
  73.7 2.0 %collective-permute-done.5.refs_2_ = bf16[256,256]{1,0:T(8,128)(2,1)S(1)} collective-permute-done((bf16[256,256]{1,0:T(8,128)(2,1)S(1)}, bf16[256,256]{1,0:T(8,128)(2,1)S(1)}, u32[]{:S(2)}, u32[]{:S(2)}) %collective-permute-start.5) | collective-permute-done | bytes 131104 | tf_op jit(solution)/shard_map/ppermute | solution.py:33
  75.7 0.8 %shard_map.124 = bf16[256,256]{1,0:T(8,128)(2,1)} custom-call(bf16[256,256]{1,0:T(8,128)(2,1)S(1)} %collective-permute-done.3.refs_0_, bf16[256,256]{1,0:T(8,128)(2,1)S(1)} %collective-permute-done.4.refs_1_, bf16[256,256]{1,0:T(8,128)(2,1)S(1)} %collective-permute-done.5.refs_2_, bf16[256,256]{1,0:T(8,128)(2,1)S(1)} %get-tuple-element.20.refs_3_), custom_call_target="tpu_custom_call" | custom-call | tf_op jit(solution)/shard_map/pallas_call | solution.py:185
  (4 shorter events, 0.0 us)
Async XLA Ops:
  0.0 28.8 %copy-start.6 = (f32[33,256]{1,0:T(8,128)S(1)}, f32[33,256]{1,0:T(8,128)}, u32[]{:S(2)}) copy-start(f32[33,256]{1,0:T(8,128)} %constant.32.clone.refs_6_) | copy-start | bytes 101380
  0.0 28.8 %copy-start.7 = (f32[33,256]{1,0:T(8,128)S(1)}, f32[33,256]{1,0:T(8,128)}, u32[]{:S(2)}) copy-start(f32[33,256]{1,0:T(8,128)} %constant.31.clone.refs_5_) | copy-start | bytes 101380
  0.0 28.8 %copy-start.3 = (bf16[256,528]{1,0:T(8,128)(2,1)S(1)}, bf16[256,528]{1,0:T(8,128)(2,1)}, u32[]{:S(2)}) copy-start(bf16[256,528]{1,0:T(8,128)(2,1)} %constant.30.clone.refs_4_) | copy-start | bytes 811012
  0.0 28.8 %copy-start.4 = (bf16[256,256]{1,0:T(8,128)(2,1)S(1)}, bf16[256,256]{1,0:T(8,128)(2,1)}, u32[]{:S(2)}) copy-start(bf16[256,256]{1,0:T(8,128)(2,1)} %constant.29.clone.refs_3_) | copy-start | bytes 393220
  0.0 28.8 %copy-start.5 = (bf16[256,256]{1,0:T(8,128)(2,1)S(1)}, bf16[256,256]{1,0:T(8,128)(2,1)}, u32[]{:S(2)}) copy-start(bf16[256,256]{1,0:T(8,128)(2,1)} %constant.28.clone.refs_2_) | copy-start | bytes 393220
  0.0 28.8 %copy-start.8 = (bf16[66,32]{1,0:T(8,128)(2,1)S(1)}, bf16[66,32]{1,0:T(8,128)(2,1)}, u32[]{:S(2)}) copy-start(bf16[66,32]{1,0:T(8,128)(2,1)} %constant.27.clone.refs_1_) | copy-start | bytes 12676
  1.9 26.8 %all-to-all-start = ((bf16[32,16,256]{2,1,0:T(8,128)(2,1)}), bf16[32,16,256]{2,1,0:T(8,128)(2,1)S(1)}, u32[]{:S(2)}, u32[]{:S(2)}) async-start(bf16[32,16,256]{2,1,0:T(8,128)(2,1)} %bitcast.8), calls=%async_computation | async-start | bytes 524288 | tf_op jit(solution)/shard_map/all_to_all | solution.py:347
  20.4 22.6 %collective-permute-start = (bf16[256,1024]{1,0:T(8,128)(2,1)}, bf16[256,1024]{1,0:T(8,128)(2,1)S(1)}, u32[]{:S(2)}, u32[]{:S(2)}) collective-permute-start(bf16[256,1024]{1,0:T(8,128)(2,1)} %get-tuple-element.14), channel_id=1, source_target_pairs={{0,2},{1,3},{2,0},{3,1},{4,6},{5,7},{6,4},{7,5},{8,10},{9,11},{10,... | collective-permute-start | bytes 1572872 | tf_op jit(solution)/shard_map/ppermute | solution.py:368
  23.7 24.1 %collective-permute-start.1 = (bf16[256,1024]{1,0:T(8,128)(2,1)}, bf16[256,1024]{1,0:T(8,128)(2,1)S(1)}, u32[]{:S(2)}, u32[]{:S(2)}) collective-permute-start(bf16[256,1024]{1,0:T(8,128)(2,1)} %get-tuple-element.15), channel_id=1, source_target_pairs={{0,3},{1,2},{2,1},{3,0},{4,7},{5,6},{6,5},{7,4},{8,11},{9,10},{10,... | collective-permute-start | bytes 1572872 | tf_op jit(solution)/shard_map/ppermute | solution.py:368
  26.9 20.9 %collective-permute-start.2 = (bf16[256,1024]{1,0:T(8,128)(2,1)}, bf16[256,1024]{1,0:T(8,128)(2,1)S(1)}, u32[]{:S(2)}, u32[]{:S(2)}) collective-permute-start(bf16[256,1024]{1,0:T(8,128)(2,1)} %get-tuple-element.16), channel_id=1, source_target_pairs={{0,1},{1,0},{2,3},{3,2},{4,5},{5,4},{6,7},{7,6},{8,9},{9,8},{10,11... | collective-permute-start | bytes 1572872 | tf_op jit(solution)/shard_map/ppermute | solution.py:368
  31.5 11.4 %copy-start.9 = (f32[256]{0:T(256)S(1)}, f32[256]{0:T(256)}, u32[]{:S(2)}) copy-start(f32[256]{0:T(256)} %param.16) | copy-start | bytes 3076
  31.5 16.3 %copy-start = (bf16[256,256]{1,0:T(8,128)(2,1)S(1)}, bf16[256,256]{1,0:T(8,128)(2,1)}, u32[]{:S(2)}) copy-start(bf16[256,256]{1,0:T(8,128)(2,1)} %signal_ref.1) | copy-start | bytes 393220
  31.5 16.3 %copy-start.1 = (bf16[256,256]{1,0:T(8,128)(2,1)S(1)}, bf16[256,256]{1,0:T(8,128)(2,1)}, u32[]{:S(2)}) copy-start(bf16[256,256]{1,0:T(8,128)(2,1)} %pre_ref.1) | copy-start | bytes 393220
  31.5 16.3 %copy-start.2 = (bf16[256,256]{1,0:T(8,128)(2,1)S(1)}, bf16[256,256]{1,0:T(8,128)(2,1)}, u32[]{:S(2)}) copy-start(bf16[256,256]{1,0:T(8,128)(2,1)} %post_ref.1) | copy-start | bytes 393220
  31.5 16.2 %all-to-all-start.1 = ((bf16[32,8,256]{2,1,0:T(8,128)(2,1)}), bf16[32,8,256]{2,1,0:T(8,128)(2,1)S(1)}, u32[]{:S(2)}, u32[]{:S(2)}) async-start(bf16[32,8,256]{2,1,0:T(8,128)(2,1)} %bitcast.3), calls=%async_computation.1 | async-start | bytes 262144 | tf_op jit(solution)/shard_map/all_to_all | solution.py:347
  57.3 13.6 %collective-permute-start.3 = (bf16[256,256]{1,0:T(8,128)(2,1)S(1)}, bf16[256,256]{1,0:T(8,128)(2,1)S(1)}, u32[]{:S(2)}, u32[]{:S(2)}) collective-permute-start(bf16[256,256]{1,0:T(8,128)(2,1)S(1)} %get-tuple-element.17), channel_id=1, source_target_pairs={{0,10},{1,11},{2,8},{3,9},{4,14},{5,15},{6,12},{7,13},{8,2},{9,3},... | collective-permute-start | bytes 393224 | tf_op jit(solution)/shard_map/ppermute | solution.py:33
  63.8 9.9 %collective-permute-start.4 = (bf16[256,256]{1,0:T(8,128)(2,1)S(1)}, bf16[256,256]{1,0:T(8,128)(2,1)S(1)}, u32[]{:S(2)}, u32[]{:S(2)}) collective-permute-start(bf16[256,256]{1,0:T(8,128)(2,1)S(1)} %get-tuple-element.18), channel_id=1, source_target_pairs={{0,12},{1,13},{2,6},{3,7},{4,0},{5,1},{6,10},{7,11},{8,4},{9,5},{1... | collective-permute-start | bytes 393224 | tf_op jit(solution)/shard_map/ppermute | solution.py:33
  66.5 9.1 %collective-permute-start.5 = (bf16[256,256]{1,0:T(8,128)(2,1)S(1)}, bf16[256,256]{1,0:T(8,128)(2,1)S(1)}, u32[]{:S(2)}, u32[]{:S(2)}) collective-permute-start(bf16[256,256]{1,0:T(8,128)(2,1)S(1)} %get-tuple-element.19), channel_id=1, source_target_pairs={{0,14},{1,15},{2,4},{3,5},{4,2},{5,3},{6,8},{7,9},{8,6},{9,7},{10,... | collective-permute-start | bytes 393224 | tf_op jit(solution)/shard_map/ppermute | solution.py:33

commit v12 on v11

--- a/solution.py
+++ b/solution.py
@@ -191,12 +191,16 @@
     )(*shares)
 
 
+def exchange_order(devices):
+    return [(2 * devices // 3 - n) % devices for n in range(devices)]
+
+
 def dft_tables(blocks, tokens, channels):
     period = 2 * blocks
     total = period * tokens
     low = blocks + 1
     k1 = np.arange(low)
-    i = np.arange(blocks)[::-1]
+    i = np.array(exchange_order(blocks))
     s = np.arange(tokens)
     first = 2 * np.pi * (np.outer(k1, i) % period) / period
     turn = 2 * np.pi * (np.outer(k1, s) % total) / total
@@ -343,9 +347,13 @@
 
 
 def exchange(parts, devices):
-    backwards = [list(range(devices))[::-1]]
     return lax.all_to_all(
-        parts, "ctx", split_axis=0, concat_axis=0, axis_index_groups=backwards, tiled=True
+        parts,
+        "ctx",
+        split_axis=0,
+        concat_axis=0,
+        axis_index_groups=[exchange_order(devices)],
+        tiled=True,
     )
 
 

time: 77 us -> 77.3 us (level)
  starting transfers between devices: 46.8 us -> 47.9 us
where the time goes in v12:
time: 77.3 us; the launch traced here: 76.8 us
  starting transfers between devices  47.9 us (62%)
  Pallas kernels  12.1 us (16%)
  waiting for transfers between devices  9.02 us (12%)
  blocking collectives  7.29 us (9%)
    all_to_all x2, starting transfers between devices, exchange(): lax.all_to_all(parts, 'ctx', split_axis=0, concat_axis=0, axis_index_grou...  25.6 us
    ppermute x3, starting transfers between devices, send_to_target(): return lax.ppermute(share, TP_AXES, pairs)  13.6 us
    ppermute x3, starting transfers between devices, per_device(): lax.ppermute(piece, GROUP, [(t, t ^ r) for t in range(group)])  8.6 us
    all_gather x1, blocking collectives, per_device(): gathered = lax.all_gather(mixed, GROUP, axis=0, tiled=True)  7.29 us
    ppermute x3, waiting for transfers between devices, send_to_target(): return lax.ppermute(share, TP_AXES, pairs)  4.9 us
    ppermute x3, waiting for transfers between devices, per_device(): lax.ppermute(piece, GROUP, [(t, t ^ r) for t in range(group)])  4.11 us
    pallas_call x1, Pallas kernels, arrange(): pl.pallas_call(lambda *refs: arrange_kernel(group, quads, width, members,...  2.96 us
    pallas_call x1, Pallas kernels, convolve(): pl.pallas_call(lambda *refs: convolve_kernel(channels, *refs), out_shape=...  2.64 us
  transfers between devices with their start and end apart: 8, of which 3 were waited for; matrix products, arithmetic and copies ran while one was open for 0% of the time, Pallas kernels for 10%

profile of v12, /device:TPU:1, one launch (start us, length us, event | category | flops | bytes accessed | tf_op | source)
XLA Modules:
  0.0 76.8 jit_solution(1455795927123403930)
XLA Ops:
  0.0 0.0 copy-start.6
  0.0 0.0 copy-start.7
  0.0 0.0 copy-start.3
  0.0 0.0 copy-start.4
  0.0 0.0 copy-start.5
  0.0 0.0 copy-start.8
  0.0 1.9 %shard_map.118 = bf16[512,256]{1,0:T(8,128)(2,1)} custom-call(bf16[256,256]{1,0:T(8,128)(2,1)} %signal_ref.1, bf16[256,256]{1,0:T(8,128)(2,1)} %pre_ref.1, f32[256,256]{1,0:T(8,128)} %refs_2_.2), custom_call_target="tpu_custom_call" | custom-call | tf_op jit(solution)/shard_map/pallas_call | solution.py:312
  1.9 16.2 %all-to-all-start = ((bf16[32,16,256]{2,1,0:T(8,128)(2,1)}), bf16[32,16,256]{2,1,0:T(8,128)(2,1)S(1)}, u32[]{:S(2)}, u32[]{:S(2)}) async-start(bf16[32,16,256]{2,1,0:T(8,128)(2,1)} %bitcast.8), calls=%async_computation | async-start | bytes 524288 | tf_op jit(solution)/shard_map/all_to_all | solution.py:350
  18.2 3.0 %shard_map.119 = (bf16[256,1024]{1,0:T(8,128)(2,1)}, bf16[256,1024]{1,0:T(8,128)(2,1)}, bf16[256,1024]{1,0:T(8,128)(2,1)}, s32[1]{0:T(128)}) custom-call(s32[1]{0:T(128)} %bitcast.refs_0_, bf16[256,4096]{1,0:T(8,128)(2,1)} %refs_1_.6), custom_call_target="tpu_custom_call" | custom-call | bytes 3145728 | tf_op jit(solution)/shard_map/pallas_call | solution.py:71
  21.2 3.2 %collective-permute-start = (bf16[256,1024]{1,0:T(8,128)(2,1)}, bf16[256,1024]{1,0:T(8,128)(2,1)S(1)}, u32[]{:S(2)}, u32[]{:S(2)}) collective-permute-start(bf16[256,1024]{1,0:T(8,128)(2,1)} %get-tuple-element.14), channel_id=1, source_target_pairs={{0,2},{1,3},{2,0},{3,1},{4,6},{5,7},{6,4},{7,5},{8,10},{9,11},{10,... | collective-permute-start | bytes 1572872 | tf_op jit(solution)/shard_map/ppermute | solution.py:376
  24.4 3.5 %collective-permute-start.1 = (bf16[256,1024]{1,0:T(8,128)(2,1)}, bf16[256,1024]{1,0:T(8,128)(2,1)S(1)}, u32[]{:S(2)}, u32[]{:S(2)}) collective-permute-start(bf16[256,1024]{1,0:T(8,128)(2,1)} %get-tuple-element.15), channel_id=1, source_target_pairs={{0,3},{1,2},{2,1},{3,0},{4,7},{5,6},{6,5},{7,4},{8,11},{9,10},{10,... | collective-permute-start | bytes 1572872 | tf_op jit(solution)/shard_map/ppermute | solution.py:376
  27.9 1.9 %collective-permute-start.2 = (bf16[256,1024]{1,0:T(8,128)(2,1)}, bf16[256,1024]{1,0:T(8,128)(2,1)S(1)}, u32[]{:S(2)}, u32[]{:S(2)}) collective-permute-start(bf16[256,1024]{1,0:T(8,128)(2,1)} %get-tuple-element.16), channel_id=1, source_target_pairs={{0,1},{1,0},{2,3},{3,2},{4,5},{5,4},{6,7},{7,6},{8,9},{9,8},{10,11... | collective-permute-start | bytes 1572872 | tf_op jit(solution)/shard_map/ppermute | solution.py:376
  29.8 0.0 all-to-all-done
  29.8 0.0 copy-done.6
  29.8 0.0 copy-done.7
  29.8 0.0 copy-done.3
  29.8 0.0 copy-done.4
  29.8 0.0 copy-done.5
  29.8 0.0 copy-done.8
  29.9 2.6 %shard_map.120 = bf16[256,256]{1,0:T(8,128)(2,1)} custom-call(bf16[512,256]{1,0:T(8,128)(2,1)S(1)} %bitcast.7, bf16[66,32]{1,0:T(8,128)(2,1)S(1)} %copy-done.8, bf16[256,256]{1,0:T(8,128)(2,1)S(1)} %copy-done.5, bf16[256,256]{1,0:T(8,128)(2,1)S(1)} %copy-done.4, bf16[256,528]{1,0:T(8,128)(2,1)S(1)} %copy-done.3, f32[33,256]{1,0:T(8,128)S(1)} %copy-done.7, ...), custom_call_target="tpu_custom_call" | custom-call | flops 800000000 | bytes 3000000 | tf_op jit(solution)/shard_map/pallas_call | solution.py:272
  32.5 0.0 copy-start.9
  32.5 0.0 copy-start
  32.5 0.0 copy-start.1
  32.5 0.0 copy-start.2
  32.5 9.4 %all-to-all-start.1 = ((bf16[32,8,256]{2,1,0:T(8,128)(2,1)}), bf16[32,8,256]{2,1,0:T(8,128)(2,1)S(1)}, u32[]{:S(2)}, u32[]{:S(2)}) async-start(bf16[32,8,256]{2,1,0:T(8,128)(2,1)} %bitcast.3), calls=%async_computation.1 | async-start | bytes 262144 | tf_op jit(solution)/shard_map/all_to_all | solution.py:350
  41.9 2.0 %shard_map.122.refs_2_ = bf16[256,1024]{1,0:T(8,128)(2,1)} custom-call(s32[1]{0:T(128)} %bitcast.refs_0_, bf16[256,4096]{1,0:T(8,128)(2,1)} %refs_1_.6), custom_call_target="tpu_custom_call" | custom-call | bytes 1048576 | tf_op jit(solution)/shard_map/pallas_call | solution.py:114
  43.9 0.0 copy-done.9
  43.9 0.1 copy.13.gain_ref
  44.0 0.0 collective-permute-done.refs_4_
  44.0 4.1 %collective-permute-done.1.refs_5_ = bf16[256,1024]{1,0:T(8,128)(2,1)S(1)} collective-permute-done((bf16[256,1024]{1,0:T(8,128)(2,1)}, bf16[256,1024]{1,0:T(8,128)(2,1)S(1)}, u32[]{:S(2)}, u32[]{:S(2)}) %collective-permute-start.1) | collective-permute-done | bytes 524320 | tf_op jit(solution)/shard_map/ppermute | solution.py:376
  48.1 0.0 collective-permute-done.2.refs_3_
  48.2 0.0 all-to-all-done.1
  48.2 0.0 copy-done
  48.2 0.0 copy-done.1
  48.2 0.0 copy-done.2
  48.2 0.2 shard_map.121
  48.4 7.3 %all_gather.3.refs_1_ = bf16[1024,256]{1,0:T(8,128)(2,1)S(1)} all-gather(bf16[256,256]{1,0:T(8,128)(2,1)S(1)} %shard_map.121), channel_id=1, replica_groups=mesh['ctx'=32,'quad'=4,'pair'=2,'core'=2] {'pair','core'}, dimensions={0}, use_global_device_ids=true | all-gather | bytes 655360 | tf_op jit(solution)/shard_map/all_gather | solution.py:385
  55.7 1.7 %shard_map.123 = (bf16[256,256]{1,0:T(8,128)(2,1)S(1)}, bf16[256,256]{1,0:T(8,128)(2,1)S(1)}, bf16[256,256]{1,0:T(8,128)(2,1)S(1)}, bf16[256,256]{1,0:T(8,128)(2,1)S(1)}) custom-call(s32[1]{0:T(128)} %bitcast.refs_0_, bf16[1024,256]{1,0:T(8,128)(2,1)S(1)} %all_gather.3.refs_1_, bf16[256,1024]{1,0:T(8,128)(2,1)} %shard_map.122.refs_2_, ...), custom_call_target="tpu_custom_call" | custom-call | flops 536870912 | bytes 3145728 | tf_op jit(solution)/shard_map/pallas_call | solution.py:156
  57.4 6.7 %collective-permute-start.3 = (bf16[256,256]{1,0:T(8,128)(2,1)S(1)}, bf16[256,256]{1,0:T(8,128)(2,1)S(1)}, u32[]{:S(2)}, u32[]{:S(2)}) collective-permute-start(bf16[256,256]{1,0:T(8,128)(2,1)S(1)} %get-tuple-element.17), channel_id=1, source_target_pairs={{0,10},{1,11},{2,8},{3,9},{4,14},{5,15},{6,12},{7,13},{8,2},{9,3},... | collective-permute-start | bytes 393224 | tf_op jit(solution)/shard_map/ppermute | solution.py:33
  64.1 2.6 %collective-permute-start.4 = (bf16[256,256]{1,0:T(8,128)(2,1)S(1)}, bf16[256,256]{1,0:T(8,128)(2,1)S(1)}, u32[]{:S(2)}, u32[]{:S(2)}) collective-permute-start(bf16[256,256]{1,0:T(8,128)(2,1)S(1)} %get-tuple-element.18), channel_id=1, source_target_pairs={{0,12},{1,13},{2,6},{3,7},{4,0},{5,1},{6,10},{7,11},{8,4},{9,5},{1... | collective-permute-start | bytes 393224 | tf_op jit(solution)/shard_map/ppermute | solution.py:33
  66.7 4.4 %collective-permute-start.5 = (bf16[256,256]{1,0:T(8,128)(2,1)S(1)}, bf16[256,256]{1,0:T(8,128)(2,1)S(1)}, u32[]{:S(2)}, u32[]{:S(2)}) collective-permute-start(bf16[256,256]{1,0:T(8,128)(2,1)S(1)} %get-tuple-element.19), channel_id=1, source_target_pairs={{0,14},{1,15},{2,4},{3,5},{4,2},{5,3},{6,8},{7,9},{8,6},{9,7},{10,... | collective-permute-start | bytes 393224 | tf_op jit(solution)/shard_map/ppermute | solution.py:33
  71.1 0.0 collective-permute-done.3.refs_0_
  71.1 3.1 %collective-permute-done.4.refs_1_ = bf16[256,256]{1,0:T(8,128)(2,1)S(1)} collective-permute-done((bf16[256,256]{1,0:T(8,128)(2,1)S(1)}, bf16[256,256]{1,0:T(8,128)(2,1)S(1)}, u32[]{:S(2)}, u32[]{:S(2)}) %collective-permute-start.4) | collective-permute-done | bytes 131104 | tf_op jit(solution)/shard_map/ppermute | solution.py:33
  74.2 1.8 %collective-permute-done.5.refs_2_ = bf16[256,256]{1,0:T(8,128)(2,1)S(1)} collective-permute-done((bf16[256,256]{1,0:T(8,128)(2,1)S(1)}, bf16[256,256]{1,0:T(8,128)(2,1)S(1)}, u32[]{:S(2)}, u32[]{:S(2)}) %collective-permute-start.5) | collective-permute-done | bytes 131104 | tf_op jit(solution)/shard_map/ppermute | solution.py:33
  76.0 0.8 %shard_map.124 = bf16[256,256]{1,0:T(8,128)(2,1)} custom-call(bf16[256,256]{1,0:T(8,128)(2,1)S(1)} %collective-permute-done.3.refs_0_, bf16[256,256]{1,0:T(8,128)(2,1)S(1)} %collective-permute-done.4.refs_1_, bf16[256,256]{1,0:T(8,128)(2,1)S(1)} %collective-permute-done.5.refs_2_, bf16[256,256]{1,0:T(8,128)(2,1)S(1)} %get-tuple-element.20.refs_3_), custom_call_target="tpu_custom_call" | custom-call | tf_op jit(solution)/shard_map/pallas_call | solution.py:185
  (4 shorter events, 0.0 us)
Async XLA Ops:
  0.0 29.8 %copy-start.6 = (f32[33,256]{1,0:T(8,128)S(1)}, f32[33,256]{1,0:T(8,128)}, u32[]{:S(2)}) copy-start(f32[33,256]{1,0:T(8,128)} %constant.32.clone.refs_6_) | copy-start | bytes 101380
  0.0 29.8 %copy-start.7 = (f32[33,256]{1,0:T(8,128)S(1)}, f32[33,256]{1,0:T(8,128)}, u32[]{:S(2)}) copy-start(f32[33,256]{1,0:T(8,128)} %constant.31.clone.refs_5_) | copy-start | bytes 101380
  0.0 29.8 %copy-start.3 = (bf16[256,528]{1,0:T(8,128)(2,1)S(1)}, bf16[256,528]{1,0:T(8,128)(2,1)}, u32[]{:S(2)}) copy-start(bf16[256,528]{1,0:T(8,128)(2,1)} %constant.30.clone.refs_4_) | copy-start | bytes 811012
  0.0 29.8 %copy-start.4 = (bf16[256,256]{1,0:T(8,128)(2,1)S(1)}, bf16[256,256]{1,0:T(8,128)(2,1)}, u32[]{:S(2)}) copy-start(bf16[256,256]{1,0:T(8,128)(2,1)} %constant.29.clone.refs_3_) | copy-start | bytes 393220
  0.0 29.8 %copy-start.5 = (bf16[256,256]{1,0:T(8,128)(2,1)S(1)}, bf16[256,256]{1,0:T(8,128)(2,1)}, u32[]{:S(2)}) copy-start(bf16[256,256]{1,0:T(8,128)(2,1)} %constant.28.clone.refs_2_) | copy-start | bytes 393220
  0.0 29.8 %copy-start.8 = (bf16[66,32]{1,0:T(8,128)(2,1)S(1)}, bf16[66,32]{1,0:T(8,128)(2,1)}, u32[]{:S(2)}) copy-start(bf16[66,32]{1,0:T(8,128)(2,1)} %constant.27.clone.refs_1_) | copy-start | bytes 12676
  1.9 27.8 %all-to-all-start = ((bf16[32,16,256]{2,1,0:T(8,128)(2,1)}), bf16[32,16,256]{2,1,0:T(8,128)(2,1)S(1)}, u32[]{:S(2)}, u32[]{:S(2)}) async-start(bf16[32,16,256]{2,1,0:T(8,128)(2,1)} %bitcast.8), calls=%async_computation | async-start | bytes 524288 | tf_op jit(solution)/shard_map/all_to_all | solution.py:350
  21.2 22.9 %collective-permute-start = (bf16[256,1024]{1,0:T(8,128)(2,1)}, bf16[256,1024]{1,0:T(8,128)(2,1)S(1)}, u32[]{:S(2)}, u32[]{:S(2)}) collective-permute-start(bf16[256,1024]{1,0:T(8,128)(2,1)} %get-tuple-element.14), channel_id=1, source_target_pairs={{0,2},{1,3},{2,0},{3,1},{4,6},{5,7},{6,4},{7,5},{8,10},{9,11},{10,... | collective-permute-start | bytes 1572872 | tf_op jit(solution)/shard_map/ppermute | solution.py:376
  24.4 23.8 %collective-permute-start.1 = (bf16[256,1024]{1,0:T(8,128)(2,1)}, bf16[256,1024]{1,0:T(8,128)(2,1)S(1)}, u32[]{:S(2)}, u32[]{:S(2)}) collective-permute-start(bf16[256,1024]{1,0:T(8,128)(2,1)} %get-tuple-element.15), channel_id=1, source_target_pairs={{0,3},{1,2},{2,1},{3,0},{4,7},{5,6},{6,5},{7,4},{8,11},{9,10},{10,... | collective-permute-start | bytes 1572872 | tf_op jit(solution)/shard_map/ppermute | solution.py:376
  27.9 20.3 %collective-permute-start.2 = (bf16[256,1024]{1,0:T(8,128)(2,1)}, bf16[256,1024]{1,0:T(8,128)(2,1)S(1)}, u32[]{:S(2)}, u32[]{:S(2)}) collective-permute-start(bf16[256,1024]{1,0:T(8,128)(2,1)} %get-tuple-element.16), channel_id=1, source_target_pairs={{0,1},{1,0},{2,3},{3,2},{4,5},{5,4},{6,7},{7,6},{8,9},{9,8},{10,11... | collective-permute-start | bytes 1572872 | tf_op jit(solution)/shard_map/ppermute | solution.py:376
  32.5 11.4 %copy-start.9 = (f32[256]{0:T(256)S(1)}, f32[256]{0:T(256)}, u32[]{:S(2)}) copy-start(f32[256]{0:T(256)} %param.16) | copy-start | bytes 3076
  32.5 15.7 %copy-start = (bf16[256,256]{1,0:T(8,128)(2,1)S(1)}, bf16[256,256]{1,0:T(8,128)(2,1)}, u32[]{:S(2)}) copy-start(bf16[256,256]{1,0:T(8,128)(2,1)} %signal_ref.1) | copy-start | bytes 393220
  32.5 15.7 %copy-start.1 = (bf16[256,256]{1,0:T(8,128)(2,1)S(1)}, bf16[256,256]{1,0:T(8,128)(2,1)}, u32[]{:S(2)}) copy-start(bf16[256,256]{1,0:T(8,128)(2,1)} %pre_ref.1) | copy-start | bytes 393220
  32.5 15.7 %copy-start.2 = (bf16[256,256]{1,0:T(8,128)(2,1)S(1)}, bf16[256,256]{1,0:T(8,128)(2,1)}, u32[]{:S(2)}) copy-start(bf16[256,256]{1,0:T(8,128)(2,1)} %post_ref.1) | copy-start | bytes 393220
  32.5 15.7 %all-to-all-start.1 = ((bf16[32,8,256]{2,1,0:T(8,128)(2,1)}), bf16[32,8,256]{2,1,0:T(8,128)(2,1)S(1)}, u32[]{:S(2)}, u32[]{:S(2)}) async-start(bf16[32,8,256]{2,1,0:T(8,128)(2,1)} %bitcast.3), calls=%async_computation.1 | async-start | bytes 262144 | tf_op jit(solution)/shard_map/all_to_all | solution.py:350
  57.4 13.7 %collective-permute-start.3 = (bf16[256,256]{1,0:T(8,128)(2,1)S(1)}, bf16[256,256]{1,0:T(8,128)(2,1)S(1)}, u32[]{:S(2)}, u32[]{:S(2)}) collective-permute-start(bf16[256,256]{1,0:T(8,128)(2,1)S(1)} %get-tuple-element.17), channel_id=1, source_target_pairs={{0,10},{1,11},{2,8},{3,9},{4,14},{5,15},{6,12},{7,13},{8,2},{9,3},... | collective-permute-start | bytes 393224 | tf_op jit(solution)/shard_map/ppermute | solution.py:33
  64.1 10.1 %collective-permute-start.4 = (bf16[256,256]{1,0:T(8,128)(2,1)S(1)}, bf16[256,256]{1,0:T(8,128)(2,1)S(1)}, u32[]{:S(2)}, u32[]{:S(2)}) collective-permute-start(bf16[256,256]{1,0:T(8,128)(2,1)S(1)} %get-tuple-element.18), channel_id=1, source_target_pairs={{0,12},{1,13},{2,6},{3,7},{4,0},{5,1},{6,10},{7,11},{8,4},{9,5},{1... | collective-permute-start | bytes 393224 | tf_op jit(solution)/shard_map/ppermute | solution.py:33
  66.7 9.3 %collective-permute-start.5 = (bf16[256,256]{1,0:T(8,128)(2,1)S(1)}, bf16[256,256]{1,0:T(8,128)(2,1)S(1)}, u32[]{:S(2)}, u32[]{:S(2)}) collective-permute-start(bf16[256,256]{1,0:T(8,128)(2,1)S(1)} %get-tuple-element.19), channel_id=1, source_target_pairs={{0,14},{1,15},{2,4},{3,5},{4,2},{5,3},{6,8},{7,9},{8,6},{9,7},{10,... | collective-permute-start | bytes 393224 | tf_op jit(solution)/shard_map/ppermute | solution.py:33

commit v13 on v11

--- a/solution.py
+++ b/solution.py
@@ -128,9 +128,16 @@
 
 
 def project_kernel(group, place_ref, mixed_ref, own_hbm, *refs):
-    out_refs, own_ref, sem = refs[group - 1 : -2], refs[-2], refs[-1]
-    load = pltpu.make_async_copy(own_hbm, own_ref, sem)
-    load.start()
+    out_refs, own_ref, sems = refs[group - 1 : -2], refs[-2], refs[-1]
+    step = own_ref.shape[1] // group
+    loads = [
+        pltpu.make_async_copy(
+            own_hbm.at[:, pl.ds(i * step, step)], own_ref.at[:, pl.ds(i * step, step)], sems.at[i]
+        )
+        for i in range(group)
+    ]
+    for load in loads:
+        load.start()
     weight_refs = (own_ref,) + refs[: group - 1]
     tokens = mixed_ref.shape[0] // group
     width = out_refs[0].shape[1]
@@ -144,10 +151,14 @@
         weights = weight_refs[r][:, i * width : (i + 1) * width]
         return jnp.dot(mixed[r], weights, preferred_element_type=jnp.float32)
 
-    totals = [sum(product(r, i) for r in range(1, group)) for i in range(group)]
-    load.wait()
-    for i in range(group):
-        out_refs[i][...] = (totals[i] + product(0, i)).astype(out_refs[i].dtype)
+    totals = {}
+    for i in range(group + 2):
+        if i < group:
+            totals[i] = sum(product(r, i) for r in range(1, group))
+        if i >= 2:
+            loads[i - 2].wait()
+            total = totals.pop(i - 2) + product(0, i - 2)
+            out_refs[i - 2][...] = total.astype(out_refs[i - 2].dtype)
 
 
 def project(place, mixed, weights, width):
@@ -162,7 +173,7 @@
         out_specs=[pl.BlockSpec(memory_space=pltpu.VMEM)] * group,
         scratch_shapes=[
             pltpu.VMEM(weights[0].shape, weights[0].dtype),
-            pltpu.SemaphoreType.DMA,
+            pltpu.SemaphoreType.DMA((group,)),
         ],
         compiler_params=pltpu.CompilerParams(vmem_limit_bytes=10 * MIB),
         cost_estimate=pl.CostEstimate(

time: 77 us -> 77.4 us (level)
  no operation moved by 1% of the time
where the time goes in v13:
time: 77.4 us; the launch traced here: 76.9 us
  starting transfers between devices  46.8 us (60%)
  Pallas kernels  12.6 us (16%)
  waiting for transfers between devices  9.38 us (12%)
  blocking collectives  7.63 us (10%)
    all_to_all x2, starting transfers between devices, exchange(): lax.all_to_all(parts, 'ctx', split_axis=0, concat_axis=0, axis_index_grou...  24.9 us
    ppermute x3, starting transfers between devices, send_to_target(): return lax.ppermute(share, TP_AXES, pairs)  13.6 us
    ppermute x3, starting transfers between devices, per_device(): lax.ppermute(piece, GROUP, [(t, t ^ r) for t in range(group)])  8.32 us
    all_gather x1, blocking collectives, per_device(): gathered = lax.all_gather(mixed, GROUP, axis=0, tiled=True)  7.63 us
    ppermute x3, waiting for transfers between devices, per_device(): lax.ppermute(piece, GROUP, [(t, t ^ r) for t in range(group)])  4.69 us
    ppermute x3, waiting for transfers between devices, send_to_target(): return lax.ppermute(share, TP_AXES, pairs)  4.68 us
    pallas_call x1, Pallas kernels, arrange(): pl.pallas_call(lambda *refs: arrange_kernel(group, quads, width, members,...  2.96 us
    pallas_call x1, Pallas kernels, convolve(): pl.pallas_call(lambda *refs: convolve_kernel(channels, *refs), out_shape=...  2.63 us
  transfers between devices with their start and end apart: 8, of which 3 were waited for; matrix products, arithmetic and copies ran while one was open for 0% of the time, Pallas kernels for 10%

profile of v13, /device:TPU:1, one launch (start us, length us, event | category | flops | bytes accessed | tf_op | source)
XLA Modules:
  0.0 76.9 jit_solution(15554685765417420902)
XLA Ops:
  0.0 0.0 copy-start.6
  0.0 0.0 copy-start.7
  0.0 0.0 copy-start.3
  0.0 0.0 copy-start.4
  0.0 0.0 copy-start.5
  0.0 0.0 copy-start.8
  0.0 1.9 %shard_map.118 = bf16[512,256]{1,0:T(8,128)(2,1)} custom-call(bf16[256,256]{1,0:T(8,128)(2,1)} %signal_ref.1, bf16[256,256]{1,0:T(8,128)(2,1)} %pre_ref.1, f32[256,256]{1,0:T(8,128)} %refs_2_.2), custom_call_target="tpu_custom_call" | custom-call | tf_op jit(solution)/shard_map/pallas_call | solution.py:319
  1.9 15.5 %all-to-all-start = ((bf16[32,16,256]{2,1,0:T(8,128)(2,1)}), bf16[32,16,256]{2,1,0:T(8,128)(2,1)S(1)}, u32[]{:S(2)}, u32[]{:S(2)}) async-start(bf16[32,16,256]{2,1,0:T(8,128)(2,1)} %bitcast.8), calls=%async_computation | async-start | bytes 524288 | tf_op jit(solution)/shard_map/all_to_all | solution.py:358
  17.5 3.0 %shard_map.119 = (bf16[256,1024]{1,0:T(8,128)(2,1)}, bf16[256,1024]{1,0:T(8,128)(2,1)}, bf16[256,1024]{1,0:T(8,128)(2,1)}, s32[1]{0:T(128)}) custom-call(s32[1]{0:T(128)} %bitcast.refs_0_, bf16[256,4096]{1,0:T(8,128)(2,1)} %refs_1_.6), custom_call_target="tpu_custom_call" | custom-call | bytes 3145728 | tf_op jit(solution)/shard_map/pallas_call | solution.py:71
  20.4 3.2 %collective-permute-start = (bf16[256,1024]{1,0:T(8,128)(2,1)}, bf16[256,1024]{1,0:T(8,128)(2,1)S(1)}, u32[]{:S(2)}, u32[]{:S(2)}) collective-permute-start(bf16[256,1024]{1,0:T(8,128)(2,1)} %get-tuple-element.14), channel_id=1, source_target_pairs={{0,2},{1,3},{2,0},{3,1},{4,6},{5,7},{6,4},{7,5},{8,10},{9,11},{10,... | collective-permute-start | bytes 1572872 | tf_op jit(solution)/shard_map/ppermute | solution.py:379
  23.7 3.2 %collective-permute-start.1 = (bf16[256,1024]{1,0:T(8,128)(2,1)}, bf16[256,1024]{1,0:T(8,128)(2,1)S(1)}, u32[]{:S(2)}, u32[]{:S(2)}) collective-permute-start(bf16[256,1024]{1,0:T(8,128)(2,1)} %get-tuple-element.15), channel_id=1, source_target_pairs={{0,3},{1,2},{2,1},{3,0},{4,7},{5,6},{6,5},{7,4},{8,11},{9,10},{10,... | collective-permute-start | bytes 1572872 | tf_op jit(solution)/shard_map/ppermute | solution.py:379
  26.9 1.9 %collective-permute-start.2 = (bf16[256,1024]{1,0:T(8,128)(2,1)}, bf16[256,1024]{1,0:T(8,128)(2,1)S(1)}, u32[]{:S(2)}, u32[]{:S(2)}) collective-permute-start(bf16[256,1024]{1,0:T(8,128)(2,1)} %get-tuple-element.16), channel_id=1, source_target_pairs={{0,1},{1,0},{2,3},{3,2},{4,5},{5,4},{6,7},{7,6},{8,9},{9,8},{10,11... | collective-permute-start | bytes 1572872 | tf_op jit(solution)/shard_map/ppermute | solution.py:379
  28.8 0.0 all-to-all-done
  28.8 0.0 copy-done.6
  28.8 0.0 copy-done.7
  28.8 0.0 copy-done.3
  28.8 0.0 copy-done.4
  28.8 0.0 copy-done.5
  28.9 0.0 copy-done.8
  28.9 2.6 %shard_map.120 = bf16[256,256]{1,0:T(8,128)(2,1)} custom-call(bf16[512,256]{1,0:T(8,128)(2,1)S(1)} %bitcast.7, bf16[66,32]{1,0:T(8,128)(2,1)S(1)} %copy-done.8, bf16[256,256]{1,0:T(8,128)(2,1)S(1)} %copy-done.5, bf16[256,256]{1,0:T(8,128)(2,1)S(1)} %copy-done.4, bf16[256,528]{1,0:T(8,128)(2,1)S(1)} %copy-done.3, f32[33,256]{1,0:T(8,128)S(1)} %copy-done.7, ...), custom_call_target="tpu_custom_call" | custom-call | flops 800000000 | bytes 3000000 | tf_op jit(solution)/shard_map/pallas_call | solution.py:279
  31.5 0.0 copy-start.9
  31.5 0.0 copy-start
  31.5 0.0 copy-start.1
  31.5 0.0 copy-start.2
  31.5 9.4 %all-to-all-start.1 = ((bf16[32,8,256]{2,1,0:T(8,128)(2,1)}), bf16[32,8,256]{2,1,0:T(8,128)(2,1)S(1)}, u32[]{:S(2)}, u32[]{:S(2)}) async-start(bf16[32,8,256]{2,1,0:T(8,128)(2,1)} %bitcast.3), calls=%async_computation.1 | async-start | bytes 262144 | tf_op jit(solution)/shard_map/all_to_all | solution.py:358
  40.9 2.0 %shard_map.122.refs_2_ = bf16[256,1024]{1,0:T(8,128)(2,1)} custom-call(s32[1]{0:T(128)} %bitcast.refs_0_, bf16[256,4096]{1,0:T(8,128)(2,1)} %refs_1_.6), custom_call_target="tpu_custom_call" | custom-call | bytes 1048576 | tf_op jit(solution)/shard_map/pallas_call | solution.py:114
  42.9 0.0 copy-done.9
  42.9 0.1 copy.13.gain_ref
  43.0 0.0 collective-permute-done.refs_4_
  43.0 4.7 %collective-permute-done.1.refs_5_ = bf16[256,1024]{1,0:T(8,128)(2,1)S(1)} collective-permute-done((bf16[256,1024]{1,0:T(8,128)(2,1)}, bf16[256,1024]{1,0:T(8,128)(2,1)S(1)}, u32[]{:S(2)}, u32[]{:S(2)}) %collective-permute-start.1) | collective-permute-done | bytes 524320 | tf_op jit(solution)/shard_map/ppermute | solution.py:379
  47.7 0.0 collective-permute-done.2.refs_3_
  47.8 0.0 all-to-all-done.1
  47.8 0.0 copy-done
  47.8 0.0 copy-done.1
  47.8 0.0 copy-done.2
  47.8 0.2 shard_map.121
  48.0 7.6 %all_gather.3.refs_1_ = bf16[1024,256]{1,0:T(8,128)(2,1)S(1)} all-gather(bf16[256,256]{1,0:T(8,128)(2,1)S(1)} %shard_map.121), channel_id=1, replica_groups=mesh['ctx'=32,'quad'=4,'pair'=2,'core'=2] {'pair','core'}, dimensions={0}, use_global_device_ids=true | all-gather | bytes 655360 | tf_op jit(solution)/shard_map/all_gather | solution.py:388
  55.6 2.1 %shard_map.123 = (bf16[256,256]{1,0:T(8,128)(2,1)S(1)}, bf16[256,256]{1,0:T(8,128)(2,1)S(1)}, bf16[256,256]{1,0:T(8,128)(2,1)S(1)}, bf16[256,256]{1,0:T(8,128)(2,1)S(1)}) custom-call(s32[1]{0:T(128)} %bitcast.refs_0_, bf16[1024,256]{1,0:T(8,128)(2,1)S(1)} %all_gather.3.refs_1_, bf16[256,1024]{1,0:T(8,128)(2,1)} %shard_map.122.refs_2_, ...), custom_call_target="tpu_custom_call" | custom-call | flops 536870912 | bytes 3145728 | tf_op jit(solution)/shard_map/pallas_call | solution.py:167
  57.8 6.4 %collective-permute-start.3 = (bf16[256,256]{1,0:T(8,128)(2,1)S(1)}, bf16[256,256]{1,0:T(8,128)(2,1)S(1)}, u32[]{:S(2)}, u32[]{:S(2)}) collective-permute-start(bf16[256,256]{1,0:T(8,128)(2,1)S(1)} %get-tuple-element.17), channel_id=1, source_target_pairs={{0,10},{1,11},{2,8},{3,9},{4,14},{5,15},{6,12},{7,13},{8,2},{9,3},... | collective-permute-start | bytes 393224 | tf_op jit(solution)/shard_map/ppermute | solution.py:33
  64.2 2.7 %collective-permute-start.4 = (bf16[256,256]{1,0:T(8,128)(2,1)S(1)}, bf16[256,256]{1,0:T(8,128)(2,1)S(1)}, u32[]{:S(2)}, u32[]{:S(2)}) collective-permute-start(bf16[256,256]{1,0:T(8,128)(2,1)S(1)} %get-tuple-element.18), channel_id=1, source_target_pairs={{0,12},{1,13},{2,6},{3,7},{4,0},{5,1},{6,10},{7,11},{8,4},{9,5},{1... | collective-permute-start | bytes 393224 | tf_op jit(solution)/shard_map/ppermute | solution.py:33
  67.0 4.4 %collective-permute-start.5 = (bf16[256,256]{1,0:T(8,128)(2,1)S(1)}, bf16[256,256]{1,0:T(8,128)(2,1)S(1)}, u32[]{:S(2)}, u32[]{:S(2)}) collective-permute-start(bf16[256,256]{1,0:T(8,128)(2,1)S(1)} %get-tuple-element.19), channel_id=1, source_target_pairs={{0,14},{1,15},{2,4},{3,5},{4,2},{5,3},{6,8},{7,9},{8,6},{9,7},{10,... | collective-permute-start | bytes 393224 | tf_op jit(solution)/shard_map/ppermute | solution.py:33
  71.4 0.0 collective-permute-done.3.refs_0_
  71.4 2.7 %collective-permute-done.4.refs_1_ = bf16[256,256]{1,0:T(8,128)(2,1)S(1)} collective-permute-done((bf16[256,256]{1,0:T(8,128)(2,1)S(1)}, bf16[256,256]{1,0:T(8,128)(2,1)S(1)}, u32[]{:S(2)}, u32[]{:S(2)}) %collective-permute-start.4) | collective-permute-done | bytes 131104 | tf_op jit(solution)/shard_map/ppermute | solution.py:33
  74.1 2.0 %collective-permute-done.5.refs_2_ = bf16[256,256]{1,0:T(8,128)(2,1)S(1)} collective-permute-done((bf16[256,256]{1,0:T(8,128)(2,1)S(1)}, bf16[256,256]{1,0:T(8,128)(2,1)S(1)}, u32[]{:S(2)}, u32[]{:S(2)}) %collective-permute-start.5) | collective-permute-done | bytes 131104 | tf_op jit(solution)/shard_map/ppermute | solution.py:33
  76.1 0.8 %shard_map.124 = bf16[256,256]{1,0:T(8,128)(2,1)} custom-call(bf16[256,256]{1,0:T(8,128)(2,1)S(1)} %collective-permute-done.3.refs_0_, bf16[256,256]{1,0:T(8,128)(2,1)S(1)} %collective-permute-done.4.refs_1_, bf16[256,256]{1,0:T(8,128)(2,1)S(1)} %collective-permute-done.5.refs_2_, bf16[256,256]{1,0:T(8,128)(2,1)S(1)} %get-tuple-element.20.refs_3_), custom_call_target="tpu_custom_call" | custom-call | tf_op jit(solution)/shard_map/pallas_call | solution.py:196
  (4 shorter events, 0.0 us)
Async XLA Ops:
  0.0 28.8 %copy-start.6 = (f32[33,256]{1,0:T(8,128)S(1)}, f32[33,256]{1,0:T(8,128)}, u32[]{:S(2)}) copy-start(f32[33,256]{1,0:T(8,128)} %constant.32.clone.refs_6_) | copy-start | bytes 101380
  0.0 28.8 %copy-start.7 = (f32[33,256]{1,0:T(8,128)S(1)}, f32[33,256]{1,0:T(8,128)}, u32[]{:S(2)}) copy-start(f32[33,256]{1,0:T(8,128)} %constant.31.clone.refs_5_) | copy-start | bytes 101380
  0.0 28.8 %copy-start.3 = (bf16[256,528]{1,0:T(8,128)(2,1)S(1)}, bf16[256,528]{1,0:T(8,128)(2,1)}, u32[]{:S(2)}) copy-start(bf16[256,528]{1,0:T(8,128)(2,1)} %constant.30.clone.refs_4_) | copy-start | bytes 811012
  0.0 28.8 %copy-start.4 = (bf16[256,256]{1,0:T(8,128)(2,1)S(1)}, bf16[256,256]{1,0:T(8,128)(2,1)}, u32[]{:S(2)}) copy-start(bf16[256,256]{1,0:T(8,128)(2,1)} %constant.29.clone.refs_3_) | copy-start | bytes 393220
  0.0 28.8 %copy-start.5 = (bf16[256,256]{1,0:T(8,128)(2,1)S(1)}, bf16[256,256]{1,0:T(8,128)(2,1)}, u32[]{:S(2)}) copy-start(bf16[256,256]{1,0:T(8,128)(2,1)} %constant.28.clone.refs_2_) | copy-start | bytes 393220
  0.0 28.8 %copy-start.8 = (bf16[66,32]{1,0:T(8,128)(2,1)S(1)}, bf16[66,32]{1,0:T(8,128)(2,1)}, u32[]{:S(2)}) copy-start(bf16[66,32]{1,0:T(8,128)(2,1)} %constant.27.clone.refs_1_) | copy-start | bytes 12676
  1.9 26.8 %all-to-all-start = ((bf16[32,16,256]{2,1,0:T(8,128)(2,1)}), bf16[32,16,256]{2,1,0:T(8,128)(2,1)S(1)}, u32[]{:S(2)}, u32[]{:S(2)}) async-start(bf16[32,16,256]{2,1,0:T(8,128)(2,1)} %bitcast.8), calls=%async_computation | async-start | bytes 524288 | tf_op jit(solution)/shard_map/all_to_all | solution.py:358
  20.4 22.6 %collective-permute-start = (bf16[256,1024]{1,0:T(8,128)(2,1)}, bf16[256,1024]{1,0:T(8,128)(2,1)S(1)}, u32[]{:S(2)}, u32[]{:S(2)}) collective-permute-start(bf16[256,1024]{1,0:T(8,128)(2,1)} %get-tuple-element.14), channel_id=1, source_target_pairs={{0,2},{1,3},{2,0},{3,1},{4,6},{5,7},{6,4},{7,5},{8,10},{9,11},{10,... | collective-permute-start | bytes 1572872 | tf_op jit(solution)/shard_map/ppermute | solution.py:379
  23.7 24.1 %collective-permute-start.1 = (bf16[256,1024]{1,0:T(8,128)(2,1)}, bf16[256,1024]{1,0:T(8,128)(2,1)S(1)}, u32[]{:S(2)}, u32[]{:S(2)}) collective-permute-start(bf16[256,1024]{1,0:T(8,128)(2,1)} %get-tuple-element.15), channel_id=1, source_target_pairs={{0,3},{1,2},{2,1},{3,0},{4,7},{5,6},{6,5},{7,4},{8,11},{9,10},{10,... | collective-permute-start | bytes 1572872 | tf_op jit(solution)/shard_map/ppermute | solution.py:379
  26.9 20.9 %collective-permute-start.2 = (bf16[256,1024]{1,0:T(8,128)(2,1)}, bf16[256,1024]{1,0:T(8,128)(2,1)S(1)}, u32[]{:S(2)}, u32[]{:S(2)}) collective-permute-start(bf16[256,1024]{1,0:T(8,128)(2,1)} %get-tuple-element.16), channel_id=1, source_target_pairs={{0,1},{1,0},{2,3},{3,2},{4,5},{5,4},{6,7},{7,6},{8,9},{9,8},{10,11... | collective-permute-start | bytes 1572872 | tf_op jit(solution)/shard_map/ppermute | solution.py:379
  31.5 11.4 %copy-start.9 = (f32[256]{0:T(256)S(1)}, f32[256]{0:T(256)}, u32[]{:S(2)}) copy-start(f32[256]{0:T(256)} %param.16) | copy-start | bytes 3076
  31.5 16.3 %copy-start = (bf16[256,256]{1,0:T(8,128)(2,1)S(1)}, bf16[256,256]{1,0:T(8,128)(2,1)}, u32[]{:S(2)}) copy-start(bf16[256,256]{1,0:T(8,128)(2,1)} %signal_ref.1) | copy-start | bytes 393220
  31.5 16.3 %copy-start.1 = (bf16[256,256]{1,0:T(8,128)(2,1)S(1)}, bf16[256,256]{1,0:T(8,128)(2,1)}, u32[]{:S(2)}) copy-start(bf16[256,256]{1,0:T(8,128)(2,1)} %pre_ref.1) | copy-start | bytes 393220
  31.5 16.3 %copy-start.2 = (bf16[256,256]{1,0:T(8,128)(2,1)S(1)}, bf16[256,256]{1,0:T(8,128)(2,1)}, u32[]{:S(2)}) copy-start(bf16[256,256]{1,0:T(8,128)(2,1)} %post_ref.1) | copy-start | bytes 393220
  31.5 16.2 %all-to-all-start.1 = ((bf16[32,8,256]{2,1,0:T(8,128)(2,1)}), bf16[32,8,256]{2,1,0:T(8,128)(2,1)S(1)}, u32[]{:S(2)}, u32[]{:S(2)}) async-start(bf16[32,8,256]{2,1,0:T(8,128)(2,1)} %bitcast.3), calls=%async_computation.1 | async-start | bytes 262144 | tf_op jit(solution)/shard_map/all_to_all | solution.py:358
  57.8 13.6 %collective-permute-start.3 = (bf16[256,256]{1,0:T(8,128)(2,1)S(1)}, bf16[256,256]{1,0:T(8,128)(2,1)S(1)}, u32[]{:S(2)}, u32[]{:S(2)}) collective-permute-start(bf16[256,256]{1,0:T(8,128)(2,1)S(1)} %get-tuple-element.17), channel_id=1, source_target_pairs={{0,10},{1,11},{2,8},{3,9},{4,14},{5,15},{6,12},{7,13},{8,2},{9,3},... | collective-permute-start | bytes 393224 | tf_op jit(solution)/shard_map/ppermute | solution.py:33
  64.2 9.9 %collective-permute-start.4 = (bf16[256,256]{1,0:T(8,128)(2,1)S(1)}, bf16[256,256]{1,0:T(8,128)(2,1)S(1)}, u32[]{:S(2)}, u32[]{:S(2)}) collective-permute-start(bf16[256,256]{1,0:T(8,128)(2,1)S(1)} %get-tuple-element.18), channel_id=1, source_target_pairs={{0,12},{1,13},{2,6},{3,7},{4,0},{5,1},{6,10},{7,11},{8,4},{9,5},{1... | collective-permute-start | bytes 393224 | tf_op jit(solution)/shard_map/ppermute | solution.py:33
  67.0 9.1 %collective-permute-start.5 = (bf16[256,256]{1,0:T(8,128)(2,1)S(1)}, bf16[256,256]{1,0:T(8,128)(2,1)S(1)}, u32[]{:S(2)}, u32[]{:S(2)}) collective-permute-start(bf16[256,256]{1,0:T(8,128)(2,1)S(1)} %get-tuple-element.19), channel_id=1, source_target_pairs={{0,14},{1,15},{2,4},{3,5},{4,2},{5,3},{6,8},{7,9},{8,6},{9,7},{10,... | collective-permute-start | bytes 393224 | tf_op jit(solution)/shard_map/ppermute | solution.py:33
